TPU v7x, 512 devices: a whole 4x8x8 slice. The times are simulated.
512 devices in a mesh: batch: 4 (over x), seq: 32 (over z_hi, y), head: 4 (over z_lo, core).
Axes of the slice: x: 4, y: 8, z: 8 (z_hi: 4, z_lo: 2; z = z_hi * 2 + z_lo), core: 2. Of those that a mesh axis runs over, the one named last changes fastest.
Arguments:
- queries: bfloat16 [4096, 8192], P(('batch', 'seq'), 'head'), parts along dimension 0, may hold values from -21 to 21
- kv_cache: bfloat16 [98304, 2, 512], P(('batch', 'seq'), None, 'head'), parts along dimension 0, may hold values from -6 to 6
- new_kv: bfloat16 [4096, 2, 512], P(('batch', 'seq'), None, 'head'), parts along dimension 0, may hold values from -7.5 to 7.5
- cache_len: int32 [512], P(('batch', 'seq')), parts along dimension 0, may hold values from 1 to 192, 15360 in all
- new_pos: int32 [4096], P(('batch', 'seq')), parts along dimension 0, may hold values from 0 to 1023, as said below
Outputs:
- attended: bfloat16 [4096, 8192], P(('batch', 'seq'), 'head'), parts along dimension 0
There are 4 independent parts, one for each index of `batch`. A program takes and returns all parts, laid end to end along the dimension named above; each array names one. Nothing has to cross between parts.
Inputs may be any that keep to these rules, and one draw needn't show every extreme that they name: new_pos holds every number of 0 to 1023 once; the 32 tokens of one index of seq are two runs of 16 consecutive positions, in rising order within a run, the runs b and 63 - b (counted in runs of 16) for some b, in either order.
All inputs are finite; a program needn't handle non-finite values. No bound on the sum of `cache_len` on one device may be relied on, other than what follows from the above.
Results may differ from a plain program's by a relative error of at most 0.0055.
Values may be sent and summed in bfloat16 or wider, within the bound.
No kernel may reach another device: no remote copies, remote signals or barrier semaphores. Data moves between devices by JAX's collectives and lax.ppermute only.
A program may use at most 64 MiB of HBM per device.

v0:
```python
import math

import jax
import jax.numpy as jnp
from jax import lax
from jax.sharding import PartitionSpec as P

HPK = 16
DH = 128


def group_partial(query_rows, query_pos, key_rows, key_codes):
    count = query_rows.shape[0]
    heads_here = key_rows.shape[2] // DH
    query_heads = query_rows.reshape(count, heads_here, HPK, DH)
    keys_only = key_rows[:, 0].reshape(-1, heads_here, DH)
    values_only = key_rows[:, 1].reshape(-1, heads_here, DH)
    scores = jnp.einsum(
        "tghd,kgd->gthk", query_heads, keys_only, preferred_element_type=jnp.float32
    ) * (1.0 / math.sqrt(DH))
    visible = key_codes[None, :] <= query_pos[:, None]
    scores = jnp.where(visible[None, :, None, :], scores, -jnp.inf)
    top = jnp.max(scores, axis=-1, keepdims=True)
    weights = jnp.exp(scores - top)
    totals = jnp.sum(weights, axis=-1)
    mixed = jnp.einsum(
        "gthk,kgd->gthd",
        weights.astype(jnp.bfloat16),
        values_only,
        preferred_element_type=jnp.float32,
    )
    output = (mixed / totals[..., None]).astype(jnp.bfloat16)
    log_total = top[..., 0] + jnp.log(totals)
    output = jnp.transpose(output, (1, 0, 2, 3)).reshape(count, heads_here * HPK * DH)
    log_total = jnp.transpose(log_total, (1, 0, 2)).reshape(count, heads_here * HPK)
    return (output, log_total)


def combine(outputs, logs):
    groups, count, heads_out = logs.shape
    peak = jnp.max(logs, axis=0)
    shares = jnp.exp(logs - peak)
    totals = jnp.sum(shares, axis=0)
    outputs_heads = outputs.reshape(groups, count, heads_out, DH)
    summed = jnp.einsum("snh,snhd->nhd", shares, outputs_heads, preferred_element_type=jnp.float32)
    return (summed / totals[..., None]).reshape(count, heads_out * DH).astype(jnp.bfloat16)


def largest_step():
    for stride in (4, 3, 2):
        return stride
    return 1


def body(queries, kv_cache, new_kv, cache_len, new_pos):
    own_rows = new_pos.shape[0]
    slot_count = kv_cache.shape[0]
    groups = lax.axis_size("seq")
    all_new = own_rows * groups
    group_rows = slot_count + own_rows
    width_out = queries.shape[1]
    heads_out = width_out // DH
    block_size = slot_count // 4
    key_rows = jnp.concatenate([kv_cache, new_kv], axis=0)
    within = jnp.arange(slot_count, dtype=jnp.int32) % block_size
    lengths = jnp.repeat(cache_len, block_size, total_repeat_length=slot_count)
    slot_codes = jnp.where(within < lengths, -1, all_new).astype(jnp.int32)
    key_codes = jnp.concatenate([slot_codes, new_pos], axis=0)
    initial = (
        jnp.zeros((groups, own_rows, width_out), jnp.bfloat16),
        jnp.zeros((groups, own_rows, heads_out), jnp.float32),
    )
    key_piece = lax.all_gather(key_rows, "seq", axis=0, tiled=True)
    code_piece = lax.all_gather(key_codes, "seq", axis=0, tiled=True)
    count = key_piece.shape[0] // group_rows
    stride = largest_step()

    def one_block(index, state):
        out_all, log_all = state
        lead = index * stride
        keys_here = lax.dynamic_slice_in_dim(key_piece, lead * group_rows, stride * group_rows, 0)
        keys_here = keys_here.reshape(stride, group_rows, 2, key_piece.shape[2])
        codes_here = lax.dynamic_slice_in_dim(code_piece, lead * group_rows, stride * group_rows, 0)
        codes_here = codes_here.reshape(stride, group_rows)
        output, log_total = jax.vmap(group_partial, in_axes=(None, None, 0, 0))(
            queries, new_pos, keys_here, codes_here
        )
        out_all = lax.dynamic_update_slice_in_dim(out_all, output, lead, 0)
        log_all = lax.dynamic_update_slice_in_dim(log_all, log_total, lead, 0)
        return (out_all, log_all)

    outputs, logs = lax.fori_loop(0, count // stride, one_block, initial)
    return combine(outputs, logs)


def solution(mesh):
    return jax.shard_map(
        body,
        mesh=mesh,
        in_specs=(
            P(("batch", "seq"), "head"),
            P(("batch", "seq"), None, "head"),
            P(("batch", "seq"), None, "head"),
            P(("batch", "seq")),
            P(("batch", "seq")),
        ),
        out_specs=P(("batch", "seq"), "head"),
        check_vma=False,
    )
```

profile of v0, /device:TPU:6, one launch (start us, length us, event | category | flops | bytes accessed | tf_op | source)
XLA Modules:
  0.0 595.4 jit_solution(3515883866151075886)
XLA Ops:
  6.5 1.5 fusion.21
  8.0 1.3 dynamic-slice.6
  9.9 3.2 fusion.19
  15.4 1.0 copy.14
  17.3 284.3 %all-reduce.3.cloned.1.call-done = s32[25600]{0:T(1024)} async-done(((s32[25600]{0:T(1024)}), s32[25600]{0:T(1024)}) %all-reduce.3.cloned.1.call-update) | async-done | bytes 102416
  301.6 181.4 %all-gather.2.cloned.1.call-done = bf16[25600,2,128]{2,0,1:T(8,128)(2,1)} async-done(((bf16[800,2,128]{2,0,1:T(8,128)(2,1)}), bf16[25600,2,128]{2,0,1:T(8,128)(2,1)}) %all-gather.2.cloned.1.call-update) | async-done | bytes 13107216 | tf_op jit(solution)/shard_map/all_gather | solution.py:73
  483.0 2.5 broadcast_in_dim.62
  485.5 91.3 %while.18 = (s32[]{:T(128)}, bf16[32,32,2048]{2,1,0:T(8,128)(2,1)}, f32[32,32,16]{1,2,0:T(8,128)S(1)}, s32[25600]{0:T(1024)}, s32[32]{0:T(128)}, /*index=5*/bf16...) while((s32[]{:T(128)}, bf16[32,32,2048]{2,1,0:T(8,128)(2,1)}, ...), condition=%wide.region_3.4_spmd, body=%wide.region_0.3_spmd.sunk | while | flops 857507840 | bytes 30890864 | solution.py:92
  487.1 1.5 constant_dynamic-slice_fusion.2
  488.7 2.2 fusion.32
  490.9 2.1 fusion.33
  493.0 2.0 fusion.34
  496.0 0.9 constant_dynamic-update-slice_fusion.2
  498.6 1.5 constant_dynamic-slice_fusion.2
  500.1 2.2 fusion.32
  502.3 2.1 fusion.33
  504.4 2.0 fusion.34
  510.0 1.5 constant_dynamic-slice_fusion.2
  511.5 2.2 fusion.32
  513.7 2.1 fusion.33
  515.8 2.0 fusion.34
  518.9 0.8 constant_dynamic-update-slice_fusion.2
  521.4 1.5 constant_dynamic-slice_fusion.2
  522.9 2.2 fusion.32
  525.1 2.1 fusion.33
  527.2 2.0 fusion.34
  530.3 0.9 constant_dynamic-update-slice_fusion.2
  532.8 1.5 constant_dynamic-slice_fusion.2
  534.4 2.2 fusion.32
  536.5 2.1 fusion.33
  538.6 2.0 fusion.34
  541.7 0.9 constant_dynamic-update-slice_fusion.2
  544.2 1.5 constant_dynamic-slice_fusion.2
  545.8 2.2 fusion.32
  548.0 2.1 fusion.33
  550.1 2.0 fusion.34
  555.6 1.5 constant_dynamic-slice_fusion.2
  557.2 2.2 fusion.32
  559.3 2.1 fusion.33
  561.4 2.0 fusion.34
  564.5 0.8 constant_dynamic-update-slice_fusion.2
  567.0 1.5 constant_dynamic-slice_fusion.2
  568.6 2.2 fusion.32
  570.7 2.1 fusion.33
  572.8 2.0 fusion.34
  575.9 0.8 constant_dynamic-update-slice_fusion.2
  576.9 5.5 copy.25
  582.9 4.8 fusion.12
  (76 shorter events, 28.0 us)
Async XLA Ops:
  6.5 295.1 %all-reduce.3.cloned.1.call-start = ((), (), s32[]{:S(2)}) async-start(), calls=%async_computation.1 | async-start | bytes 204800
  13.9 0.6 copy-start
  14.6 468.4 %all-gather.2.cloned.1.call-start = ((), (), s32[]{:S(2)}) async-start(), calls=%async_computation | async-start | bytes 13516800 | tf_op jit(solution)/shard_map/all_gather | solution.py:73
Sparse Core Ops, SparseCore 0:
  14.7 286.8 all-reduce.2
  305.2 177.7 all-gather.1
where the time goes:
time: 601 us; the launch traced here: 595 us
  waiting for transfers between devices  466 us (78%)
  local copies, waits for them, and re-layouts  43 us (7%)
  matrix products  39 us (6%)
  other arithmetic  33.2 us (6%)
  between operations  14.1 us (2%)
    unnamed x3, waiting for transfers between devices  284 us
    all_gather x1, waiting for transfers between devices, body(): key_piece = lax.all_gather(key_rows, 'seq', axis=0, tiled=True)  181 us
    dot_general x8, matrix products, group_partial(): jnp.einsum('tghd,kgd->gthk', query_heads, keys_only, preferred_element_ty...  17.5 us
    dot_general x8, matrix products, group_partial(): jnp.einsum('gthk,kgd->gthd', weights.astype(jnp.bfloat16), values_only, p...  16.7 us
    reduce_sum x8, other arithmetic, group_partial(): totals = jnp.sum(weights, axis=-1)  15.7 us
    dynamic_slice x8, local copies, waits for them, and re-layouts, one_block(): lax.dynamic_slice_in_dim(key_piece, lead * group_rows, stride * group_row...  12.4 us
  transfers between devices with their start and end apart: 2, of which 2 were waited for; matrix products, arithmetic and copies ran while one was open for 0% of the time, Pallas kernels for 0%

commit v1 on v0

v1 whole, which is shorter than its diff:
```python
import functools
import math

import jax
import jax.numpy as jnp
from jax import lax
from jax.experimental import pallas as pl
from jax.experimental.pallas import tpu as pltpu
from jax.sharding import PartitionSpec as P

HPK = 16
DH = 128
NEW_DEV = 32
CACHE_DEV = 768
BLOCK = CACHE_DEV // 4
RUN = NEW_DEV // 2
LAST_RUN = 1024 - RUN
SEQ_Z = 4
SEQ_Y = 8
ROWS = NEW_DEV * HPK
INFO = 16
NEW_PAD = 128
V_AT = CACHE_DEV
NEW_K_AT = 2 * CACHE_DEV
NEW_V_AT = NEW_K_AT + NEW_DEV
INFO_AT = NEW_V_AT + NEW_DEV
KV_ROWS = INFO_AT + INFO
SCALE = math.log2(math.e) / math.sqrt(DH)
HIDDEN = -1e30
CHUNK = 512

F32 = jnp.float32
BF16 = jnp.bfloat16


def iota(shape, dim):
    return lax.broadcasted_iota(jnp.int32, shape, dim)


def pack_kernel(cache_len, new_pos, q_ref, kv_ref, new_ref, qp_ref, kv_out):
    run = (new_pos[0] // RUN).astype(F32)
    info_row = iota((INFO, DH), 0)
    for i in range(SEQ_Y):
        qp_ref[i, ROWS : ROWS + INFO] = jnp.full((INFO, DH), run, F32).astype(BF16)
        for h in range(HPK):
            qp_ref[i, h * NEW_DEV : (h + 1) * NEW_DEV] = q_ref[:, h * DH : (h + 1) * DH]
    first_key = kv_ref[0, 0:16, :].astype(F32)[0:1]
    info = jnp.full((INFO, DH), run, F32)
    kept = []
    for b in range(4):
        length = cache_len[b]
        info = jnp.where(info_row == b, length.astype(F32), info)
        rows = slice(b * BLOCK, (b + 1) * BLOCK)
        live = iota((BLOCK, DH), 0) < length
        kept.append(jnp.where(live, kv_ref[0, rows, :].astype(F32), first_key))
        values = kv_ref[1, rows, :].astype(F32)
        kv_out[V_AT + b * BLOCK : V_AT + (b + 1) * BLOCK] = jnp.where(live, values, 0.0).astype(BF16)
    keys = jnp.concatenate(kept, axis=0)
    for t in range(CACHE_DEV // DH):
        rows = slice(t * DH, (t + 1) * DH)
        kv_out[rows] = jnp.transpose(keys[rows]).astype(BF16)
    kv_out[NEW_K_AT:NEW_V_AT] = new_ref[0]
    kv_out[NEW_V_AT:INFO_AT] = new_ref[1]
    kv_out[INFO_AT:KV_ROWS] = info.astype(BF16)


def pack(queries, kv_cache, new_kv, cache_len, new_pos):
    smem = pl.BlockSpec(memory_space=pltpu.SMEM)
    vmem = pl.BlockSpec(memory_space=pltpu.VMEM)
    return pl.pallas_call(
        pack_kernel,
        out_shape=(
            jax.ShapeDtypeStruct((SEQ_Y, ROWS + INFO, DH), BF16),
            jax.ShapeDtypeStruct((KV_ROWS, DH), BF16),
        ),
        in_specs=[smem, smem, vmem, vmem, vmem],
        out_specs=(vmem, vmem),
        compiler_params=pltpu.CompilerParams(vmem_limit_bytes=16 << 20),
        name="pack",
    )(cache_len, new_pos, queries, jnp.transpose(kv_cache, (1, 0, 2)), jnp.transpose(new_kv, (1, 0, 2)))


def attend_kernel(q_ref, kv_ref, out_ref, kk, vv, bias, lse):
    nq, g = q_ref.shape[0], kv_ref.shape[0]
    lane = iota((NEW_DEV, DH), 1)
    within = lane % NEW_DEV
    token = iota((NEW_DEV, DH), 0)
    base = jnp.zeros((1, DH), F32)
    new_row = g * CACHE_DEV
    fresh_keys = []
    for j in range(g):
        info = kv_ref[j, INFO_AT:KV_ROWS].astype(F32)
        base = jnp.where(lane[0:1] // NEW_DEV == j, info[4:5] * RUN, base)
        for t in range(CACHE_DEV // DH):
            at = j * CACHE_DEV + t * DH
            kk[:, at : at + DH] = kv_ref[j, t * DH : (t + 1) * DH]
        for b in range(4):
            dst = slice(j * CACHE_DEV + b * BLOCK, j * CACHE_DEV + (b + 1) * BLOCK)
            vv[dst, 0:DH] = kv_ref[j, V_AT + b * BLOCK : V_AT + (b + 1) * BLOCK]
            live = iota((BLOCK, DH), 0).astype(F32) < info[b : b + 1]
            vv[dst, DH:] = jnp.where(live, 1.0, 0.0).astype(BF16)
        fresh_keys.append(kv_ref[j, NEW_K_AT:NEW_V_AT].astype(F32))
        dst = slice(new_row + j * NEW_DEV, new_row + (j + 1) * NEW_DEV)
        vv[dst, 0:DH] = kv_ref[j, NEW_V_AT:INFO_AT]
        vv[dst, DH:] = jnp.ones((NEW_DEV, DH), BF16)
    kk[:, new_row : new_row + NEW_PAD] = jnp.transpose(jnp.concatenate(fresh_keys, axis=0)).astype(BF16)
    within_f = within.astype(F32)
    key_pos = jnp.where(within < RUN, base + within_f, LAST_RUN - RUN - base + within_f)
    token_f = token.astype(F32)
    for i in range(nq):
        start = q_ref[i, ROWS : ROWS + INFO].astype(F32)[0:1] * RUN
        pos = jnp.where(token < RUN, start + token_f, LAST_RUN - RUN - start + token_f)
        bias[i * NEW_DEV : (i + 1) * NEW_DEV] = jnp.where(key_pos <= pos, 0.0, HIDDEN)

    def block(i, carry):
        q = q_ref[i, 0:ROWS]

        def scores_of(lo, hi):
            return jnp.dot(q, kk[:, lo:hi], preferred_element_type=F32)

        mask = bias[pl.ds(pl.multiple_of(i * NEW_DEV, NEW_DEV), NEW_DEV), :]
        fresh = scores_of(new_row, new_row + NEW_PAD).reshape(HPK, NEW_DEV, NEW_PAD)
        fresh = (fresh + mask[None]).reshape(ROWS, NEW_PAD)
        scores = [scores_of(j * CACHE_DEV, (j + 1) * CACHE_DEV) for j in range(g)]
        top = fresh
        for s in scores:
            for part in range(CACHE_DEV // DH):
                top = jnp.maximum(top, s[:, part * DH : (part + 1) * DH])
        top = jnp.max(top, axis=1, keepdims=True)

        def mixed(s, lo, hi):
            weights = jnp.exp2((s - top) * SCALE).astype(BF16)
            return jnp.dot(weights, vv[lo:hi, :], preferred_element_type=F32)

        total = mixed(fresh, new_row, new_row + NEW_PAD)
        for j, s in enumerate(scores):
            total += mixed(s, j * CACHE_DEV, (j + 1) * CACHE_DEV)
        acc, length = total[:, 0:DH], total[:, DH:]
        out_ref[i, 0:ROWS] = (acc / length).astype(BF16)
        lse[...] = top * SCALE + jnp.log2(length)
        row = iota((INFO, DH), 0)
        tile = jnp.zeros((INFO, DH), F32)
        for part in range(ROWS // DH):
            turned = jnp.transpose(lse[part * DH : (part + 1) * DH, :])[0:INFO]
            high = turned.astype(BF16).astype(F32)
            middle = (turned - high).astype(BF16).astype(F32)
            low = turned - high - middle
            tile = jnp.where(row == part, high, tile)
            tile = jnp.where(row == 4 + part, middle, tile)
            tile = jnp.where(row == 8 + part, low, tile)
        out_ref[i, ROWS : ROWS + INFO] = tile.astype(BF16)
        return carry

    lax.fori_loop(0, nq, block, 0)


def attend(qs, kvs):
    nq, g = qs.shape[0], kvs.shape[0]
    keys = g * CACHE_DEV + NEW_PAD
    vmem = pl.BlockSpec(memory_space=pltpu.VMEM)
    return pl.pallas_call(
        attend_kernel,
        out_shape=jax.ShapeDtypeStruct(qs.shape, BF16),
        in_specs=[vmem, vmem],
        out_specs=vmem,
        scratch_shapes=[
            pltpu.VMEM((DH, keys), BF16),
            pltpu.VMEM((keys, 2 * DH), BF16),
            pltpu.VMEM((nq * NEW_DEV, DH), F32),
            pltpu.VMEM((ROWS, DH), F32),
        ],
        compiler_params=pltpu.CompilerParams(vmem_limit_bytes=40 << 20),
        cost_estimate=pl.CostEstimate(
            flops=4 * nq * ROWS * keys * DH, bytes_accessed=4 << 20, transcendentals=nq * ROWS * keys
        ),
        name="attend",
    )(qs, kvs)


def combine_kernel(parts_ref, out_ref):
    n = parts_ref.shape[0]
    tiles = [parts_ref[i, ROWS : ROWS + INFO].astype(F32) for i in range(n)]
    for c in range(ROWS // DH):
        logs = []
        for tile in tiles:
            line = tile[c : c + 1] + tile[4 + c : 5 + c] + tile[8 + c : 9 + c]
            logs.append(jnp.transpose(jnp.broadcast_to(line, (DH, DH))))
        peak = functools.reduce(jnp.maximum, logs)
        shares = [jnp.exp2(x - peak) for x in logs]
        total = functools.reduce(jnp.add, shares)
        summed = functools.reduce(
            jnp.add,
            [w * parts_ref[i, c * DH : (c + 1) * DH].astype(F32) for i, w in enumerate(shares)],
        )
        result = (summed / total).astype(BF16)
        for k in range(DH // NEW_DEV):
            h = c * (DH // NEW_DEV) + k
            out_ref[:, h * DH : (h + 1) * DH] = result[k * NEW_DEV : (k + 1) * NEW_DEV]


def combine(parts):
    vmem = pl.BlockSpec(memory_space=pltpu.VMEM)
    return pl.pallas_call(
        combine_kernel,
        out_shape=jax.ShapeDtypeStruct((NEW_DEV, HPK * DH), BF16),
        in_specs=[vmem],
        out_specs=vmem,
        compiler_params=pltpu.CompilerParams(vmem_limit_bytes=16 << 20),
        name="combine",
    )(parts)


ALONG_Y = [[z * SEQ_Y + y for y in range(SEQ_Y)] for z in range(SEQ_Z)]
ALONG_Z = [[z * SEQ_Y + y for z in range(SEQ_Z)] for y in range(SEQ_Y)]


def swap_y(x):
    return lax.all_to_all(x, "seq", 0, 0, axis_index_groups=ALONG_Y, tiled=True)


def body(queries, kv_cache, new_kv, cache_len, new_pos):
    copies, own_kv = pack(queries, kv_cache, new_kv, cache_len, new_pos)
    kvs = lax.all_gather(own_kv, "seq", axis=0, axis_index_groups=ALONG_Z)
    qs = swap_y(copies)
    return combine(swap_y(attend(qs, kvs)))


def solution(mesh):
    return jax.shard_map(
        body,
        mesh=mesh,
        in_specs=(
            P(("batch", "seq"), "head"),
            P(("batch", "seq"), None, "head"),
            P(("batch", "seq"), None, "head"),
            P(("batch", "seq")),
            P(("batch", "seq")),
        ),
        out_specs=P(("batch", "seq"), "head"),
        check_vma=False,
    )
```

time: 601 us -> 139 us (0.23)
  waiting for transfers between devices: 466 us -> 16.2 us
  blocking collectives: 0 us -> 72.2 us
  matrix products: 39 us -> 0 us
  local copies, waits for them, and re-layouts: 43 us -> 5.42 us
  other arithmetic: 33.2 us -> 0 us
  Pallas kernels: 0 us -> 31.7 us
    unnamed x3 -> x1, waiting for transfers between devices: 284 us -> 0.02 us
    all_gather x1, waiting for transfers between devices: 181 us -> 16.2 us  [body(): kvs = lax.all_gather(own_kv, 'seq', axis=0, axis_index_groups=ALONG_Z)]
    all_to_all x0 -> x2, blocking collectives: none -> 72.2 us  [swap_y(): return lax.all_to_all(x, 'seq', 0, 0, axis_index_groups=ALONG_Y, tiled=True)]
    dot_general x17 -> x0, matrix products: 39 us -> none  [the longest x8 17.5 us: group_partial(): jnp.einsum('tghd,kgd->gthk', query_heads, keys_only, preferred_element_ty...]
    pallas_call x0 -> x3, Pallas kernels: none -> 31.7 us  [the longest x1 28.6 us: attend(): pl.pallas_call(attend_kernel, out_shape=jax.ShapeDtypeStruct(qs.shape, BF...]
    dynamic_slice x16 -> x0, local copies, waits for them, and re-layouts: 18.8 us -> none  [the longest x8 12.4 us: one_block(): lax.dynamic_slice_in_dim(key_piece, lead * group_rows, stride * group_row...]
    reduce_sum x9 -> x0, other arithmetic: 15.8 us -> none  [the longest x8 15.7 us: group_partial(): totals = jnp.sum(weights, axis=-1)]
    dynamic_update_slice x8 -> x0, local copies, waits for them, and re-layouts: 6.75 us -> none  [one_block(): out_all = lax.dynamic_update_slice_in_dim(out_all, output, lead, 0)]
  transfers between devices with their start and end apart: 2 -> 1, of which waited for: 2 -> 1; matrix products, arithmetic and copies ran while one was open for 0% -> 0% of each run, Pallas kernels for 0% -> 0%
where the time goes in v1:
time: 139 us
  blocking collectives  72.2 us (52%)
  Pallas kernels  31.7 us (23%)
  waiting for transfers between devices  16.2 us (12%)
  between operations  13.4 us (10%)
  local copies, waits for them, and re-layouts  5.42 us (4%)
    all_to_all x2, blocking collectives, swap_y(): return lax.all_to_all(x, 'seq', 0, 0, axis_index_groups=ALONG_Y, tiled=True)  72.2 us
    pallas_call x1, Pallas kernels, attend(): pl.pallas_call(attend_kernel, out_shape=jax.ShapeDtypeStruct(qs.shape, BF...  28.6 us
    all_gather x1, waiting for transfers between devices, body(): kvs = lax.all_gather(own_kv, 'seq', axis=0, axis_index_groups=ALONG_Z)  16.2 us
    unnamed x10, local copies, waits for them, and re-layouts  5.42 us
  transfers between devices with their start and end apart: 1, of which 1 were waited for; matrix products, arithmetic and copies ran while one was open for 0% of the time, Pallas kernels for 0%

profile of v1, /device:TPU:6, one launch (start us, length us, event | category | flops | bytes accessed | tf_op | source)
XLA Modules:
  0.0 138.9 jit_solution(5547036247014339120)
XLA Ops:
  6.5 0.0 all-gather.3.cloned.1.call-start
  6.5 1.0 copy.10
  7.6 0.7 copy.11
  8.3 0.0 copy-start
  8.3 0.9 copy-done
  9.2 0.0 copy-start.1
  9.2 0.7 copy-done.1
  9.9 0.0 copy-start.2
  9.9 0.7 copy-done.2
  10.5 1.5 %pack.1 = (bf16[8,528,128]{2,1,0:T(8,128)(2,1)S(1)}, bf16[1616,128]{1,0:T(8,128)(2,1)}) custom-call(s32[4]{0:T(128)S(1)} %copy-done.1, s32[32]{0:T(128)S(1)} %copy-done.2, bf16[32,2048]{1,0:T(8,128)(2,1)S(1)} %copy-done, bf16[2,768,128]{2,1,0:T(8,128)(2,1)S(1)} %bitcast.7, bf16[2,32,128]{2,1,0:T(8,128)(2,1)S(1)} %bitcast.8), custom_call_target="tpu_custom_call" | custom-call | tf_op jit(solution)/shard_map/pack/pallas_call | solution.py:70
  12.1 0.0 all-gather.3.cloned.1.call-update
  12.1 36.3 %all_to_all.10.q_ref = bf16[8,528,128]{2,1,0:T(8,128)(2,1)S(1)} all-to-all(bf16[8,528,128]{2,1,0:T(8,128)(2,1)S(1)} %get-tuple-element.7), channel_id=1, replica_groups={{0,4,8,12,16,20,24,28},{32,36,40,44,48,52,56,60},{64,68,72,76,80,84,88,..., dimensions={0} | all-to-all | bytes 2162688 | tf_op jit(solution)/shard_map/all_to_all | solution.py:218
  48.4 16.2 %all-gather.3.cloned.1.call-done = bf16[6464,128]{1,0:T(8,128)(2,1)} async-done(((bf16[1616,128]{1,0:T(8,128)(2,1)}), bf16[6464,128]{1,0:T(8,128)(2,1)}) %all-gather.3.cloned.1.call-update) | async-done | bytes 1654800 | tf_op jit(solution)/shard_map/all_gather | solution.py:223
  64.6 0.0 copy-start.3
  64.6 1.4 %copy-done.3 = bf16[6464,128]{1,0:T(8,128)(2,1)S(1)} copy-done((bf16[6464,128]{1,0:T(8,128)(2,1)S(1)}, bf16[6464,128]{1,0:T(8,128)(2,1)}, u32[]{:S(2)}) %copy-start.3) | copy-done | bytes 1654808
  66.1 28.6 %attend.1 = bf16[8,528,128]{2,1,0:T(8,128)(2,1)S(1)} custom-call(bf16[8,528,128]{2,1,0:T(8,128)(2,1)S(1)} %all_to_all.10.q_ref, bf16[4,1616,128]{2,1,0:T(8,128)(2,1)S(1)} %bitcast.9), custom_call_target="tpu_custom_call" | custom-call | flops 6710886400 | bytes 4194304 | tf_op jit(solution)/shard_map/attend/pallas_call | solution.py:161
  94.6 35.8 %all_to_all.11.parts_ref = bf16[8,528,128]{2,1,0:T(8,128)(2,1)S(1)} all-to-all(bf16[8,528,128]{2,1,0:T(8,128)(2,1)S(1)} %attend.1), channel_id=1, replica_groups={{0,4,8,12,16,20,24,28},{32,36,40,44,48,52,56,60},{64,68,72,76,80,84,88,..., dimensions={0} | all-to-all | bytes 2162688 | tf_op jit(solution)/shard_map/all_to_all | solution.py:218
  130.5 1.6 %combine.1 = bf16[32,2048]{1,0:T(8,128)(2,1)} custom-call(bf16[8,528,128]{2,1,0:T(8,128)(2,1)S(1)} %all_to_all.11.parts_ref), custom_call_target="tpu_custom_call" | custom-call | tf_op jit(solution)/shard_map/combine/pallas_call | solution.py:203
Async XLA Ops:
  6.5 58.1 %all-gather.3.cloned.1.call-start = ((), (), s32[]{:S(2)}) async-start(), calls=%async_computation.2 | async-start | bytes 2068480 | tf_op jit(solution)/shard_map/all_gather | solution.py:223
  8.3 0.9 copy-start
  9.2 0.7 copy-start.1
  9.9 0.7 copy-start.2
  64.6 1.4 %copy-start.3 = (bf16[6464,128]{1,0:T(8,128)(2,1)S(1)}, bf16[6464,128]{1,0:T(8,128)(2,1)}, u32[]{:S(2)}) copy-start(bf16[6464,128]{1,0:T(8,128)(2,1)} %all-gather.3.cloned.1.call-done) | copy-start | bytes 4964356
Sparse Core Ops, SparseCore 0:
  12.2 52.3 all-gather.2

commit v2 on v1

v2 whole, which is shorter than its diff:
```python
import functools
import math

import jax
import jax.numpy as jnp
from jax import lax
from jax.experimental import pallas as pl
from jax.experimental.pallas import tpu as pltpu
from jax.sharding import PartitionSpec as P

HPK = 16
DH = 128
NEW_DEV = 32
CACHE_DEV = 768
BLOCK = CACHE_DEV // 4
RUN = NEW_DEV // 2
LAST_RUN = 1024 - RUN
SEQ_Z = 4
SEQ_Y = 8
ROWS = NEW_DEV * HPK
INFO = 16
NEW_PAD = 128
V_AT = CACHE_DEV
NEW_K_AT = 2 * CACHE_DEV
NEW_V_AT = NEW_K_AT + NEW_DEV
INFO_AT = NEW_V_AT + NEW_DEV
KV_ROWS = INFO_AT + INFO
SCALE = math.log2(math.e) / math.sqrt(DH)
HIDDEN = -1e30
CHUNK = 512

F32 = jnp.float32
BF16 = jnp.bfloat16


def iota(shape, dim):
    return lax.broadcasted_iota(jnp.int32, shape, dim)


def pack_kv_kernel(len_hbm, pos_hbm, kv_ref, new_ref, kv_out, cache_len, new_pos, sems):
    copies = [
        pltpu.make_async_copy(len_hbm, cache_len, sems.at[0]),
        pltpu.make_async_copy(pos_hbm, new_pos, sems.at[1]),
    ]
    for copy in copies:
        copy.start()
    kv_out[NEW_K_AT:NEW_V_AT] = new_ref[0]
    kv_out[NEW_V_AT:INFO_AT] = new_ref[1]
    first_key = kv_ref[0, 0:16, :].astype(F32)[0:1]
    for copy in copies:
        copy.wait()
    info_row = iota((INFO, DH), 0)
    info = jnp.full((INFO, DH), (new_pos[0] // RUN).astype(F32), F32)
    kept = []
    for b in range(4):
        length = cache_len[b]
        info = jnp.where(info_row == b, length.astype(F32), info)
        rows = slice(b * BLOCK, (b + 1) * BLOCK)
        live = iota((BLOCK, DH), 0) < length
        kept.append(jnp.where(live, kv_ref[0, rows, :].astype(F32), first_key))
        values = kv_ref[1, rows, :].astype(F32)
        kv_out[V_AT + b * BLOCK : V_AT + (b + 1) * BLOCK] = jnp.where(live, values, 0.0).astype(BF16)
    keys = jnp.concatenate(kept, axis=0)
    for t in range(CACHE_DEV // DH):
        rows = slice(t * DH, (t + 1) * DH)
        kv_out[rows] = jnp.transpose(keys[rows]).astype(BF16)
    kv_out[INFO_AT:KV_ROWS] = info.astype(BF16)


def pack_kv(kv_cache, new_kv, cache_len, new_pos):
    vmem = pl.BlockSpec(memory_space=pltpu.VMEM)
    hbm = pl.BlockSpec(memory_space=pl.ANY)
    return pl.pallas_call(
        pack_kv_kernel,
        out_shape=jax.ShapeDtypeStruct((KV_ROWS, DH), BF16),
        in_specs=[hbm, hbm, vmem, vmem],
        out_specs=vmem,
        scratch_shapes=[
            pltpu.SMEM(cache_len.shape, jnp.int32),
            pltpu.SMEM(new_pos.shape, jnp.int32),
            pltpu.SemaphoreType.DMA((2,)),
        ],
        compiler_params=pltpu.CompilerParams(vmem_limit_bytes=16 << 20),
        name="pack_kv",
    )(cache_len, new_pos, jnp.transpose(kv_cache, (1, 0, 2)), jnp.transpose(new_kv, (1, 0, 2)))


def pack_q_kernel(q_ref, kv_ref, out_ref):
    for h in range(HPK):
        out_ref[h * NEW_DEV : (h + 1) * NEW_DEV] = q_ref[:, h * DH : (h + 1) * DH]
    run = kv_ref[INFO_AT:KV_ROWS].astype(F32)[4:5]
    out_ref[ROWS : ROWS + INFO] = jnp.broadcast_to(run, (INFO, DH)).astype(BF16)


def pack_q(queries, own_kv):
    vmem = pl.BlockSpec(memory_space=pltpu.VMEM)
    return pl.pallas_call(
        pack_q_kernel,
        out_shape=jax.ShapeDtypeStruct((ROWS + INFO, DH), BF16),
        in_specs=[vmem, vmem],
        out_specs=vmem,
        compiler_params=pltpu.CompilerParams(vmem_limit_bytes=16 << 20),
        name="pack_q",
    )(queries, own_kv)


def stage_kernel(nq, g, first, last, *refs):
    refs = list(refs)
    take = lambda n: [refs.pop(0) for _ in range(n)]
    q_refs, kv_refs = take(nq), take(g)
    if not first:
        acc_in, top_in = take(2)
    if last:
        outs = take(nq)
    else:
        acc_out, top_out = take(2)
    qs, kk, vv, bias = take(4)
    if last:
        lse = refs.pop(0)

    lane = iota((NEW_DEV, DH), 1)
    within = lane % NEW_DEV
    token = iota((NEW_DEV, DH), 0)
    base = jnp.zeros((1, DH), F32)
    new_row = g * CACHE_DEV
    fresh_keys = []
    for j, kv_ref in enumerate(kv_refs):
        info = kv_ref[INFO_AT:KV_ROWS].astype(F32)
        base = jnp.where(lane[0:1] // NEW_DEV == j, info[4:5] * RUN, base)
        for t in range(CACHE_DEV // DH):
            at = j * CACHE_DEV + t * DH
            kk[:, at : at + DH] = kv_ref[t * DH : (t + 1) * DH]
        for b in range(4):
            dst = slice(j * CACHE_DEV + b * BLOCK, j * CACHE_DEV + (b + 1) * BLOCK)
            vv[dst, 0:DH] = kv_ref[V_AT + b * BLOCK : V_AT + (b + 1) * BLOCK]
            live = iota((BLOCK, DH), 0).astype(F32) < info[b : b + 1]
            vv[dst, DH:] = jnp.where(live, 1.0, 0.0).astype(BF16)
        fresh_keys.append(kv_ref[NEW_K_AT:NEW_V_AT].astype(F32))
        dst = slice(new_row + j * NEW_DEV, new_row + (j + 1) * NEW_DEV)
        vv[dst, 0:DH] = kv_ref[NEW_V_AT:INFO_AT]
        vv[dst, DH:] = jnp.ones((NEW_DEV, DH), BF16)
    if g * NEW_DEV < NEW_PAD:
        rest = NEW_PAD - g * NEW_DEV
        fresh_keys.append(jnp.zeros((rest, DH), F32))
        vv[new_row + g * NEW_DEV : new_row + NEW_PAD, :] = jnp.zeros((rest, 2 * DH), BF16)
    kk[:, new_row : new_row + NEW_PAD] = jnp.transpose(jnp.concatenate(fresh_keys, axis=0)).astype(BF16)
    within_f = within.astype(F32)
    key_pos = jnp.where(within < RUN, base + within_f, LAST_RUN - RUN - base + within_f)
    token_f = token.astype(F32)
    for i, q_ref in enumerate(q_refs):
        qs[i * ROWS : (i + 1) * ROWS] = q_ref[0:ROWS]
        start = q_ref[ROWS : ROWS + INFO].astype(F32)[0:1] * RUN
        pos = jnp.where(token < RUN, start + token_f, LAST_RUN - RUN - start + token_f)
        seen = (key_pos <= pos) & (lane < g * NEW_DEV)
        bias[i * NEW_DEV : (i + 1) * NEW_DEV] = jnp.where(seen, 0.0, HIDDEN)

    def chunk(c, carry):
        at = pl.multiple_of(c * CHUNK, CHUNK)
        rows = pl.ds(at, CHUNK)
        q = qs[rows, :]

        def scores_of(lo, hi):
            return jnp.dot(q, kk[:, lo:hi], preferred_element_type=F32)

        mask = bias[pl.ds(pl.multiple_of((c * CHUNK // ROWS) * NEW_DEV, NEW_DEV), NEW_DEV), :]
        fresh = scores_of(new_row, new_row + NEW_PAD).reshape(CHUNK // NEW_DEV, NEW_DEV, NEW_PAD)
        fresh = (fresh + mask[None]).reshape(CHUNK, NEW_PAD)
        scores = [scores_of(j * CACHE_DEV, (j + 1) * CACHE_DEV) for j in range(g)]
        top = fresh
        for s in scores:
            for part in range(CACHE_DEV // DH):
                top = jnp.maximum(top, s[:, part * DH : (part + 1) * DH])
        top = jnp.max(top, axis=1, keepdims=True)
        if not first:
            old = top_in[rows, :]
            top = jnp.maximum(top, old[:, 0:1])

        def mixed(s, lo, hi):
            weights = jnp.exp2((s - top) * SCALE).astype(BF16)
            return jnp.dot(weights, vv[lo:hi, :], preferred_element_type=F32)

        total = mixed(fresh, new_row, new_row + NEW_PAD)
        for j, s in enumerate(scores):
            total += mixed(s, j * CACHE_DEV, (j + 1) * CACHE_DEV)
        if not first:
            keep = jnp.exp2((old - top) * SCALE)
            total += acc_in[rows, :] * jnp.concatenate([keep, keep], axis=1)
        if last:
            acc, length = total[:, 0:DH], total[:, DH:]
            qs[rows, :] = (acc / length).astype(BF16)
            lse[rows, :] = top * SCALE + jnp.log2(length)
        else:
            acc_out[rows, :] = total
            top_out[rows, :] = jnp.broadcast_to(top, (CHUNK, DH))
        return carry

    lax.fori_loop(0, nq * ROWS // CHUNK, chunk, 0)
    if last:
        row = iota((INFO, DH), 0)
        for i in range(nq):
            outs[i][0:ROWS] = qs[i * ROWS : (i + 1) * ROWS]
            tile = jnp.zeros((INFO, DH), F32)
            for part in range(ROWS // DH):
                at = i * ROWS + part * DH
                turned = jnp.transpose(lse[at : at + DH, :])[0:INFO]
                high = turned.astype(BF16).astype(F32)
                middle = (turned - high).astype(BF16).astype(F32)
                low = turned - high - middle
                tile = jnp.where(row == part, high, tile)
                tile = jnp.where(row == 4 + part, middle, tile)
                tile = jnp.where(row == 8 + part, low, tile)
            outs[i][ROWS : ROWS + INFO] = tile.astype(BF16)


def stage(qs, kvs, state, last, name):
    nq, g, first = len(qs), len(kvs), state is None
    rows, keys = nq * ROWS, g * CACHE_DEV + NEW_PAD
    vmem = pl.BlockSpec(memory_space=pltpu.VMEM)
    if last:
        out_shape = tuple(jax.ShapeDtypeStruct((ROWS + INFO, DH), BF16) for _ in range(nq))
    else:
        out_shape = (
            jax.ShapeDtypeStruct((rows, 2 * DH), F32),
            jax.ShapeDtypeStruct((rows, DH), F32),
        )
    scratch = [
        pltpu.VMEM((rows, DH), BF16),
        pltpu.VMEM((DH, keys), BF16),
        pltpu.VMEM((keys, 2 * DH), BF16),
        pltpu.VMEM((nq * NEW_DEV, DH), F32),
    ]
    if last:
        scratch.append(pltpu.VMEM((rows, DH), F32))
    operands = [*qs, *kvs, *(() if first else state)]
    return pl.pallas_call(
        functools.partial(stage_kernel, nq, g, first, last),
        out_shape=out_shape,
        in_specs=[vmem] * len(operands),
        out_specs=(vmem,) * len(out_shape),
        scratch_shapes=scratch,
        compiler_params=pltpu.CompilerParams(vmem_limit_bytes=32 << 20),
        cost_estimate=pl.CostEstimate(
            flops=4 * rows * keys * DH, bytes_accessed=4 << 20, transcendentals=rows * keys
        ),
        name=name,
    )(*operands)


def combine_kernel(*refs):
    parts, out_ref = refs[:-1], refs[-1]
    n = len(parts)
    tiles = [parts[i][ROWS : ROWS + INFO].astype(F32) for i in range(n)]
    for c in range(ROWS // DH):
        logs = []
        for tile in tiles:
            line = tile[c : c + 1] + tile[4 + c : 5 + c] + tile[8 + c : 9 + c]
            logs.append(jnp.transpose(jnp.broadcast_to(line, (DH, DH))))
        peak = functools.reduce(jnp.maximum, logs)
        shares = [jnp.exp2(x - peak) for x in logs]
        total = functools.reduce(jnp.add, shares)
        summed = functools.reduce(
            jnp.add,
            [w * parts[i][c * DH : (c + 1) * DH].astype(F32) for i, w in enumerate(shares)],
        )
        result = (summed / total).astype(BF16)
        for k in range(DH // NEW_DEV):
            h = c * (DH // NEW_DEV) + k
            out_ref[:, h * DH : (h + 1) * DH] = result[k * NEW_DEV : (k + 1) * NEW_DEV]


def combine(parts):
    vmem = pl.BlockSpec(memory_space=pltpu.VMEM)
    return pl.pallas_call(
        combine_kernel,
        out_shape=jax.ShapeDtypeStruct((NEW_DEV, HPK * DH), BF16),
        in_specs=[vmem] * len(parts),
        out_specs=vmem,
        compiler_params=pltpu.CompilerParams(vmem_limit_bytes=16 << 20),
        name="combine",
    )(*parts)


def shift_y(x, d):
    pairs = [
        (z * SEQ_Y + y, z * SEQ_Y + (y + d) % SEQ_Y) for z in range(SEQ_Z) for y in range(SEQ_Y)
    ]
    return lax.ppermute(x, "seq", pairs)


def shift_z(x, d):
    pairs = [
        (z * SEQ_Y + y, (z + d) % SEQ_Z * SEQ_Y + y) for z in range(SEQ_Z) for y in range(SEQ_Y)
    ]
    return lax.ppermute(x, "seq", pairs)


def body(queries, kv_cache, new_kv, cache_len, new_pos):
    own_kv = pack_kv(kv_cache, new_kv, cache_len, new_pos)
    up = shift_y(own_kv, 1)
    down = shift_y(own_kv, -1)
    own_q = pack_q(queries, own_kv)
    offsets = (2, 1, -1)
    qs = [own_q] + [shift_z(own_q, d) for d in offsets]
    up, down, qs = lax.optimization_barrier((up, down, qs))
    next_up, next_down = shift_y(up, 1), shift_y(down, -1)
    state = stage(qs, [own_kv, up, down], None, False, "reach1")
    up, down, state = lax.optimization_barrier((next_up, next_down, state))
    next_up, next_down = shift_y(up, 1), shift_y(down, -1)
    state = stage(qs, [up, down], state, False, "reach2")
    up, down, state = lax.optimization_barrier((next_up, next_down, state))
    far = shift_y(up, 1)
    state = stage(qs, [up, down], state, False, "reach3")
    far, state = lax.optimization_barrier((far, state))
    parts = stage(qs, [far], state, True, "reach4")
    back = [parts[0]] + [shift_z(p, -d) for d, p in zip(offsets, parts[1:])]
    return combine(back)


def solution(mesh):
    return jax.shard_map(
        body,
        mesh=mesh,
        in_specs=(
            P(("batch", "seq"), "head"),
            P(("batch", "seq"), None, "head"),
            P(("batch", "seq"), None, "head"),
            P(("batch", "seq")),
            P(("batch", "seq")),
        ),
        out_specs=P(("batch", "seq"), "head"),
        check_vma=False,
    )
```

time: 139 us -> 116 us (0.83)
  blocking collectives: 72.2 us -> 0 us
  starting transfers between devices: 0.01 us -> 54.6 us
  between operations: 13.4 us -> 0.22 us
  Pallas kernels: 31.7 us -> 38.4 us
  local copies, waits for them, and re-layouts: 5.42 us -> 3.97 us
    all_to_all x2 -> x0, blocking collectives: 72.2 us -> none  [swap_y(): return lax.all_to_all(x, 'seq', 0, 0, axis_index_groups=ALONG_Y, tiled=True)]
    ppermute x0 -> x13, starting transfers between devices: none -> 54.6 us  [the longest x6 31.3 us: shift_z(): return lax.ppermute(x, 'seq', pairs)]
    ppermute x0 -> x13, waiting for transfers between devices: none -> 17.5 us  [the longest x6 17 us: shift_z(): return lax.ppermute(x, 'seq', pairs)]
    all_gather x1 -> x0, waiting for transfers between devices: 16.2 us -> none  [body(): kvs = lax.all_gather(own_kv, 'seq', axis=0, axis_index_groups=ALONG_Z)]
    pallas_call x2 -> x6, Pallas kernels: 30.1 us -> 37.4 us  [the longest x4 36.6 us: stage(): pl.pallas_call(functools.partial(stage_kernel, nq, g, first, last), out_s...]
    unnamed x10 -> x8, local copies, waits for them, and re-layouts: 5.42 us -> 3.97 us
  transfers between devices with their start and end apart: 1 -> 13, of which waited for: 1 -> 4; matrix products, arithmetic and copies ran while one was open for 0% -> 0% of each run, Pallas kernels for 0% -> 26%
where the time goes in v2:
time: 116 us; the launch traced here: 115 us
  starting transfers between devices  54.6 us (47%)
  Pallas kernels  38.4 us (33%)
  waiting for transfers between devices  17.5 us (15%)
  local copies, waits for them, and re-layouts  3.97 us (3%)
    pallas_call x4, Pallas kernels, stage(): pl.pallas_call(functools.partial(stage_kernel, nq, g, first, last), out_s...  36.6 us
    ppermute x6, starting transfers between devices, shift_z(): return lax.ppermute(x, 'seq', pairs)  31.3 us
    ppermute x7, starting transfers between devices, shift_y(): return lax.ppermute(x, 'seq', pairs)  23.3 us
    ppermute x6, waiting for transfers between devices, shift_z(): return lax.ppermute(x, 'seq', pairs)  17 us
    unnamed x8, local copies, waits for them, and re-layouts  3.97 us
  transfers between devices with their start and end apart: 13, of which 4 were waited for; matrix products, arithmetic and copies ran while one was open for 0% of the time, Pallas kernels for 26%

profile of v2, /device:TPU:6, one launch (start us, length us, event | category | flops | bytes accessed | tf_op | source)
XLA Modules:
  0.0 114.7 jit_solution(12247721178169221337)
XLA Ops:
  0.0 0.7 copy.11
  0.7 1.0 copy.10
  1.8 0.0 copy-start.1
  1.8 0.6 copy-done.1
  2.4 0.0 copy-start.2
  2.4 0.7 copy-done.2
  3.1 0.7 pack_kv.1.kv_ref.refs_4_
  3.8 5.4 %collective-permute-start.1 = (bf16[1616,128]{1,0:T(8,128)(2,1)S(1)}, bf16[1616,128]{1,0:T(8,128)(2,1)S(1)}, u32[]{:S(2)}, u32[]{:S(2)}) collective-permute-start(bf16[1616,128]{1,0:T(8,128)(2,1)S(1)} %pack_kv.1.kv_ref.refs_4_), channel_id=1, source_target_pairs={{0,28},{4,0},{8,4},{12,8},{16,12},{20,16},{24,20},{28,24},{32,60},... | collective-permute-start | bytes 1241096 | tf_op jit(solution)/shard_map/ppermute | solution.py:287
  9.2 1.9 %collective-permute-start = (bf16[1616,128]{1,0:T(8,128)(2,1)S(1)}, bf16[1616,128]{1,0:T(8,128)(2,1)S(1)}, u32[]{:S(2)}, u32[]{:S(2)}) collective-permute-start(bf16[1616,128]{1,0:T(8,128)(2,1)S(1)} %pack_kv.1.kv_ref.refs_4_), channel_id=1, source_target_pairs={{0,4},{4,8},{8,12},{12,16},{16,20},{20,24},{24,28},{28,0},{32,36},... | collective-permute-start | bytes 1241096 | tf_op jit(solution)/shard_map/ppermute | solution.py:287
  11.1 0.0 copy-start
  11.1 0.9 copy-done
  12.1 10.9 %collective-permute-start.4 = (bf16[528,128]{1,0:T(8,128)(2,1)S(1)}, bf16[528,128]{1,0:T(8,128)(2,1)S(1)}, u32[]{:S(2)}, u32[]{:S(2)}) collective-permute-start(bf16[528,128]{1,0:T(8,128)(2,1)S(1)} %pack_q.1.refs_0_), channel_id=1, source_target_pairs={{0,96},{4,100},{8,104},{12,108},{16,112},{20,116},{24,120},{28,124... | collective-permute-start | bytes 405512 | tf_op jit(solution)/shard_map/ppermute | solution.py:294
  23.0 1.9 %collective-permute-start.3 = (bf16[528,128]{1,0:T(8,128)(2,1)S(1)}, bf16[528,128]{1,0:T(8,128)(2,1)S(1)}, u32[]{:S(2)}, u32[]{:S(2)}) collective-permute-start(bf16[528,128]{1,0:T(8,128)(2,1)S(1)} %pack_q.1.refs_0_), channel_id=1, source_target_pairs={{0,32},{4,36},{8,40},{12,44},{16,48},{20,52},{24,56},{28,60},{32,6... | collective-permute-start | bytes 405512 | tf_op jit(solution)/shard_map/ppermute | solution.py:294
  24.9 4.8 %collective-permute-start.2 = (bf16[528,128]{1,0:T(8,128)(2,1)S(1)}, bf16[528,128]{1,0:T(8,128)(2,1)S(1)}, u32[]{:S(2)}, u32[]{:S(2)}) collective-permute-start(bf16[528,128]{1,0:T(8,128)(2,1)S(1)} %pack_q.1.refs_0_), channel_id=1, source_target_pairs={{0,64},{4,68},{8,72},{12,76},{16,80},{20,84},{24,88},{28,92},{32,9... | collective-permute-start | bytes 405512 | tf_op jit(solution)/shard_map/ppermute | solution.py:294
  29.7 0.0 collective-permute-done.4.refs_3_
  29.8 9.0 %collective-permute-done.3.refs_2_ = bf16[528,128]{1,0:T(8,128)(2,1)S(1)} collective-permute-done((bf16[528,128]{1,0:T(8,128)(2,1)S(1)}, bf16[528,128]{1,0:T(8,128)(2,1)S(1)}, u32[]{:S(2)}, u32[]{:S(2)}) %collective-permute-start.3) | collective-permute-done | bytes 135200 | tf_op jit(solution)/shard_map/ppermute | solution.py:294
  38.8 0.0 collective-permute-done.2.refs_1_
  38.8 0.0 collective-permute-done.1.refs_6_
  38.8 0.0 collective-permute-done.refs_5_
  38.8 2.0 %collective-permute-start.5 = (bf16[1616,128]{1,0:T(8,128)(2,1)S(1)}, bf16[1616,128]{1,0:T(8,128)(2,1)S(1)}, u32[]{:S(2)}, u32[]{:S(2)}) collective-permute-start(bf16[1616,128]{1,0:T(8,128)(2,1)S(1)} %collective-permute-done.refs_5_), channel_id=1, source_target_pairs={{0,4},{4,8},{8,12},{12,16},{16,20},{20,24},{24,28},{28,0},{32,36},... | collective-permute-start | bytes 1241096 | tf_op jit(solution)/shard_map/ppermute | solution.py:287
  40.8 5.1 %collective-permute-start.6 = (bf16[1616,128]{1,0:T(8,128)(2,1)S(1)}, bf16[1616,128]{1,0:T(8,128)(2,1)S(1)}, u32[]{:S(2)}, u32[]{:S(2)}) collective-permute-start(bf16[1616,128]{1,0:T(8,128)(2,1)S(1)} %collective-permute-done.1.refs_6_), channel_id=1, source_target_pairs={{0,28},{4,0},{8,4},{12,8},{16,12},{20,16},{24,20},{28,24},{32,60},... | collective-permute-start | bytes 1241096 | tf_op jit(solution)/shard_map/ppermute | solution.py:287
  45.9 11.2 %reach1.1 = (f32[2048,256]{1,0:T(8,128)S(1)}, f32[2048,128]{1,0:T(8,128)S(1)}) custom-call(bf16[528,128]{1,0:T(8,128)(2,1)S(1)} %pack_q.1.refs_0_, bf16[528,128]{1,0:T(8,128)(2,1)S(1)} %collective-permute-done.2.refs_1_, bf16[528,128]{1,0:T(8,128)(2,1)S(1)} %collective-permute-done.3.refs_2_, bf16[528,128]{1,0:T(8,128)(2,1)S(1)} %collective-permute-done.4.refs_3_, ...), custom_call_target="tpu_custom_call" | custom-call | flops 2550136832 | bytes 4194304 | tf_op jit(solution)/shard_map/reach1/pallas_call | solution.py:235
  57.1 0.0 collective-permute-done.5.refs_4_
  57.1 0.0 collective-permute-done.6.refs_5_
  57.1 1.9 %collective-permute-start.7 = (bf16[1616,128]{1,0:T(8,128)(2,1)S(1)}, bf16[1616,128]{1,0:T(8,128)(2,1)S(1)}, u32[]{:S(2)}, u32[]{:S(2)}) collective-permute-start(bf16[1616,128]{1,0:T(8,128)(2,1)S(1)} %collective-permute-done.5.refs_4_), channel_id=1, source_target_pairs={{0,4},{4,8},{8,12},{12,16},{16,20},{20,24},{24,28},{28,0},{32,36},... | collective-permute-start | bytes 1241096 | tf_op jit(solution)/shard_map/ppermute | solution.py:287
  59.0 5.1 %collective-permute-start.8 = (bf16[1616,128]{1,0:T(8,128)(2,1)S(1)}, bf16[1616,128]{1,0:T(8,128)(2,1)S(1)}, u32[]{:S(2)}, u32[]{:S(2)}) collective-permute-start(bf16[1616,128]{1,0:T(8,128)(2,1)S(1)} %collective-permute-done.6.refs_5_), channel_id=1, source_target_pairs={{0,28},{4,0},{8,4},{12,8},{16,12},{20,16},{24,20},{28,24},{32,60},... | collective-permute-start | bytes 1241096 | tf_op jit(solution)/shard_map/ppermute | solution.py:287
  64.1 9.5 %reach2.1 = (f32[2048,256]{1,0:T(8,128)S(1)}, f32[2048,128]{1,0:T(8,128)S(1)}) custom-call(bf16[528,128]{1,0:T(8,128)(2,1)S(1)} %pack_q.1.refs_0_, bf16[528,128]{1,0:T(8,128)(2,1)S(1)} %collective-permute-done.2.refs_1_, bf16[528,128]{1,0:T(8,128)(2,1)S(1)} %collective-permute-done.3.refs_2_, bf16[528,128]{1,0:T(8,128)(2,1)S(1)} %collective-permute-done.4.refs_3_, ...), custom_call_target="tpu_custom_call" | custom-call | flops 1744830464 | bytes 4194304 | tf_op jit(solution)/shard_map/reach2/pallas_call | solution.py:235
  73.7 0.0 collective-permute-done.7.refs_4_
  73.7 0.0 collective-permute-done.8.refs_5_
  73.7 1.9 %collective-permute-start.9 = (bf16[1616,128]{1,0:T(8,128)(2,1)S(1)}, bf16[1616,128]{1,0:T(8,128)(2,1)S(1)}, u32[]{:S(2)}, u32[]{:S(2)}) collective-permute-start(bf16[1616,128]{1,0:T(8,128)(2,1)S(1)} %collective-permute-done.7.refs_4_), channel_id=1, source_target_pairs={{0,4},{4,8},{8,12},{12,16},{16,20},{20,24},{24,28},{28,0},{32,36},... | collective-permute-start | bytes 1241096 | tf_op jit(solution)/shard_map/ppermute | solution.py:287
  75.6 9.6 %reach3.1 = (f32[2048,256]{1,0:T(8,128)S(1)}, f32[2048,128]{1,0:T(8,128)S(1)}) custom-call(bf16[528,128]{1,0:T(8,128)(2,1)S(1)} %pack_q.1.refs_0_, bf16[528,128]{1,0:T(8,128)(2,1)S(1)} %collective-permute-done.2.refs_1_, bf16[528,128]{1,0:T(8,128)(2,1)S(1)} %collective-permute-done.3.refs_2_, bf16[528,128]{1,0:T(8,128)(2,1)S(1)} %collective-permute-done.4.refs_3_, ...), custom_call_target="tpu_custom_call" | custom-call | flops 1744830464 | bytes 4194304 | tf_op jit(solution)/shard_map/reach3/pallas_call | solution.py:235
  85.2 0.5 collective-permute-done.9.refs_4_
  85.8 6.3 %reach4.1 = (bf16[528,128]{1,0:T(8,128)(2,1)S(1)}, bf16[528,128]{1,0:T(8,128)(2,1)S(1)}, bf16[528,128]{1,0:T(8,128)(2,1)S(1)}, bf16[528,128]{1,0:T(8,128)(2,1)S(1)}) custom-call(bf16[528,128]{1,0:T(8,128)(2,1)S(1)} %pack_q.1.refs_0_, bf16[528,128]{1,0:T(8,128)(2,1)S(1)} %collective-permute-done.2.refs_1_, ...), custom_call_target="tpu_custom_call" | custom-call | flops 939524096 | bytes 4194304 | tf_op jit(solution)/shard_map/reach4/pallas_call | solution.py:235
  92.1 5.0 %collective-permute-start.10 = (bf16[528,128]{1,0:T(8,128)(2,1)S(1)}, bf16[528,128]{1,0:T(8,128)(2,1)S(1)}, u32[]{:S(2)}, u32[]{:S(2)}) collective-permute-start(bf16[528,128]{1,0:T(8,128)(2,1)S(1)} %get-tuple-element.56), channel_id=1, source_target_pairs={{0,64},{4,68},{8,72},{12,76},{16,80},{20,84},{24,88},{28,92},{32,9... | collective-permute-start | bytes 405512 | tf_op jit(solution)/shard_map/ppermute | solution.py:294
  97.1 6.7 %collective-permute-start.11 = (bf16[528,128]{1,0:T(8,128)(2,1)S(1)}, bf16[528,128]{1,0:T(8,128)(2,1)S(1)}, u32[]{:S(2)}, u32[]{:S(2)}) collective-permute-start(bf16[528,128]{1,0:T(8,128)(2,1)S(1)} %get-tuple-element.57), channel_id=1, source_target_pairs={{0,96},{4,100},{8,104},{12,108},{16,112},{20,116},{24,120},{28,124... | collective-permute-start | bytes 405512 | tf_op jit(solution)/shard_map/ppermute | solution.py:294
  103.8 1.9 %collective-permute-start.12 = (bf16[528,128]{1,0:T(8,128)(2,1)S(1)}, bf16[528,128]{1,0:T(8,128)(2,1)S(1)}, u32[]{:S(2)}, u32[]{:S(2)}) collective-permute-start(bf16[528,128]{1,0:T(8,128)(2,1)S(1)} %get-tuple-element.58), channel_id=1, source_target_pairs={{0,32},{4,36},{8,40},{12,44},{16,48},{20,52},{24,56},{28,60},{32,6... | collective-permute-start | bytes 405512 | tf_op jit(solution)/shard_map/ppermute | solution.py:294
  105.7 0.0 collective-permute-done.10.refs_1_
  105.7 2.4 %collective-permute-done.11.refs_2_ = bf16[528,128]{1,0:T(8,128)(2,1)S(1)} collective-permute-done((bf16[528,128]{1,0:T(8,128)(2,1)S(1)}, bf16[528,128]{1,0:T(8,128)(2,1)S(1)}, u32[]{:S(2)}, u32[]{:S(2)}) %collective-permute-start.11) | collective-permute-done | bytes 135200 | tf_op jit(solution)/shard_map/ppermute | solution.py:294
  108.1 5.5 %collective-permute-done.12.refs_3_ = bf16[528,128]{1,0:T(8,128)(2,1)S(1)} collective-permute-done((bf16[528,128]{1,0:T(8,128)(2,1)S(1)}, bf16[528,128]{1,0:T(8,128)(2,1)S(1)}, u32[]{:S(2)}, u32[]{:S(2)}) %collective-permute-start.12) | collective-permute-done | bytes 135200 | tf_op jit(solution)/shard_map/ppermute | solution.py:294
  113.7 1.1 combine.1
  (1 shorter events, 0.0 us)
Async XLA Ops:
  1.8 0.7 copy-start.1
  2.4 0.7 copy-start.2
  3.8 35.0 %collective-permute-start.1 = (bf16[1616,128]{1,0:T(8,128)(2,1)S(1)}, bf16[1616,128]{1,0:T(8,128)(2,1)S(1)}, u32[]{:S(2)}, u32[]{:S(2)}) collective-permute-start(bf16[1616,128]{1,0:T(8,128)(2,1)S(1)} %pack_kv.1.kv_ref.refs_4_), channel_id=1, source_target_pairs={{0,28},{4,0},{8,4},{12,8},{16,12},{20,16},{24,20},{28,24},{32,60},... | collective-permute-start | bytes 1241096 | tf_op jit(solution)/shard_map/ppermute | solution.py:287
  9.2 29.6 %collective-permute-start = (bf16[1616,128]{1,0:T(8,128)(2,1)S(1)}, bf16[1616,128]{1,0:T(8,128)(2,1)S(1)}, u32[]{:S(2)}, u32[]{:S(2)}) collective-permute-start(bf16[1616,128]{1,0:T(8,128)(2,1)S(1)} %pack_kv.1.kv_ref.refs_4_), channel_id=1, source_target_pairs={{0,4},{4,8},{8,12},{12,16},{16,20},{20,24},{24,28},{28,0},{32,36},... | collective-permute-start | bytes 1241096 | tf_op jit(solution)/shard_map/ppermute | solution.py:287
  11.1 0.9 copy-start
  12.1 17.7 %collective-permute-start.4 = (bf16[528,128]{1,0:T(8,128)(2,1)S(1)}, bf16[528,128]{1,0:T(8,128)(2,1)S(1)}, u32[]{:S(2)}, u32[]{:S(2)}) collective-permute-start(bf16[528,128]{1,0:T(8,128)(2,1)S(1)} %pack_q.1.refs_0_), channel_id=1, source_target_pairs={{0,96},{4,100},{8,104},{12,108},{16,112},{20,116},{24,120},{28,124... | collective-permute-start | bytes 405512 | tf_op jit(solution)/shard_map/ppermute | solution.py:294
  23.0 15.8 %collective-permute-start.3 = (bf16[528,128]{1,0:T(8,128)(2,1)S(1)}, bf16[528,128]{1,0:T(8,128)(2,1)S(1)}, u32[]{:S(2)}, u32[]{:S(2)}) collective-permute-start(bf16[528,128]{1,0:T(8,128)(2,1)S(1)} %pack_q.1.refs_0_), channel_id=1, source_target_pairs={{0,32},{4,36},{8,40},{12,44},{16,48},{20,52},{24,56},{28,60},{32,6... | collective-permute-start | bytes 405512 | tf_op jit(solution)/shard_map/ppermute | solution.py:294
  24.9 13.8 %collective-permute-start.2 = (bf16[528,128]{1,0:T(8,128)(2,1)S(1)}, bf16[528,128]{1,0:T(8,128)(2,1)S(1)}, u32[]{:S(2)}, u32[]{:S(2)}) collective-permute-start(bf16[528,128]{1,0:T(8,128)(2,1)S(1)} %pack_q.1.refs_0_), channel_id=1, source_target_pairs={{0,64},{4,68},{8,72},{12,76},{16,80},{20,84},{24,88},{28,92},{32,9... | collective-permute-start | bytes 405512 | tf_op jit(solution)/shard_map/ppermute | solution.py:294
  38.8 18.3 %collective-permute-start.5 = (bf16[1616,128]{1,0:T(8,128)(2,1)S(1)}, bf16[1616,128]{1,0:T(8,128)(2,1)S(1)}, u32[]{:S(2)}, u32[]{:S(2)}) collective-permute-start(bf16[1616,128]{1,0:T(8,128)(2,1)S(1)} %collective-permute-done.refs_5_), channel_id=1, source_target_pairs={{0,4},{4,8},{8,12},{12,16},{16,20},{20,24},{24,28},{28,0},{32,36},... | collective-permute-start | bytes 1241096 | tf_op jit(solution)/shard_map/ppermute | solution.py:287
  40.8 16.3 %collective-permute-start.6 = (bf16[1616,128]{1,0:T(8,128)(2,1)S(1)}, bf16[1616,128]{1,0:T(8,128)(2,1)S(1)}, u32[]{:S(2)}, u32[]{:S(2)}) collective-permute-start(bf16[1616,128]{1,0:T(8,128)(2,1)S(1)} %collective-permute-done.1.refs_6_), channel_id=1, source_target_pairs={{0,28},{4,0},{8,4},{12,8},{16,12},{20,16},{24,20},{28,24},{32,60},... | collective-permute-start | bytes 1241096 | tf_op jit(solution)/shard_map/ppermute | solution.py:287
  57.1 16.6 %collective-permute-start.7 = (bf16[1616,128]{1,0:T(8,128)(2,1)S(1)}, bf16[1616,128]{1,0:T(8,128)(2,1)S(1)}, u32[]{:S(2)}, u32[]{:S(2)}) collective-permute-start(bf16[1616,128]{1,0:T(8,128)(2,1)S(1)} %collective-permute-done.5.refs_4_), channel_id=1, source_target_pairs={{0,4},{4,8},{8,12},{12,16},{16,20},{20,24},{24,28},{28,0},{32,36},... | collective-permute-start | bytes 1241096 | tf_op jit(solution)/shard_map/ppermute | solution.py:287
  59.0 14.7 %collective-permute-start.8 = (bf16[1616,128]{1,0:T(8,128)(2,1)S(1)}, bf16[1616,128]{1,0:T(8,128)(2,1)S(1)}, u32[]{:S(2)}, u32[]{:S(2)}) collective-permute-start(bf16[1616,128]{1,0:T(8,128)(2,1)S(1)} %collective-permute-done.6.refs_5_), channel_id=1, source_target_pairs={{0,28},{4,0},{8,4},{12,8},{16,12},{20,16},{24,20},{28,24},{32,60},... | collective-permute-start | bytes 1241096 | tf_op jit(solution)/shard_map/ppermute | solution.py:287
  73.7 12.0 %collective-permute-start.9 = (bf16[1616,128]{1,0:T(8,128)(2,1)S(1)}, bf16[1616,128]{1,0:T(8,128)(2,1)S(1)}, u32[]{:S(2)}, u32[]{:S(2)}) collective-permute-start(bf16[1616,128]{1,0:T(8,128)(2,1)S(1)} %collective-permute-done.7.refs_4_), channel_id=1, source_target_pairs={{0,4},{4,8},{8,12},{12,16},{16,20},{20,24},{24,28},{28,0},{32,36},... | collective-permute-start | bytes 1241096 | tf_op jit(solution)/shard_map/ppermute | solution.py:287
  92.1 13.6 %collective-permute-start.10 = (bf16[528,128]{1,0:T(8,128)(2,1)S(1)}, bf16[528,128]{1,0:T(8,128)(2,1)S(1)}, u32[]{:S(2)}, u32[]{:S(2)}) collective-permute-start(bf16[528,128]{1,0:T(8,128)(2,1)S(1)} %get-tuple-element.56), channel_id=1, source_target_pairs={{0,64},{4,68},{8,72},{12,76},{16,80},{20,84},{24,88},{28,92},{32,9... | collective-permute-start | bytes 405512 | tf_op jit(solution)/shard_map/ppermute | solution.py:294
  97.1 11.1 %collective-permute-start.11 = (bf16[528,128]{1,0:T(8,128)(2,1)S(1)}, bf16[528,128]{1,0:T(8,128)(2,1)S(1)}, u32[]{:S(2)}, u32[]{:S(2)}) collective-permute-start(bf16[528,128]{1,0:T(8,128)(2,1)S(1)} %get-tuple-element.57), channel_id=1, source_target_pairs={{0,96},{4,100},{8,104},{12,108},{16,112},{20,116},{24,120},{28,124... | collective-permute-start | bytes 405512 | tf_op jit(solution)/shard_map/ppermute | solution.py:294
  103.8 9.9 %collective-permute-start.12 = (bf16[528,128]{1,0:T(8,128)(2,1)S(1)}, bf16[528,128]{1,0:T(8,128)(2,1)S(1)}, u32[]{:S(2)}, u32[]{:S(2)}) collective-permute-start(bf16[528,128]{1,0:T(8,128)(2,1)S(1)} %get-tuple-element.58), channel_id=1, source_target_pairs={{0,32},{4,36},{8,40},{12,44},{16,48},{20,52},{24,56},{28,60},{32,6... | collective-permute-start | bytes 405512 | tf_op jit(solution)/shard_map/ppermute | solution.py:294

commit v3 on v2

--- a/solution.py
+++ b/solution.py
@@ -19,7 +19,6 @@
 SEQ_Y = 8
 ROWS = NEW_DEV * HPK
 INFO = 16
-NEW_PAD = 128
 V_AT = CACHE_DEV
 NEW_K_AT = 2 * CACHE_DEV
 NEW_V_AT = NEW_K_AT + NEW_DEV
@@ -28,6 +27,8 @@
 SCALE = math.log2(math.e) / math.sqrt(DH)
 HIDDEN = -1e30
 CHUNK = 512
+PIECE = 64
+CEILING = 2.0**60
 
 F32 = jnp.float32
 BF16 = jnp.bfloat16
@@ -116,17 +117,19 @@
         acc_out, top_out = take(2)
     qs, kk, vv, bias = take(4)
     if last:
-        lse = refs.pop(0)
-
-    lane = iota((NEW_DEV, DH), 1)
+        mix, lse = take(2)
+    new_pad = bias.shape[1]
+
+    lane = iota((NEW_DEV, new_pad), 1)
     within = lane % NEW_DEV
-    token = iota((NEW_DEV, DH), 0)
-    base = jnp.zeros((1, DH), F32)
+    token = iota((NEW_DEV, new_pad), 0)
+    base = jnp.zeros((1, new_pad), F32)
     new_row = g * CACHE_DEV
     fresh_keys = []
     for j, kv_ref in enumerate(kv_refs):
         info = kv_ref[INFO_AT:KV_ROWS].astype(F32)
-        base = jnp.where(lane[0:1] // NEW_DEV == j, info[4:5] * RUN, base)
+        wide = jnp.concatenate([info] * (new_pad // DH), axis=1)
+        base = jnp.where(lane[0:1] // NEW_DEV == j, wide[4:5] * RUN, base)
         for t in range(CACHE_DEV // DH):
             at = j * CACHE_DEV + t * DH
             kk[:, at : at + DH] = kv_ref[t * DH : (t + 1) * DH]
@@ -139,66 +142,102 @@
         dst = slice(new_row + j * NEW_DEV, new_row + (j + 1) * NEW_DEV)
         vv[dst, 0:DH] = kv_ref[NEW_V_AT:INFO_AT]
         vv[dst, DH:] = jnp.ones((NEW_DEV, DH), BF16)
-    if g * NEW_DEV < NEW_PAD:
-        rest = NEW_PAD - g * NEW_DEV
+    rest = new_pad - g * NEW_DEV
+    if rest:
         fresh_keys.append(jnp.zeros((rest, DH), F32))
-        vv[new_row + g * NEW_DEV : new_row + NEW_PAD, :] = jnp.zeros((rest, 2 * DH), BF16)
-    kk[:, new_row : new_row + NEW_PAD] = jnp.transpose(jnp.concatenate(fresh_keys, axis=0)).astype(BF16)
+        vv[new_row + g * NEW_DEV : new_row + new_pad, :] = jnp.zeros((rest, 2 * DH), BF16)
+    fresh_keys = jnp.concatenate(fresh_keys, axis=0)
+    for t in range(new_pad // DH):
+        turned = jnp.transpose(fresh_keys[t * DH : (t + 1) * DH])
+        kk[:, new_row + t * DH : new_row + (t + 1) * DH] = turned.astype(BF16)
     within_f = within.astype(F32)
     key_pos = jnp.where(within < RUN, base + within_f, LAST_RUN - RUN - base + within_f)
     token_f = token.astype(F32)
     for i, q_ref in enumerate(q_refs):
         qs[i * ROWS : (i + 1) * ROWS] = q_ref[0:ROWS]
-        start = q_ref[ROWS : ROWS + INFO].astype(F32)[0:1] * RUN
+        run = q_ref[ROWS : ROWS + INFO].astype(F32)[0:1] * RUN
+        start = jnp.concatenate([run] * (new_pad // DH), axis=1)
         pos = jnp.where(token < RUN, start + token_f, LAST_RUN - RUN - start + token_f)
         seen = (key_pos <= pos) & (lane < g * NEW_DEV)
         bias[i * NEW_DEV : (i + 1) * NEW_DEV] = jnp.where(seen, 0.0, HIDDEN)
+
+    def new_scores(q, at, count):
+        block = pl.multiple_of((at // ROWS) * NEW_DEV, NEW_DEV)
+        mask = bias[pl.ds(block, NEW_DEV), :]
+        fresh = jnp.dot(q, kk[:, new_row : new_row + new_pad], preferred_element_type=F32)
+        fresh = fresh.reshape(count // NEW_DEV, NEW_DEV, new_pad) + mask[None]
+        return fresh.reshape(count, new_pad)
+
+    def cached_scores(q, j):
+        keys = kk[:, j * CACHE_DEV : (j + 1) * CACHE_DEV]
+        return jnp.dot(q, keys, preferred_element_type=F32)
+
+    def weigh(s, top):
+        return jnp.exp2((s - top) * SCALE).astype(BF16)
+
+    def keep_result(rows, count, total, top):
+        if last:
+            acc, length = total[:, 0:DH], total[:, DH:]
+            mix[rows, :] = (acc / length).astype(BF16)
+            lse[rows, :] = top * SCALE + jnp.log2(length)
+        else:
+            acc_out[rows, :] = total
+            top_out[rows, :] = jnp.broadcast_to(top, (count, DH))
+
+    def piece(at):
+        rows = pl.ds(at, PIECE)
+        q = qs[rows, :]
+        fresh = new_scores(q, at, PIECE)
+        scores = [cached_scores(q, j) for j in range(g)]
+        top = jnp.max(fresh, axis=1, keepdims=True)
+        for s in scores:
+            top = jnp.maximum(top, jnp.max(s, axis=1, keepdims=True))
+        if not first:
+            old = top_in[rows, :]
+            top = jnp.maximum(top, old[:, 0:1])
+        total = jnp.dot(weigh(fresh, top), vv[new_row:, :], preferred_element_type=F32)
+        for j, s in enumerate(scores):
+            values = vv[j * CACHE_DEV : (j + 1) * CACHE_DEV, :]
+            total += jnp.dot(weigh(s, top), values, preferred_element_type=F32)
+        if not first:
+            keep = jnp.exp2((old - top) * SCALE)
+            total += acc_in[rows, :] * jnp.concatenate([keep, keep], axis=1)
+        keep_result(rows, PIECE, total, top)
 
     def chunk(c, carry):
         at = pl.multiple_of(c * CHUNK, CHUNK)
         rows = pl.ds(at, CHUNK)
         q = qs[rows, :]
-
-        def scores_of(lo, hi):
-            return jnp.dot(q, kk[:, lo:hi], preferred_element_type=F32)
-
-        mask = bias[pl.ds(pl.multiple_of((c * CHUNK // ROWS) * NEW_DEV, NEW_DEV), NEW_DEV), :]
-        fresh = scores_of(new_row, new_row + NEW_PAD).reshape(CHUNK // NEW_DEV, NEW_DEV, NEW_PAD)
-        fresh = (fresh + mask[None]).reshape(CHUNK, NEW_PAD)
-        scores = [scores_of(j * CACHE_DEV, (j + 1) * CACHE_DEV) for j in range(g)]
-        top = fresh
-        for s in scores:
-            for part in range(CACHE_DEV // DH):
-                top = jnp.maximum(top, s[:, part * DH : (part + 1) * DH])
-        top = jnp.max(top, axis=1, keepdims=True)
+        if first:
+            lead = jnp.dot(q, kk[:, 0:DH], preferred_element_type=F32)
+            top = jnp.max(lead, axis=1, keepdims=True)
+        else:
+            top = top_in[rows, 0:1]
+        fresh = weigh(new_scores(q, at, CHUNK), top)
+        total = jnp.dot(fresh, vv[new_row:, :], preferred_element_type=F32)
+        for j in range(g):
+            values = vv[j * CACHE_DEV : (j + 1) * CACHE_DEV, :]
+            total += jnp.dot(weigh(cached_scores(q, j), top), values, preferred_element_type=F32)
+        over = jnp.max(jnp.where(total[:, DH:] < CEILING, 0.0, 1.0)) > 0.0
         if not first:
-            old = top_in[rows, :]
-            top = jnp.maximum(top, old[:, 0:1])
-
-        def mixed(s, lo, hi):
-            weights = jnp.exp2((s - top) * SCALE).astype(BF16)
-            return jnp.dot(weights, vv[lo:hi, :], preferred_element_type=F32)
-
-        total = mixed(fresh, new_row, new_row + NEW_PAD)
-        for j, s in enumerate(scores):
-            total += mixed(s, j * CACHE_DEV, (j + 1) * CACHE_DEV)
-        if not first:
-            keep = jnp.exp2((old - top) * SCALE)
-            total += acc_in[rows, :] * jnp.concatenate([keep, keep], axis=1)
-        if last:
-            acc, length = total[:, 0:DH], total[:, DH:]
-            qs[rows, :] = (acc / length).astype(BF16)
-            lse[rows, :] = top * SCALE + jnp.log2(length)
-        else:
-            acc_out[rows, :] = total
-            top_out[rows, :] = jnp.broadcast_to(top, (CHUNK, DH))
+            total += acc_in[rows, :]
+        keep_result(rows, CHUNK, total, top)
+
+        @pl.when(over)
+        def _():
+            def careful(k, carry):
+                piece(pl.multiple_of(at + k * PIECE, PIECE))
+                return carry
+
+            lax.fori_loop(0, CHUNK // PIECE, careful, 0)
+
         return carry
 
     lax.fori_loop(0, nq * ROWS // CHUNK, chunk, 0)
     if last:
         row = iota((INFO, DH), 0)
         for i in range(nq):
-            outs[i][0:ROWS] = qs[i * ROWS : (i + 1) * ROWS]
+            outs[i][0:ROWS] = mix[i * ROWS : (i + 1) * ROWS]
             tile = jnp.zeros((INFO, DH), F32)
             for part in range(ROWS // DH):
                 at = i * ROWS + part * DH
@@ -214,7 +253,8 @@
 
 def stage(qs, kvs, state, last, name):
     nq, g, first = len(qs), len(kvs), state is None
-    rows, keys = nq * ROWS, g * CACHE_DEV + NEW_PAD
+    new_pad = -(-g * NEW_DEV // DH) * DH
+    rows, keys = nq * ROWS, g * CACHE_DEV + new_pad
     vmem = pl.BlockSpec(memory_space=pltpu.VMEM)
     if last:
         out_shape = tuple(jax.ShapeDtypeStruct((ROWS + INFO, DH), BF16) for _ in range(nq))
@@ -227,10 +267,10 @@
         pltpu.VMEM((rows, DH), BF16),
         pltpu.VMEM((DH, keys), BF16),
         pltpu.VMEM((keys, 2 * DH), BF16),
-        pltpu.VMEM((nq * NEW_DEV, DH), F32),
+        pltpu.VMEM((nq * NEW_DEV, new_pad), F32),
     ]
     if last:
-        scratch.append(pltpu.VMEM((rows, DH), F32))
+        scratch += [pltpu.VMEM((rows, DH), BF16), pltpu.VMEM((rows, DH), F32)]
     operands = [*qs, *kvs, *(() if first else state)]
     return pl.pallas_call(
         functools.partial(stage_kernel, nq, g, first, last),
@@ -240,7 +280,7 @@
         scratch_shapes=scratch,
         compiler_params=pltpu.CompilerParams(vmem_limit_bytes=32 << 20),
         cost_estimate=pl.CostEstimate(
-            flops=4 * rows * keys * DH, bytes_accessed=4 << 20, transcendentals=rows * keys
+            flops=8 * rows * keys * DH, bytes_accessed=4 << 20, transcendentals=rows * keys
         ),
         name=name,
     )(*operands)
@@ -296,20 +336,19 @@
 
 def body(queries, kv_cache, new_kv, cache_len, new_pos):
     own_kv = pack_kv(kv_cache, new_kv, cache_len, new_pos)
-    up = shift_y(own_kv, 1)
-    down = shift_y(own_kv, -1)
     own_q = pack_q(queries, own_kv)
+    own_kv, own_q = lax.optimization_barrier((own_kv, own_q))
+    up1, down1 = shift_y(own_kv, 1), shift_y(own_kv, -1)
     offsets = (2, 1, -1)
     qs = [own_q] + [shift_z(own_q, d) for d in offsets]
-    up, down, qs = lax.optimization_barrier((up, down, qs))
-    next_up, next_down = shift_y(up, 1), shift_y(down, -1)
-    state = stage(qs, [own_kv, up, down], None, False, "reach1")
-    up, down, state = lax.optimization_barrier((next_up, next_down, state))
-    next_up, next_down = shift_y(up, 1), shift_y(down, -1)
-    state = stage(qs, [up, down], state, False, "reach2")
-    up, down, state = lax.optimization_barrier((next_up, next_down, state))
-    far = shift_y(up, 1)
-    state = stage(qs, [up, down], state, False, "reach3")
+    up1, down1, qs[2], qs[3] = lax.optimization_barrier((up1, down1, qs[2], qs[3]))
+    up2, down2 = shift_y(up1, 1), shift_y(down1, -1)
+    up2, down2 = lax.optimization_barrier((up2, down2))
+    up3, down3 = shift_y(up2, 1), shift_y(down2, -1)
+    state = stage(qs, [own_kv, up1, down1, up2, down2], None, False, "reach2")
+    up3, down3, state = lax.optimization_barrier((up3, down3, state))
+    far = shift_y(up3, 1)
+    state = stage(qs, [up3, down3], state, False, "reach3")
     far, state = lax.optimization_barrier((far, state))
     parts = stage(qs, [far], state, True, "reach4")
     back = [parts[0]] + [shift_z(p, -d) for d, p in zip(offsets, parts[1:])]

time: 116 us -> 131 us (1.13)
  the two profiles are of different devices: /device:TPU:6 before, /device:TPU:88 now
where the time goes in v3:
time: 131 us; the launch traced here: 130 us
  starting transfers between devices  55.2 us (42%)
  Pallas kernels  40.8 us (31%)
  waiting for transfers between devices  29.9 us (23%)
  local copies, waits for them, and re-layouts  3.97 us (3%)
    pallas_call x3, Pallas kernels, stage(): pl.pallas_call(functools.partial(stage_kernel, nq, g, first, last), out_s...  39 us
    ppermute x6, starting transfers between devices, shift_z(): return lax.ppermute(x, 'seq', pairs)  34.5 us
    ppermute x7, starting transfers between devices, shift_y(): return lax.ppermute(x, 'seq', pairs)  20.6 us
    ppermute x6, waiting for transfers between devices, shift_z(): return lax.ppermute(x, 'seq', pairs)  15.4 us
    ppermute x7, waiting for transfers between devices, shift_y(): return lax.ppermute(x, 'seq', pairs)  14.5 us
    unnamed x8, local copies, waits for them, and re-layouts  3.97 us
  transfers between devices with their start and end apart: 13, of which 7 were waited for; matrix products, arithmetic and copies ran while one was open for 0% of the time, Pallas kernels for 27%

profile of v3, /device:TPU:88, one launch (start us, length us, event | category | flops | bytes accessed | tf_op | source)
XLA Modules:
  0.0 130.0 jit_solution(10162972716001030217)
XLA Ops:
  0.0 0.7 copy.11
  0.7 1.0 copy.10
  1.8 0.0 copy-start.1
  1.8 0.6 copy-done.1
  2.4 0.0 copy-start.2
  2.4 0.7 copy-done.2
  3.1 0.7 pack_kv.1.kv_ref.refs_4_
  3.8 0.0 copy-start
  3.8 0.9 copy-done
  4.8 2.4 %collective-permute-start.2 = (bf16[1616,128]{1,0:T(8,128)(2,1)S(1)}, bf16[1616,128]{1,0:T(8,128)(2,1)S(1)}, u32[]{:S(2)}, u32[]{:S(2)}) collective-permute-start(bf16[1616,128]{1,0:T(8,128)(2,1)S(1)} %pack_kv.1.kv_ref.refs_4_), channel_id=1, source_target_pairs={{0,28},{4,0},{8,4},{12,8},{16,12},{20,16},{24,20},{28,24},{32,60},... | collective-permute-start | bytes 1241096 | tf_op jit(solution)/shard_map/ppermute | solution.py:327
  7.1 4.7 %collective-permute-start.1 = (bf16[1616,128]{1,0:T(8,128)(2,1)S(1)}, bf16[1616,128]{1,0:T(8,128)(2,1)S(1)}, u32[]{:S(2)}, u32[]{:S(2)}) collective-permute-start(bf16[1616,128]{1,0:T(8,128)(2,1)S(1)} %pack_kv.1.kv_ref.refs_4_), channel_id=1, source_target_pairs={{0,4},{4,8},{8,12},{12,16},{16,20},{20,24},{24,28},{28,0},{32,36},... | collective-permute-start | bytes 1241096 | tf_op jit(solution)/shard_map/ppermute | solution.py:327
  11.8 10.0 %collective-permute-start.4 = (bf16[528,128]{1,0:T(8,128)(2,1)S(1)}, bf16[528,128]{1,0:T(8,128)(2,1)S(1)}, u32[]{:S(2)}, u32[]{:S(2)}) collective-permute-start(bf16[528,128]{1,0:T(8,128)(2,1)S(1)} %pack_q.1.refs_0_), channel_id=1, source_target_pairs={{0,96},{4,100},{8,104},{12,108},{16,112},{20,116},{24,120},{28,124... | collective-permute-start | bytes 405512 | tf_op jit(solution)/shard_map/ppermute | solution.py:334
  21.9 1.9 %collective-permute-start.3 = (bf16[528,128]{1,0:T(8,128)(2,1)S(1)}, bf16[528,128]{1,0:T(8,128)(2,1)S(1)}, u32[]{:S(2)}, u32[]{:S(2)}) collective-permute-start(bf16[528,128]{1,0:T(8,128)(2,1)S(1)} %pack_q.1.refs_0_), channel_id=1, source_target_pairs={{0,32},{4,36},{8,40},{12,44},{16,48},{20,52},{24,56},{28,60},{32,6... | collective-permute-start | bytes 405512 | tf_op jit(solution)/shard_map/ppermute | solution.py:334
  23.8 0.6 collective-permute-done.4.refs_3_
  24.4 7.7 %collective-permute-done.3.refs_2_ = bf16[528,128]{1,0:T(8,128)(2,1)S(1)} collective-permute-done((bf16[528,128]{1,0:T(8,128)(2,1)S(1)}, bf16[528,128]{1,0:T(8,128)(2,1)S(1)}, u32[]{:S(2)}, u32[]{:S(2)}) %collective-permute-start.3) | collective-permute-done | bytes 135200 | tf_op jit(solution)/shard_map/ppermute | solution.py:334
  32.1 0.0 collective-permute-done.2.refs_6_
  32.1 0.0 collective-permute-done.1.refs_5_
  32.1 3.5 %collective-permute-start.5 = (bf16[1616,128]{1,0:T(8,128)(2,1)S(1)}, bf16[1616,128]{1,0:T(8,128)(2,1)S(1)}, u32[]{:S(2)}, u32[]{:S(2)}) collective-permute-start(bf16[1616,128]{1,0:T(8,128)(2,1)S(1)} %collective-permute-done.1.refs_5_), channel_id=1, source_target_pairs={{0,4},{4,8},{8,12},{12,16},{16,20},{20,24},{24,28},{28,0},{32,36},... | collective-permute-start | bytes 1241096 | tf_op jit(solution)/shard_map/ppermute | solution.py:327
  35.6 2.4 %collective-permute-start.6 = (bf16[1616,128]{1,0:T(8,128)(2,1)S(1)}, bf16[1616,128]{1,0:T(8,128)(2,1)S(1)}, u32[]{:S(2)}, u32[]{:S(2)}) collective-permute-start(bf16[1616,128]{1,0:T(8,128)(2,1)S(1)} %collective-permute-done.2.refs_6_), channel_id=1, source_target_pairs={{0,28},{4,0},{8,4},{12,8},{16,12},{20,16},{24,20},{28,24},{32,60},... | collective-permute-start | bytes 1241096 | tf_op jit(solution)/shard_map/ppermute | solution.py:327
  38.0 3.3 %collective-permute-start = (bf16[528,128]{1,0:T(8,128)(2,1)S(1)}, bf16[528,128]{1,0:T(8,128)(2,1)S(1)}, u32[]{:S(2)}, u32[]{:S(2)}) collective-permute-start(bf16[528,128]{1,0:T(8,128)(2,1)S(1)} %pack_q.1.refs_0_), channel_id=1, source_target_pairs={{0,64},{4,68},{8,72},{12,76},{16,80},{20,84},{24,88},{28,92},{32,9... | collective-permute-start | bytes 405512 | tf_op jit(solution)/shard_map/ppermute | solution.py:334
  41.3 3.6 %collective-permute-done.5.refs_7_ = bf16[1616,128]{1,0:T(8,128)(2,1)S(1)} collective-permute-done((bf16[1616,128]{1,0:T(8,128)(2,1)S(1)}, bf16[1616,128]{1,0:T(8,128)(2,1)S(1)}, u32[]{:S(2)}, u32[]{:S(2)}) %collective-permute-start.5) | collective-permute-done | bytes 413728 | tf_op jit(solution)/shard_map/ppermute | solution.py:327
  44.9 4.4 %collective-permute-done.6.refs_8_ = bf16[1616,128]{1,0:T(8,128)(2,1)S(1)} collective-permute-done((bf16[1616,128]{1,0:T(8,128)(2,1)S(1)}, bf16[1616,128]{1,0:T(8,128)(2,1)S(1)}, u32[]{:S(2)}, u32[]{:S(2)}) %collective-permute-start.6) | collective-permute-done | bytes 413728 | tf_op jit(solution)/shard_map/ppermute | solution.py:327
  49.3 1.9 %collective-permute-start.7 = (bf16[1616,128]{1,0:T(8,128)(2,1)S(1)}, bf16[1616,128]{1,0:T(8,128)(2,1)S(1)}, u32[]{:S(2)}, u32[]{:S(2)}) collective-permute-start(bf16[1616,128]{1,0:T(8,128)(2,1)S(1)} %collective-permute-done.5.refs_7_), channel_id=1, source_target_pairs={{0,4},{4,8},{8,12},{12,16},{16,20},{20,24},{24,28},{28,0},{32,36},... | collective-permute-start | bytes 1241096 | tf_op jit(solution)/shard_map/ppermute | solution.py:327
  51.2 3.9 %collective-permute-start.8 = (bf16[1616,128]{1,0:T(8,128)(2,1)S(1)}, bf16[1616,128]{1,0:T(8,128)(2,1)S(1)}, u32[]{:S(2)}, u32[]{:S(2)}) collective-permute-start(bf16[1616,128]{1,0:T(8,128)(2,1)S(1)} %collective-permute-done.6.refs_8_), channel_id=1, source_target_pairs={{0,28},{4,0},{8,4},{12,8},{16,12},{20,16},{24,20},{28,24},{32,60},... | collective-permute-start | bytes 1241096 | tf_op jit(solution)/shard_map/ppermute | solution.py:327
  55.2 0.0 collective-permute-done.refs_1_
  55.2 19.0 %reach2.1 = (f32[2048,256]{1,0:T(8,128)S(1)}, f32[2048,128]{1,0:T(8,128)S(1)}) custom-call(bf16[528,128]{1,0:T(8,128)(2,1)S(1)} %pack_q.1.refs_0_, bf16[528,128]{1,0:T(8,128)(2,1)S(1)} %collective-permute-done.refs_1_, bf16[528,128]{1,0:T(8,128)(2,1)S(1)} %collective-permute-done.3.refs_2_, bf16[528,128]{1,0:T(8,128)(2,1)S(1)} %collective-permute-done.4.refs_3_, ...), custom_call_target="tpu_custom_call" | custom-call | flops 8589934592 | bytes 4194304 | tf_op jit(solution)/shard_map/reach2/pallas_call | solution.py:275
  74.2 0.0 collective-permute-done.7.refs_4_
  74.2 0.0 collective-permute-done.8.refs_5_
  74.2 1.9 %collective-permute-start.9 = (bf16[1616,128]{1,0:T(8,128)(2,1)S(1)}, bf16[1616,128]{1,0:T(8,128)(2,1)S(1)}, u32[]{:S(2)}, u32[]{:S(2)}) collective-permute-start(bf16[1616,128]{1,0:T(8,128)(2,1)S(1)} %collective-permute-done.7.refs_4_), channel_id=1, source_target_pairs={{0,4},{4,8},{8,12},{12,16},{16,20},{20,24},{24,28},{28,0},{32,36},... | collective-permute-start | bytes 1241096 | tf_op jit(solution)/shard_map/ppermute | solution.py:327
  76.1 15.7 %reach3.1 = (f32[2048,256]{1,0:T(8,128)S(1)}, f32[2048,128]{1,0:T(8,128)S(1)}) custom-call(bf16[528,128]{1,0:T(8,128)(2,1)S(1)} %pack_q.1.refs_0_, bf16[528,128]{1,0:T(8,128)(2,1)S(1)} %collective-permute-done.refs_1_, bf16[528,128]{1,0:T(8,128)(2,1)S(1)} %collective-permute-done.3.refs_2_, bf16[528,128]{1,0:T(8,128)(2,1)S(1)} %collective-permute-done.4.refs_3_, ...), custom_call_target="tpu_custom_call" | custom-call | flops 3489660928 | bytes 4194304 | tf_op jit(solution)/shard_map/reach3/pallas_call | solution.py:275
  91.9 6.4 %collective-permute-done.9.refs_4_ = bf16[1616,128]{1,0:T(8,128)(2,1)S(1)} collective-permute-done((bf16[1616,128]{1,0:T(8,128)(2,1)S(1)}, bf16[1616,128]{1,0:T(8,128)(2,1)S(1)}, u32[]{:S(2)}, u32[]{:S(2)}) %collective-permute-start.9) | collective-permute-done | bytes 413728 | tf_op jit(solution)/shard_map/ppermute | solution.py:327
  98.3 4.3 %reach4.1 = (bf16[528,128]{1,0:T(8,128)(2,1)S(1)}, bf16[528,128]{1,0:T(8,128)(2,1)S(1)}, bf16[528,128]{1,0:T(8,128)(2,1)S(1)}, bf16[528,128]{1,0:T(8,128)(2,1)S(1)}) custom-call(bf16[528,128]{1,0:T(8,128)(2,1)S(1)} %pack_q.1.refs_0_, bf16[528,128]{1,0:T(8,128)(2,1)S(1)} %collective-permute-done.refs_1_, bf16[528,128]{1,0:T(8,128)(2,1)S(1)} %collective-permute-done.3.refs_2_, ...), custom_call_target="tpu_custom_call" | custom-call | flops 1879048192 | bytes 4194304 | tf_op jit(solution)/shard_map/reach4/pallas_call | solution.py:275
  102.6 1.9 %collective-permute-start.10 = (bf16[528,128]{1,0:T(8,128)(2,1)S(1)}, bf16[528,128]{1,0:T(8,128)(2,1)S(1)}, u32[]{:S(2)}, u32[]{:S(2)}) collective-permute-start(bf16[528,128]{1,0:T(8,128)(2,1)S(1)} %get-tuple-element.48), channel_id=1, source_target_pairs={{0,64},{4,68},{8,72},{12,76},{16,80},{20,84},{24,88},{28,92},{32,9... | collective-permute-start | bytes 405512 | tf_op jit(solution)/shard_map/ppermute | solution.py:334
  104.5 15.4 %collective-permute-start.11 = (bf16[528,128]{1,0:T(8,128)(2,1)S(1)}, bf16[528,128]{1,0:T(8,128)(2,1)S(1)}, u32[]{:S(2)}, u32[]{:S(2)}) collective-permute-start(bf16[528,128]{1,0:T(8,128)(2,1)S(1)} %get-tuple-element.49), channel_id=1, source_target_pairs={{0,96},{4,100},{8,104},{12,108},{16,112},{20,116},{24,120},{28,124... | collective-permute-start | bytes 405512 | tf_op jit(solution)/shard_map/ppermute | solution.py:334
  120.0 1.9 %collective-permute-start.12 = (bf16[528,128]{1,0:T(8,128)(2,1)S(1)}, bf16[528,128]{1,0:T(8,128)(2,1)S(1)}, u32[]{:S(2)}, u32[]{:S(2)}) collective-permute-start(bf16[528,128]{1,0:T(8,128)(2,1)S(1)} %get-tuple-element.50), channel_id=1, source_target_pairs={{0,32},{4,36},{8,40},{12,44},{16,48},{20,52},{24,56},{28,60},{32,6... | collective-permute-start | bytes 405512 | tf_op jit(solution)/shard_map/ppermute | solution.py:334
  121.9 0.0 collective-permute-done.10.refs_1_
  121.9 0.6 collective-permute-done.11.refs_2_
  122.5 6.5 %collective-permute-done.12.refs_3_ = bf16[528,128]{1,0:T(8,128)(2,1)S(1)} collective-permute-done((bf16[528,128]{1,0:T(8,128)(2,1)S(1)}, bf16[528,128]{1,0:T(8,128)(2,1)S(1)}, u32[]{:S(2)}, u32[]{:S(2)}) %collective-permute-start.12) | collective-permute-done | bytes 135200 | tf_op jit(solution)/shard_map/ppermute | solution.py:334
  129.0 1.1 combine.1
  (1 shorter events, 0.0 us)
Async XLA Ops:
  1.8 0.7 copy-start.1
  2.4 0.7 copy-start.2
  3.8 0.9 copy-start
  4.8 27.4 %collective-permute-start.2 = (bf16[1616,128]{1,0:T(8,128)(2,1)S(1)}, bf16[1616,128]{1,0:T(8,128)(2,1)S(1)}, u32[]{:S(2)}, u32[]{:S(2)}) collective-permute-start(bf16[1616,128]{1,0:T(8,128)(2,1)S(1)} %pack_kv.1.kv_ref.refs_4_), channel_id=1, source_target_pairs={{0,28},{4,0},{8,4},{12,8},{16,12},{20,16},{24,20},{28,24},{32,60},... | collective-permute-start | bytes 1241096 | tf_op jit(solution)/shard_map/ppermute | solution.py:327
  7.1 25.0 %collective-permute-start.1 = (bf16[1616,128]{1,0:T(8,128)(2,1)S(1)}, bf16[1616,128]{1,0:T(8,128)(2,1)S(1)}, u32[]{:S(2)}, u32[]{:S(2)}) collective-permute-start(bf16[1616,128]{1,0:T(8,128)(2,1)S(1)} %pack_kv.1.kv_ref.refs_4_), channel_id=1, source_target_pairs={{0,4},{4,8},{8,12},{12,16},{16,20},{20,24},{24,28},{28,0},{32,36},... | collective-permute-start | bytes 1241096 | tf_op jit(solution)/shard_map/ppermute | solution.py:327
  11.8 12.6 %collective-permute-start.4 = (bf16[528,128]{1,0:T(8,128)(2,1)S(1)}, bf16[528,128]{1,0:T(8,128)(2,1)S(1)}, u32[]{:S(2)}, u32[]{:S(2)}) collective-permute-start(bf16[528,128]{1,0:T(8,128)(2,1)S(1)} %pack_q.1.refs_0_), channel_id=1, source_target_pairs={{0,96},{4,100},{8,104},{12,108},{16,112},{20,116},{24,120},{28,124... | collective-permute-start | bytes 405512 | tf_op jit(solution)/shard_map/ppermute | solution.py:334
  21.9 10.3 %collective-permute-start.3 = (bf16[528,128]{1,0:T(8,128)(2,1)S(1)}, bf16[528,128]{1,0:T(8,128)(2,1)S(1)}, u32[]{:S(2)}, u32[]{:S(2)}) collective-permute-start(bf16[528,128]{1,0:T(8,128)(2,1)S(1)} %pack_q.1.refs_0_), channel_id=1, source_target_pairs={{0,32},{4,36},{8,40},{12,44},{16,48},{20,52},{24,56},{28,60},{32,6... | collective-permute-start | bytes 405512 | tf_op jit(solution)/shard_map/ppermute | solution.py:334
  32.1 12.8 %collective-permute-start.5 = (bf16[1616,128]{1,0:T(8,128)(2,1)S(1)}, bf16[1616,128]{1,0:T(8,128)(2,1)S(1)}, u32[]{:S(2)}, u32[]{:S(2)}) collective-permute-start(bf16[1616,128]{1,0:T(8,128)(2,1)S(1)} %collective-permute-done.1.refs_5_), channel_id=1, source_target_pairs={{0,4},{4,8},{8,12},{12,16},{16,20},{20,24},{24,28},{28,0},{32,36},... | collective-permute-start | bytes 1241096 | tf_op jit(solution)/shard_map/ppermute | solution.py:327
  35.6 13.7 %collective-permute-start.6 = (bf16[1616,128]{1,0:T(8,128)(2,1)S(1)}, bf16[1616,128]{1,0:T(8,128)(2,1)S(1)}, u32[]{:S(2)}, u32[]{:S(2)}) collective-permute-start(bf16[1616,128]{1,0:T(8,128)(2,1)S(1)} %collective-permute-done.2.refs_6_), channel_id=1, source_target_pairs={{0,28},{4,0},{8,4},{12,8},{16,12},{20,16},{24,20},{28,24},{32,60},... | collective-permute-start | bytes 1241096 | tf_op jit(solution)/shard_map/ppermute | solution.py:327
  38.0 17.2 %collective-permute-start = (bf16[528,128]{1,0:T(8,128)(2,1)S(1)}, bf16[528,128]{1,0:T(8,128)(2,1)S(1)}, u32[]{:S(2)}, u32[]{:S(2)}) collective-permute-start(bf16[528,128]{1,0:T(8,128)(2,1)S(1)} %pack_q.1.refs_0_), channel_id=1, source_target_pairs={{0,64},{4,68},{8,72},{12,76},{16,80},{20,84},{24,88},{28,92},{32,9... | collective-permute-start | bytes 405512 | tf_op jit(solution)/shard_map/ppermute | solution.py:334
  49.3 24.9 %collective-permute-start.7 = (bf16[1616,128]{1,0:T(8,128)(2,1)S(1)}, bf16[1616,128]{1,0:T(8,128)(2,1)S(1)}, u32[]{:S(2)}, u32[]{:S(2)}) collective-permute-start(bf16[1616,128]{1,0:T(8,128)(2,1)S(1)} %collective-permute-done.5.refs_7_), channel_id=1, source_target_pairs={{0,4},{4,8},{8,12},{12,16},{16,20},{20,24},{24,28},{28,0},{32,36},... | collective-permute-start | bytes 1241096 | tf_op jit(solution)/shard_map/ppermute | solution.py:327
  51.2 23.0 %collective-permute-start.8 = (bf16[1616,128]{1,0:T(8,128)(2,1)S(1)}, bf16[1616,128]{1,0:T(8,128)(2,1)S(1)}, u32[]{:S(2)}, u32[]{:S(2)}) collective-permute-start(bf16[1616,128]{1,0:T(8,128)(2,1)S(1)} %collective-permute-done.6.refs_8_), channel_id=1, source_target_pairs={{0,28},{4,0},{8,4},{12,8},{16,12},{20,16},{24,20},{28,24},{32,60},... | collective-permute-start | bytes 1241096 | tf_op jit(solution)/shard_map/ppermute | solution.py:327
  74.2 24.1 %collective-permute-start.9 = (bf16[1616,128]{1,0:T(8,128)(2,1)S(1)}, bf16[1616,128]{1,0:T(8,128)(2,1)S(1)}, u32[]{:S(2)}, u32[]{:S(2)}) collective-permute-start(bf16[1616,128]{1,0:T(8,128)(2,1)S(1)} %collective-permute-done.7.refs_4_), channel_id=1, source_target_pairs={{0,4},{4,8},{8,12},{12,16},{16,20},{20,24},{24,28},{28,0},{32,36},... | collective-permute-start | bytes 1241096 | tf_op jit(solution)/shard_map/ppermute | solution.py:327
  102.6 19.3 %collective-permute-start.10 = (bf16[528,128]{1,0:T(8,128)(2,1)S(1)}, bf16[528,128]{1,0:T(8,128)(2,1)S(1)}, u32[]{:S(2)}, u32[]{:S(2)}) collective-permute-start(bf16[528,128]{1,0:T(8,128)(2,1)S(1)} %get-tuple-element.48), channel_id=1, source_target_pairs={{0,64},{4,68},{8,72},{12,76},{16,80},{20,84},{24,88},{28,92},{32,9... | collective-permute-start | bytes 405512 | tf_op jit(solution)/shard_map/ppermute | solution.py:334
  104.5 18.0 %collective-permute-start.11 = (bf16[528,128]{1,0:T(8,128)(2,1)S(1)}, bf16[528,128]{1,0:T(8,128)(2,1)S(1)}, u32[]{:S(2)}, u32[]{:S(2)}) collective-permute-start(bf16[528,128]{1,0:T(8,128)(2,1)S(1)} %get-tuple-element.49), channel_id=1, source_target_pairs={{0,96},{4,100},{8,104},{12,108},{16,112},{20,116},{24,120},{28,124... | collective-permute-start | bytes 405512 | tf_op jit(solution)/shard_map/ppermute | solution.py:334
  120.0 9.0 %collective-permute-start.12 = (bf16[528,128]{1,0:T(8,128)(2,1)S(1)}, bf16[528,128]{1,0:T(8,128)(2,1)S(1)}, u32[]{:S(2)}, u32[]{:S(2)}) collective-permute-start(bf16[528,128]{1,0:T(8,128)(2,1)S(1)} %get-tuple-element.50), channel_id=1, source_target_pairs={{0,32},{4,36},{8,40},{12,44},{16,48},{20,52},{24,56},{28,60},{32,6... | collective-permute-start | bytes 405512 | tf_op jit(solution)/shard_map/ppermute | solution.py:334

commit v4 on v3

--- a/solution.py
+++ b/solution.py
@@ -38,20 +38,26 @@
     return lax.broadcasted_iota(jnp.int32, shape, dim)
 
 
-def pack_kv_kernel(len_hbm, pos_hbm, kv_ref, new_ref, kv_out, cache_len, new_pos, sems):
+def pack_kernel(len_hbm, pos_hbm, q_hbm, kv_ref, new_ref, q_out, kv_out, cache_len, new_pos, q_ref, sems):
     copies = [
         pltpu.make_async_copy(len_hbm, cache_len, sems.at[0]),
         pltpu.make_async_copy(pos_hbm, new_pos, sems.at[1]),
+        pltpu.make_async_copy(q_hbm, q_ref, sems.at[2]),
     ]
     for copy in copies:
         copy.start()
-    kv_out[NEW_K_AT:NEW_V_AT] = new_ref[0]
-    kv_out[NEW_V_AT:INFO_AT] = new_ref[1]
+    new = new_ref[...].astype(F32)
+    kv_out[NEW_K_AT:NEW_V_AT] = new[:, 0, :].astype(BF16)
+    kv_out[NEW_V_AT:INFO_AT] = new[:, 1, :].astype(BF16)
     first_key = kv_ref[0, 0:16, :].astype(F32)[0:1]
     for copy in copies:
         copy.wait()
     info_row = iota((INFO, DH), 0)
-    info = jnp.full((INFO, DH), (new_pos[0] // RUN).astype(F32), F32)
+    run = (new_pos[0] // RUN).astype(F32)
+    info = jnp.full((INFO, DH), run, F32)
+    q_out[ROWS : ROWS + INFO] = info.astype(BF16)
+    for h in range(HPK):
+        q_out[h * NEW_DEV : (h + 1) * NEW_DEV] = q_ref[:, h * DH : (h + 1) * DH]
     kept = []
     for b in range(4):
         length = cache_len[b]
@@ -68,49 +74,39 @@
     kv_out[INFO_AT:KV_ROWS] = info.astype(BF16)
 
 
-def pack_kv(kv_cache, new_kv, cache_len, new_pos):
+def pack(queries, kv_cache, new_kv, cache_len, new_pos):
     vmem = pl.BlockSpec(memory_space=pltpu.VMEM)
-    hbm = pl.BlockSpec(memory_space=pl.ANY)
+    hbm = pl.BlockSpec(memory_space=pltpu.HBM)
     return pl.pallas_call(
-        pack_kv_kernel,
-        out_shape=jax.ShapeDtypeStruct((KV_ROWS, DH), BF16),
-        in_specs=[hbm, hbm, vmem, vmem],
-        out_specs=vmem,
+        pack_kernel,
+        out_shape=(
+            jax.ShapeDtypeStruct((ROWS + INFO, DH), BF16),
+            jax.ShapeDtypeStruct((KV_ROWS, DH), BF16),
+        ),
+        in_specs=[hbm, hbm, hbm, vmem, vmem],
+        out_specs=(vmem, vmem),
         scratch_shapes=[
             pltpu.SMEM(cache_len.shape, jnp.int32),
             pltpu.SMEM(new_pos.shape, jnp.int32),
-            pltpu.SemaphoreType.DMA((2,)),
+            pltpu.VMEM(queries.shape, BF16),
+            pltpu.SemaphoreType.DMA((3,)),
         ],
-        compiler_params=pltpu.CompilerParams(vmem_limit_bytes=16 << 20),
-        name="pack_kv",
-    )(cache_len, new_pos, jnp.transpose(kv_cache, (1, 0, 2)), jnp.transpose(new_kv, (1, 0, 2)))
-
-
-def pack_q_kernel(q_ref, kv_ref, out_ref):
-    for h in range(HPK):
-        out_ref[h * NEW_DEV : (h + 1) * NEW_DEV] = q_ref[:, h * DH : (h + 1) * DH]
-    run = kv_ref[INFO_AT:KV_ROWS].astype(F32)[4:5]
-    out_ref[ROWS : ROWS + INFO] = jnp.broadcast_to(run, (INFO, DH)).astype(BF16)
-
-
-def pack_q(queries, own_kv):
-    vmem = pl.BlockSpec(memory_space=pltpu.VMEM)
-    return pl.pallas_call(
-        pack_q_kernel,
-        out_shape=jax.ShapeDtypeStruct((ROWS + INFO, DH), BF16),
-        in_specs=[vmem, vmem],
-        out_specs=vmem,
-        compiler_params=pltpu.CompilerParams(vmem_limit_bytes=16 << 20),
-        name="pack_q",
-    )(queries, own_kv)
-
-
-def stage_kernel(nq, g, first, last, *refs):
+        compiler_params=pltpu.CompilerParams(vmem_limit_bytes=60 << 20),
+        name="pack",
+    )(cache_len, new_pos, queries, jnp.transpose(kv_cache, (1, 0, 2)), new_kv)
+
+
+def stage_kernel(nq, g, spans, last, *refs):
+    first = not spans
     refs = list(refs)
     take = lambda n: [refs.pop(0) for _ in range(n)]
     q_refs, kv_refs = take(nq), take(g)
+    states = [(0, nq * ROWS, None, None)]
     if not first:
-        acc_in, top_in = take(2)
+        states, begin = [], 0
+        for span in spans:
+            states.append((begin, span, *take(2)))
+            begin += span
     if last:
         outs = take(nq)
     else:
@@ -184,8 +180,8 @@
             acc_out[rows, :] = total
             top_out[rows, :] = jnp.broadcast_to(top, (count, DH))
 
-    def piece(at):
-        rows = pl.ds(at, PIECE)
+    def piece(at, begin, acc_in, top_in):
+        rows, past = pl.ds(at, PIECE), pl.ds(at - begin, PIECE)
         q = qs[rows, :]
         fresh = new_scores(q, at, PIECE)
         scores = [cached_scores(q, j) for j in range(g)]
@@ -193,7 +189,7 @@
         for s in scores:
             top = jnp.maximum(top, jnp.max(s, axis=1, keepdims=True))
         if not first:
-            old = top_in[rows, :]
+            old = top_in[past, :]
             top = jnp.maximum(top, old[:, 0:1])
         total = jnp.dot(weigh(fresh, top), vv[new_row:, :], preferred_element_type=F32)
         for j, s in enumerate(scores):
@@ -201,18 +197,18 @@
             total += jnp.dot(weigh(s, top), values, preferred_element_type=F32)
         if not first:
             keep = jnp.exp2((old - top) * SCALE)
-            total += acc_in[rows, :] * jnp.concatenate([keep, keep], axis=1)
+            total += acc_in[past, :] * jnp.concatenate([keep, keep], axis=1)
         keep_result(rows, PIECE, total, top)
 
-    def chunk(c, carry):
-        at = pl.multiple_of(c * CHUNK, CHUNK)
-        rows = pl.ds(at, CHUNK)
+    def chunk(begin, acc_in, top_in, c, carry):
+        at = pl.multiple_of(begin + c * CHUNK, CHUNK)
+        rows, past = pl.ds(at, CHUNK), pl.ds(pl.multiple_of(c * CHUNK, CHUNK), CHUNK)
         q = qs[rows, :]
         if first:
             lead = jnp.dot(q, kk[:, 0:DH], preferred_element_type=F32)
             top = jnp.max(lead, axis=1, keepdims=True)
         else:
-            top = top_in[rows, 0:1]
+            top = top_in[past, 0:1]
         fresh = weigh(new_scores(q, at, CHUNK), top)
         total = jnp.dot(fresh, vv[new_row:, :], preferred_element_type=F32)
         for j in range(g):
@@ -220,20 +216,21 @@
             total += jnp.dot(weigh(cached_scores(q, j), top), values, preferred_element_type=F32)
         over = jnp.max(jnp.where(total[:, DH:] < CEILING, 0.0, 1.0)) > 0.0
         if not first:
-            total += acc_in[rows, :]
+            total += acc_in[past, :]
         keep_result(rows, CHUNK, total, top)
 
         @pl.when(over)
         def _():
             def careful(k, carry):
-                piece(pl.multiple_of(at + k * PIECE, PIECE))
+                piece(pl.multiple_of(at + k * PIECE, PIECE), begin, acc_in, top_in)
                 return carry
 
             lax.fori_loop(0, CHUNK // PIECE, careful, 0)
 
         return carry
 
-    lax.fori_loop(0, nq * ROWS // CHUNK, chunk, 0)
+    for begin, span, acc_in, top_in in states:
+        lax.fori_loop(0, span // CHUNK, functools.partial(chunk, begin, acc_in, top_in), 0)
     if last:
         row = iota((INFO, DH), 0)
         for i in range(nq):
@@ -251,8 +248,9 @@
             outs[i][ROWS : ROWS + INFO] = tile.astype(BF16)
 
 
-def stage(qs, kvs, state, last, name):
-    nq, g, first = len(qs), len(kvs), state is None
+def stage(qs, kvs, states, last, name):
+    nq, g = len(qs), len(kvs)
+    spans = tuple(acc.shape[0] for acc, _ in states)
     new_pad = -(-g * NEW_DEV // DH) * DH
     rows, keys = nq * ROWS, g * CACHE_DEV + new_pad
     vmem = pl.BlockSpec(memory_space=pltpu.VMEM)
@@ -271,9 +269,9 @@
     ]
     if last:
         scratch += [pltpu.VMEM((rows, DH), BF16), pltpu.VMEM((rows, DH), F32)]
-    operands = [*qs, *kvs, *(() if first else state)]
+    operands = [*qs, *kvs, *(x for state in states for x in state)]
     return pl.pallas_call(
-        functools.partial(stage_kernel, nq, g, first, last),
+        functools.partial(stage_kernel, nq, g, spans, last),
         out_shape=out_shape,
         in_specs=[vmem] * len(operands),
         out_specs=(vmem,) * len(out_shape),
@@ -335,23 +333,24 @@
 
 
 def body(queries, kv_cache, new_kv, cache_len, new_pos):
-    own_kv = pack_kv(kv_cache, new_kv, cache_len, new_pos)
-    own_q = pack_q(queries, own_kv)
-    own_kv, own_q = lax.optimization_barrier((own_kv, own_q))
+    own_q, own_kv = pack(queries, kv_cache, new_kv, cache_len, new_pos)
     up1, down1 = shift_y(own_kv, 1), shift_y(own_kv, -1)
-    offsets = (2, 1, -1)
-    qs = [own_q] + [shift_z(own_q, d) for d in offsets]
-    up1, down1, qs[2], qs[3] = lax.optimization_barrier((up1, down1, qs[2], qs[3]))
+    offsets = (1, -1, 2)
+    q1, q2, q3 = [shift_z(own_q, d) for d in offsets]
+    up1, q1 = lax.optimization_barrier((up1, q1))
     up2, down2 = shift_y(up1, 1), shift_y(down1, -1)
-    up2, down2 = lax.optimization_barrier((up2, down2))
     up3, down3 = shift_y(up2, 1), shift_y(down2, -1)
-    state = stage(qs, [own_kv, up1, down1, up2, down2], None, False, "reach2")
-    up3, down3, state = lax.optimization_barrier((up3, down3, state))
+    near = [own_kv, up1, down1, up2, down2]
+    state = stage([own_q, q1, q2], near, [], False, "reach2")
+    up3, state = lax.optimization_barrier((up3, state))
     far = shift_y(up3, 1)
-    state = stage(qs, [up3, down3], state, False, "reach3")
+    late = stage([q3], near, [], False, "reach2_late")
+    qs = [own_q, q1, q2, q3]
+    state = stage(qs, [up3, down3], [state, late], False, "reach3")
     far, state = lax.optimization_barrier((far, state))
-    parts = stage(qs, [far], state, True, "reach4")
-    back = [parts[0]] + [shift_z(p, -d) for d, p in zip(offsets, parts[1:])]
+    parts = stage(qs, [far], [state], True, "reach4")
+    home = {d: shift_z(p, -d) for d, p in zip((2, 1, -1), (parts[3], parts[1], parts[2]))}
+    back = [parts[0], home[1], home[-1], home[2]]
     return combine(back)
 
 

time: 131 us -> 121 us (0.924)
  the two profiles are of different devices: /device:TPU:88 before, /device:TPU:6 now
where the time goes in v4:
time: 121 us; the launch traced here: 120 us
  starting transfers between devices  65.1 us (54%)
  Pallas kernels  26.3 us (22%)
  waiting for transfers between devices  25.1 us (21%)
  local copies, waits for them, and re-layouts  3.7 us (3%)
    ppermute x6, starting transfers between devices, shift_z(): return lax.ppermute(x, 'seq', pairs)  35.4 us
    ppermute x7, starting transfers between devices, shift_y(): return lax.ppermute(x, 'seq', pairs)  29.7 us
    pallas_call x4, Pallas kernels, stage(): pl.pallas_call(functools.partial(stage_kernel, nq, g, spans, last), out_s...  22.4 us
    ppermute x6, waiting for transfers between devices, shift_z(): return lax.ppermute(x, 'seq', pairs)  16.3 us
    ppermute x7, waiting for transfers between devices, shift_y(): return lax.ppermute(x, 'seq', pairs)  8.79 us
    unnamed x7, local copies, waits for them, and re-layouts  3.7 us
    pallas_call x1, Pallas kernels, pack(): pl.pallas_call(pack_kernel, out_shape=(jax.ShapeDtypeStruct((ROWS + INFO,...  2.84 us
  transfers between devices with their start and end apart: 13, of which 5 were waited for; matrix products, arithmetic and copies ran while one was open for 0% of the time, Pallas kernels for 15%

profile of v4, /device:TPU:6, one launch (start us, length us, event | category | flops | bytes accessed | tf_op | source)
XLA Modules:
  0.0 120.4 jit_solution(4260058928757290238)
XLA Ops:
  0.0 1.8 %copy.8 = bf16[768,2,128]{2,0,1:T(8,128)(2,1)} copy(bf16[768,2,128]{2,1,0:T(2,128)(2,1)} %param.6) | data formatting | bytes 786432 | tf_op args[1]
  1.8 2.8 %pack.1 = (bf16[528,128]{1,0:T(8,128)(2,1)}, bf16[1616,128]{1,0:T(8,128)(2,1)}) custom-call(s32[4]{0:T(128)} %len_hbm.1, s32[32]{0:T(128)} %pos_hbm.1, bf16[32,2048]{1,0:T(8,128)(2,1)} %q_hbm.1, bf16[2,768,128]{2,1,0:T(8,128)(2,1)} %bitcast.3, bf16[32,2,128]{2,1,0:T(2,128)(2,1)} %new_ref.1), custom_call_target="tpu_custom_call" | custom-call | tf_op jit(solution)/shard_map/pack/pallas_call | solution.py:80
  4.6 3.5 %collective-permute-start = (bf16[1616,128]{1,0:T(8,128)(2,1)}, bf16[1616,128]{1,0:T(8,128)(2,1)S(1)}, u32[]{:S(2)}, u32[]{:S(2)}) collective-permute-start(bf16[1616,128]{1,0:T(8,128)(2,1)} %get-tuple-element.26.refs_3_.refs_1_), channel_id=1, source_target_pairs={{0,4},{4,8},{8,12},{12,16},{16,20},{20,24},{24,28},{28,0},{32,36},... | collective-permute-start | bytes 1241096 | tf_op jit(solution)/shard_map/ppermute | solution.py:325
  8.1 3.8 %collective-permute-start.6 = (bf16[1616,128]{1,0:T(8,128)(2,1)}, bf16[1616,128]{1,0:T(8,128)(2,1)S(1)}, u32[]{:S(2)}, u32[]{:S(2)}) collective-permute-start(bf16[1616,128]{1,0:T(8,128)(2,1)} %get-tuple-element.26.refs_3_.refs_1_), channel_id=1, source_target_pairs={{0,28},{4,0},{8,4},{12,8},{16,12},{20,16},{24,20},{28,24},{32,60},... | collective-permute-start | bytes 1241096 | tf_op jit(solution)/shard_map/ppermute | solution.py:325
  12.0 6.1 %collective-permute-start.1 = (bf16[528,128]{1,0:T(8,128)(2,1)}, bf16[528,128]{1,0:T(8,128)(2,1)S(1)}, u32[]{:S(2)}, u32[]{:S(2)}) collective-permute-start(bf16[528,128]{1,0:T(8,128)(2,1)} %get-tuple-element.25.refs_0_), channel_id=1, source_target_pairs={{0,32},{4,36},{8,40},{12,44},{16,48},{20,52},{24,56},{28,60},{32,6... | collective-permute-start | bytes 405512 | tf_op jit(solution)/shard_map/ppermute | solution.py:332
  18.1 8.5 %collective-permute-done.1.refs_1_ = bf16[528,128]{1,0:T(8,128)(2,1)S(1)} collective-permute-done((bf16[528,128]{1,0:T(8,128)(2,1)}, bf16[528,128]{1,0:T(8,128)(2,1)S(1)}, u32[]{:S(2)}, u32[]{:S(2)}) %collective-permute-start.1) | collective-permute-done | bytes 135200 | tf_op jit(solution)/shard_map/ppermute | solution.py:332
  26.5 0.0 collective-permute-done.refs_4_.refs_2_
  26.5 0.0 collective-permute-done.6.refs_5_.refs_3_
  26.5 3.6 %collective-permute-start.7 = (bf16[1616,128]{1,0:T(8,128)(2,1)S(1)}, bf16[1616,128]{1,0:T(8,128)(2,1)S(1)}, u32[]{:S(2)}, u32[]{:S(2)}) collective-permute-start(bf16[1616,128]{1,0:T(8,128)(2,1)S(1)} %collective-permute-done.6.refs_5_.refs_3_), channel_id=1, source_target_pairs={{0,28},{4,0},{8,4},{12,8},{16,12},{20,16},{24,20},{28,24},{32,60},... | collective-permute-start | bytes 1241096 | tf_op jit(solution)/shard_map/ppermute | solution.py:325
  30.2 2.2 %collective-permute-start.4 = (bf16[1616,128]{1,0:T(8,128)(2,1)S(1)}, bf16[1616,128]{1,0:T(8,128)(2,1)S(1)}, u32[]{:S(2)}, u32[]{:S(2)}) collective-permute-start(bf16[1616,128]{1,0:T(8,128)(2,1)S(1)} %collective-permute-done.refs_4_.refs_2_), channel_id=1, source_target_pairs={{0,4},{4,8},{8,12},{12,16},{16,20},{20,24},{24,28},{28,0},{32,36},... | collective-permute-start | bytes 1241096 | tf_op jit(solution)/shard_map/ppermute | solution.py:325
  32.4 7.3 %collective-permute-start.2 = (bf16[528,128]{1,0:T(8,128)(2,1)}, bf16[528,128]{1,0:T(8,128)(2,1)S(1)}, u32[]{:S(2)}, u32[]{:S(2)}) collective-permute-start(bf16[528,128]{1,0:T(8,128)(2,1)} %get-tuple-element.25.refs_0_), channel_id=1, source_target_pairs={{0,96},{4,100},{8,104},{12,108},{16,112},{20,116},{24,120},{28,124... | collective-permute-start | bytes 405512 | tf_op jit(solution)/shard_map/ppermute | solution.py:332
  39.7 3.1 %collective-permute-start.3 = (bf16[528,128]{1,0:T(8,128)(2,1)}, bf16[528,128]{1,0:T(8,128)(2,1)S(1)}, u32[]{:S(2)}, u32[]{:S(2)}) collective-permute-start(bf16[528,128]{1,0:T(8,128)(2,1)} %get-tuple-element.25.refs_0_), channel_id=1, source_target_pairs={{0,64},{4,68},{8,72},{12,76},{16,80},{20,84},{24,88},{28,92},{32,9... | collective-permute-start | bytes 405512 | tf_op jit(solution)/shard_map/ppermute | solution.py:332
  42.8 0.0 collective-permute-done.7.refs_7_.refs_5_
  42.8 4.7 %collective-permute-start.9 = (bf16[1616,128]{1,0:T(8,128)(2,1)S(1)}, bf16[1616,128]{1,0:T(8,128)(2,1)S(1)}, u32[]{:S(2)}, u32[]{:S(2)}) collective-permute-start(bf16[1616,128]{1,0:T(8,128)(2,1)S(1)} %collective-permute-done.7.refs_7_.refs_5_), channel_id=1, source_target_pairs={{0,28},{4,0},{8,4},{12,8},{16,12},{20,16},{24,20},{28,24},{32,60},... | collective-permute-start | bytes 1241096 | tf_op jit(solution)/shard_map/ppermute | solution.py:325
  47.5 0.0 collective-permute-done.4.refs_6_.refs_4_
  47.5 1.9 %collective-permute-start.5 = (bf16[1616,128]{1,0:T(8,128)(2,1)S(1)}, bf16[1616,128]{1,0:T(8,128)(2,1)S(1)}, u32[]{:S(2)}, u32[]{:S(2)}) collective-permute-start(bf16[1616,128]{1,0:T(8,128)(2,1)S(1)} %collective-permute-done.4.refs_6_.refs_4_), channel_id=1, source_target_pairs={{0,4},{4,8},{8,12},{12,16},{16,20},{20,24},{24,28},{28,0},{32,36},... | collective-permute-start | bytes 1241096 | tf_op jit(solution)/shard_map/ppermute | solution.py:325
  49.5 0.0 collective-permute-done.2.refs_2_
  49.5 0.0 copy-start
  49.5 1.0 copy-done
  50.5 0.0 copy-start.2
  50.5 0.9 copy-done.2
  51.4 0.0 copy-start.1
  51.4 9.0 %reach2.1 = (f32[1536,256]{1,0:T(8,128)S(1)}, f32[1536,128]{1,0:T(8,128)S(1)}) custom-call(bf16[528,128]{1,0:T(8,128)(2,1)S(1)} %copy-done.2, bf16[528,128]{1,0:T(8,128)(2,1)S(1)} %collective-permute-done.1.refs_1_, bf16[528,128]{1,0:T(8,128)(2,1)S(1)} %collective-permute-done.2.refs_2_, bf16[1616,128]{1,0:T(8,128)(2,1)S(1)} %copy-done, ...), custom_call_target="tpu_custom_call" | custom-call | flops 6442450944 | bytes 4194304 | tf_op jit(solution)/shard_map/reach2/pallas_call | solution.py:273
  60.4 0.4 collective-permute-done.5.refs_4_
  60.8 9.9 %collective-permute-start.8 = (bf16[1616,128]{1,0:T(8,128)(2,1)S(1)}, bf16[1616,128]{1,0:T(8,128)(2,1)S(1)}, u32[]{:S(2)}, u32[]{:S(2)}) collective-permute-start(bf16[1616,128]{1,0:T(8,128)(2,1)S(1)} %collective-permute-done.5.refs_4_), channel_id=1, source_target_pairs={{0,4},{4,8},{8,12},{12,16},{16,20},{20,24},{24,28},{28,0},{32,36},... | collective-permute-start | bytes 1241096 | tf_op jit(solution)/shard_map/ppermute | solution.py:325
  70.8 0.0 collective-permute-done.3.refs_0_.refs_3_
  70.8 0.0 copy-done.1
  70.8 3.3 %reach2_late.1 = (f32[512,256]{1,0:T(8,128)S(1)}, f32[512,128]{1,0:T(8,128)S(1)}) custom-call(bf16[528,128]{1,0:T(8,128)(2,1)S(1)} %collective-permute-done.3.refs_0_.refs_3_, bf16[1616,128]{1,0:T(8,128)(2,1)S(1)} %copy-done.1, bf16[1616,128]{1,0:T(8,128)(2,1)S(1)} %collective-permute-done.refs_4_.refs_2_, ...), custom_call_target="tpu_custom_call" | custom-call | flops 2147483648 | bytes 4194304 | tf_op jit(solution)/shard_map/reach2_late/pallas_call | solution.py:273
  74.0 0.0 collective-permute-done.9.refs_5_
  74.1 5.8 %reach3.1 = (f32[2048,256]{1,0:T(8,128)S(1)}, f32[2048,128]{1,0:T(8,128)S(1)}) custom-call(bf16[528,128]{1,0:T(8,128)(2,1)S(1)} %copy-done.2, bf16[528,128]{1,0:T(8,128)(2,1)S(1)} %collective-permute-done.1.refs_1_, bf16[528,128]{1,0:T(8,128)(2,1)S(1)} %collective-permute-done.2.refs_2_, bf16[528,128]{1,0:T(8,128)(2,1)S(1)} %collective-permute-done.3.refs_0_.refs_3_, ...), custom_call_target="tpu_custom_call" | custom-call | flops 3489660928 | bytes 4194304 | tf_op jit(solution)/shard_map/reach3/pallas_call | solution.py:273
  79.9 8.4 %collective-permute-done.8.refs_4_ = bf16[1616,128]{1,0:T(8,128)(2,1)S(1)} collective-permute-done((bf16[1616,128]{1,0:T(8,128)(2,1)S(1)}, bf16[1616,128]{1,0:T(8,128)(2,1)S(1)}, u32[]{:S(2)}, u32[]{:S(2)}) %collective-permute-start.8) | collective-permute-done | bytes 413728 | tf_op jit(solution)/shard_map/ppermute | solution.py:325
  88.2 4.3 %reach4.1 = (bf16[528,128]{1,0:T(8,128)(2,1)S(1)}, bf16[528,128]{1,0:T(8,128)(2,1)S(1)}, bf16[528,128]{1,0:T(8,128)(2,1)S(1)}, bf16[528,128]{1,0:T(8,128)(2,1)S(1)}) custom-call(bf16[528,128]{1,0:T(8,128)(2,1)S(1)} %copy-done.2, bf16[528,128]{1,0:T(8,128)(2,1)S(1)} %collective-permute-done.1.refs_1_, bf16[528,128]{1,0:T(8,128)(2,1)S(1)} %collective-permute-done.2.refs_2_, ...), custom_call_target="tpu_custom_call" | custom-call | flops 1879048192 | bytes 4194304 | tf_op jit(solution)/shard_map/reach4/pallas_call | solution.py:273
  92.6 12.7 %collective-permute-start.10 = (bf16[528,128]{1,0:T(8,128)(2,1)S(1)}, bf16[528,128]{1,0:T(8,128)(2,1)S(1)}, u32[]{:S(2)}, u32[]{:S(2)}) collective-permute-start(bf16[528,128]{1,0:T(8,128)(2,1)S(1)} %get-tuple-element.42), channel_id=1, source_target_pairs={{0,96},{4,100},{8,104},{12,108},{16,112},{20,116},{24,120},{28,124... | collective-permute-start | bytes 405512 | tf_op jit(solution)/shard_map/ppermute | solution.py:332
  105.3 1.9 %collective-permute-start.11 = (bf16[528,128]{1,0:T(8,128)(2,1)S(1)}, bf16[528,128]{1,0:T(8,128)(2,1)S(1)}, u32[]{:S(2)}, u32[]{:S(2)}) collective-permute-start(bf16[528,128]{1,0:T(8,128)(2,1)S(1)} %get-tuple-element.43), channel_id=1, source_target_pairs={{0,32},{4,36},{8,40},{12,44},{16,48},{20,52},{24,56},{28,60},{32,6... | collective-permute-start | bytes 405512 | tf_op jit(solution)/shard_map/ppermute | solution.py:332
  107.2 4.3 %collective-permute-start.12 = (bf16[528,128]{1,0:T(8,128)(2,1)S(1)}, bf16[528,128]{1,0:T(8,128)(2,1)S(1)}, u32[]{:S(2)}, u32[]{:S(2)}) collective-permute-start(bf16[528,128]{1,0:T(8,128)(2,1)S(1)} %get-tuple-element.44), channel_id=1, source_target_pairs={{0,64},{4,68},{8,72},{12,76},{16,80},{20,84},{24,88},{28,92},{32,9... | collective-permute-start | bytes 405512 | tf_op jit(solution)/shard_map/ppermute | solution.py:332
  111.5 0.0 collective-permute-done.10.refs_1_
  111.5 4.5 %collective-permute-done.11.refs_2_ = bf16[528,128]{1,0:T(8,128)(2,1)S(1)} collective-permute-done((bf16[528,128]{1,0:T(8,128)(2,1)S(1)}, bf16[528,128]{1,0:T(8,128)(2,1)S(1)}, u32[]{:S(2)}, u32[]{:S(2)}) %collective-permute-start.11) | collective-permute-done | bytes 135200 | tf_op jit(solution)/shard_map/ppermute | solution.py:332
  116.0 3.3 %collective-permute-done.12.refs_3_ = bf16[528,128]{1,0:T(8,128)(2,1)S(1)} collective-permute-done((bf16[528,128]{1,0:T(8,128)(2,1)S(1)}, bf16[528,128]{1,0:T(8,128)(2,1)S(1)}, u32[]{:S(2)}, u32[]{:S(2)}) %collective-permute-start.12) | collective-permute-done | bytes 135200 | tf_op jit(solution)/shard_map/ppermute | solution.py:332
  119.3 1.1 combine.1
Async XLA Ops:
  4.6 21.9 %collective-permute-start = (bf16[1616,128]{1,0:T(8,128)(2,1)}, bf16[1616,128]{1,0:T(8,128)(2,1)S(1)}, u32[]{:S(2)}, u32[]{:S(2)}) collective-permute-start(bf16[1616,128]{1,0:T(8,128)(2,1)} %get-tuple-element.26.refs_3_.refs_1_), channel_id=1, source_target_pairs={{0,4},{4,8},{8,12},{12,16},{16,20},{20,24},{24,28},{28,0},{32,36},... | collective-permute-start | bytes 1241096 | tf_op jit(solution)/shard_map/ppermute | solution.py:325
  8.1 18.4 %collective-permute-start.6 = (bf16[1616,128]{1,0:T(8,128)(2,1)}, bf16[1616,128]{1,0:T(8,128)(2,1)S(1)}, u32[]{:S(2)}, u32[]{:S(2)}) collective-permute-start(bf16[1616,128]{1,0:T(8,128)(2,1)} %get-tuple-element.26.refs_3_.refs_1_), channel_id=1, source_target_pairs={{0,28},{4,0},{8,4},{12,8},{16,12},{20,16},{24,20},{28,24},{32,60},... | collective-permute-start | bytes 1241096 | tf_op jit(solution)/shard_map/ppermute | solution.py:325
  12.0 14.6 %collective-permute-start.1 = (bf16[528,128]{1,0:T(8,128)(2,1)}, bf16[528,128]{1,0:T(8,128)(2,1)S(1)}, u32[]{:S(2)}, u32[]{:S(2)}) collective-permute-start(bf16[528,128]{1,0:T(8,128)(2,1)} %get-tuple-element.25.refs_0_), channel_id=1, source_target_pairs={{0,32},{4,36},{8,40},{12,44},{16,48},{20,52},{24,56},{28,60},{32,6... | collective-permute-start | bytes 405512 | tf_op jit(solution)/shard_map/ppermute | solution.py:332
  26.5 16.2 %collective-permute-start.7 = (bf16[1616,128]{1,0:T(8,128)(2,1)S(1)}, bf16[1616,128]{1,0:T(8,128)(2,1)S(1)}, u32[]{:S(2)}, u32[]{:S(2)}) collective-permute-start(bf16[1616,128]{1,0:T(8,128)(2,1)S(1)} %collective-permute-done.6.refs_5_.refs_3_), channel_id=1, source_target_pairs={{0,28},{4,0},{8,4},{12,8},{16,12},{20,16},{24,20},{28,24},{32,60},... | collective-permute-start | bytes 1241096 | tf_op jit(solution)/shard_map/ppermute | solution.py:325
  30.2 17.4 %collective-permute-start.4 = (bf16[1616,128]{1,0:T(8,128)(2,1)S(1)}, bf16[1616,128]{1,0:T(8,128)(2,1)S(1)}, u32[]{:S(2)}, u32[]{:S(2)}) collective-permute-start(bf16[1616,128]{1,0:T(8,128)(2,1)S(1)} %collective-permute-done.refs_4_.refs_2_), channel_id=1, source_target_pairs={{0,4},{4,8},{8,12},{12,16},{16,20},{20,24},{24,28},{28,0},{32,36},... | collective-permute-start | bytes 1241096 | tf_op jit(solution)/shard_map/ppermute | solution.py:325
  32.4 17.1 %collective-permute-start.2 = (bf16[528,128]{1,0:T(8,128)(2,1)}, bf16[528,128]{1,0:T(8,128)(2,1)S(1)}, u32[]{:S(2)}, u32[]{:S(2)}) collective-permute-start(bf16[528,128]{1,0:T(8,128)(2,1)} %get-tuple-element.25.refs_0_), channel_id=1, source_target_pairs={{0,96},{4,100},{8,104},{12,108},{16,112},{20,116},{24,120},{28,124... | collective-permute-start | bytes 405512 | tf_op jit(solution)/shard_map/ppermute | solution.py:332
  39.7 31.1 %collective-permute-start.3 = (bf16[528,128]{1,0:T(8,128)(2,1)}, bf16[528,128]{1,0:T(8,128)(2,1)S(1)}, u32[]{:S(2)}, u32[]{:S(2)}) collective-permute-start(bf16[528,128]{1,0:T(8,128)(2,1)} %get-tuple-element.25.refs_0_), channel_id=1, source_target_pairs={{0,64},{4,68},{8,72},{12,76},{16,80},{20,84},{24,88},{28,92},{32,9... | collective-permute-start | bytes 405512 | tf_op jit(solution)/shard_map/ppermute | solution.py:332
  42.8 31.3 %collective-permute-start.9 = (bf16[1616,128]{1,0:T(8,128)(2,1)S(1)}, bf16[1616,128]{1,0:T(8,128)(2,1)S(1)}, u32[]{:S(2)}, u32[]{:S(2)}) collective-permute-start(bf16[1616,128]{1,0:T(8,128)(2,1)S(1)} %collective-permute-done.7.refs_7_.refs_5_), channel_id=1, source_target_pairs={{0,28},{4,0},{8,4},{12,8},{16,12},{20,16},{24,20},{28,24},{32,60},... | collective-permute-start | bytes 1241096 | tf_op jit(solution)/shard_map/ppermute | solution.py:325
  47.5 13.3 %collective-permute-start.5 = (bf16[1616,128]{1,0:T(8,128)(2,1)S(1)}, bf16[1616,128]{1,0:T(8,128)(2,1)S(1)}, u32[]{:S(2)}, u32[]{:S(2)}) collective-permute-start(bf16[1616,128]{1,0:T(8,128)(2,1)S(1)} %collective-permute-done.4.refs_6_.refs_4_), channel_id=1, source_target_pairs={{0,4},{4,8},{8,12},{12,16},{16,20},{20,24},{24,28},{28,0},{32,36},... | collective-permute-start | bytes 1241096 | tf_op jit(solution)/shard_map/ppermute | solution.py:325
  49.5 1.0 copy-start
  50.5 0.9 copy-start.2
  51.4 19.4 %copy-start.1 = (bf16[1616,128]{1,0:T(8,128)(2,1)S(1)}, bf16[1616,128]{1,0:T(8,128)(2,1)}, u32[]{:S(2)}) copy-start(bf16[1616,128]{1,0:T(8,128)(2,1)} %get-tuple-element.26.refs_3_.refs_1_) | copy-start | bytes 1241092
  60.8 27.4 %collective-permute-start.8 = (bf16[1616,128]{1,0:T(8,128)(2,1)S(1)}, bf16[1616,128]{1,0:T(8,128)(2,1)S(1)}, u32[]{:S(2)}, u32[]{:S(2)}) collective-permute-start(bf16[1616,128]{1,0:T(8,128)(2,1)S(1)} %collective-permute-done.5.refs_4_), channel_id=1, source_target_pairs={{0,4},{4,8},{8,12},{12,16},{16,20},{20,24},{24,28},{28,0},{32,36},... | collective-permute-start | bytes 1241096 | tf_op jit(solution)/shard_map/ppermute | solution.py:325
  92.6 18.9 %collective-permute-start.10 = (bf16[528,128]{1,0:T(8,128)(2,1)S(1)}, bf16[528,128]{1,0:T(8,128)(2,1)S(1)}, u32[]{:S(2)}, u32[]{:S(2)}) collective-permute-start(bf16[528,128]{1,0:T(8,128)(2,1)S(1)} %get-tuple-element.42), channel_id=1, source_target_pairs={{0,96},{4,100},{8,104},{12,108},{16,112},{20,116},{24,120},{28,124... | collective-permute-start | bytes 405512 | tf_op jit(solution)/shard_map/ppermute | solution.py:332
  105.3 10.7 %collective-permute-start.11 = (bf16[528,128]{1,0:T(8,128)(2,1)S(1)}, bf16[528,128]{1,0:T(8,128)(2,1)S(1)}, u32[]{:S(2)}, u32[]{:S(2)}) collective-permute-start(bf16[528,128]{1,0:T(8,128)(2,1)S(1)} %get-tuple-element.43), channel_id=1, source_target_pairs={{0,32},{4,36},{8,40},{12,44},{16,48},{20,52},{24,56},{28,60},{32,6... | collective-permute-start | bytes 405512 | tf_op jit(solution)/shard_map/ppermute | solution.py:332
  107.2 12.1 %collective-permute-start.12 = (bf16[528,128]{1,0:T(8,128)(2,1)S(1)}, bf16[528,128]{1,0:T(8,128)(2,1)S(1)}, u32[]{:S(2)}, u32[]{:S(2)}) collective-permute-start(bf16[528,128]{1,0:T(8,128)(2,1)S(1)} %get-tuple-element.44), channel_id=1, source_target_pairs={{0,64},{4,68},{8,72},{12,76},{16,80},{20,84},{24,88},{28,92},{32,9... | collective-permute-start | bytes 405512 | tf_op jit(solution)/shard_map/ppermute | solution.py:332

commit v5 on v3

--- a/solution.py
+++ b/solution.py
@@ -28,6 +28,7 @@
 HIDDEN = -1e30
 CHUNK = 512
 PIECE = 64
+UNROLL = 2
 CEILING = 2.0**60
 
 F32 = jnp.float32
@@ -105,12 +106,17 @@
     )(queries, own_kv)
 
 
-def stage_kernel(nq, g, first, last, *refs):
+def stage_kernel(nq, g, spans, last, *refs):
+    first = not spans
     refs = list(refs)
     take = lambda n: [refs.pop(0) for _ in range(n)]
     q_refs, kv_refs = take(nq), take(g)
+    states = [(0, nq * ROWS, None, None)]
     if not first:
-        acc_in, top_in = take(2)
+        states, begin = [], 0
+        for span in spans:
+            states.append((begin, span, *take(2)))
+            begin += span
     if last:
         outs = take(nq)
     else:
@@ -184,8 +190,8 @@
             acc_out[rows, :] = total
             top_out[rows, :] = jnp.broadcast_to(top, (count, DH))
 
-    def piece(at):
-        rows = pl.ds(at, PIECE)
+    def piece(at, begin, acc_in, top_in):
+        rows, past = pl.ds(at, PIECE), pl.ds(at - begin, PIECE)
         q = qs[rows, :]
         fresh = new_scores(q, at, PIECE)
         scores = [cached_scores(q, j) for j in range(g)]
@@ -193,7 +199,7 @@
         for s in scores:
             top = jnp.maximum(top, jnp.max(s, axis=1, keepdims=True))
         if not first:
-            old = top_in[rows, :]
+            old = top_in[past, :]
             top = jnp.maximum(top, old[:, 0:1])
         total = jnp.dot(weigh(fresh, top), vv[new_row:, :], preferred_element_type=F32)
         for j, s in enumerate(scores):
@@ -201,39 +207,47 @@
             total += jnp.dot(weigh(s, top), values, preferred_element_type=F32)
         if not first:
             keep = jnp.exp2((old - top) * SCALE)
-            total += acc_in[rows, :] * jnp.concatenate([keep, keep], axis=1)
+            total += acc_in[past, :] * jnp.concatenate([keep, keep], axis=1)
         keep_result(rows, PIECE, total, top)
 
-    def chunk(c, carry):
-        at = pl.multiple_of(c * CHUNK, CHUNK)
-        rows = pl.ds(at, CHUNK)
+    def chunk(begin, acc_in, top_in, c, carry):
+        at = pl.multiple_of(begin + c * CHUNK, CHUNK)
+        rows, past = pl.ds(at, CHUNK), pl.ds(pl.multiple_of(c * CHUNK, CHUNK), CHUNK)
         q = qs[rows, :]
         if first:
             lead = jnp.dot(q, kk[:, 0:DH], preferred_element_type=F32)
             top = jnp.max(lead, axis=1, keepdims=True)
         else:
-            top = top_in[rows, 0:1]
+            top = top_in[past, 0:1]
         fresh = weigh(new_scores(q, at, CHUNK), top)
         total = jnp.dot(fresh, vv[new_row:, :], preferred_element_type=F32)
         for j in range(g):
             values = vv[j * CACHE_DEV : (j + 1) * CACHE_DEV, :]
             total += jnp.dot(weigh(cached_scores(q, j), top), values, preferred_element_type=F32)
-        over = jnp.max(jnp.where(total[:, DH:] < CEILING, 0.0, 1.0)) > 0.0
+        over = jnp.where(total[:, DH:] < CEILING, 0.0, 1.0).reshape(CHUNK // 8, 8, DH)
+        carry = jnp.maximum(carry, jnp.max(over, axis=0))
         if not first:
-            total += acc_in[rows, :]
+            total += acc_in[past, :]
         keep_result(rows, CHUNK, total, top)
 
-        @pl.when(over)
-        def _():
+        return carry
+
+    worst = jnp.zeros((8, DH), F32)
+    for begin, span, acc_in, top_in in states:
+        step = functools.partial(chunk, begin, acc_in, top_in)
+        count = span // CHUNK
+        worst = lax.fori_loop(0, count, step, worst, unroll=UNROLL if count % UNROLL == 0 else 1)
+
+    @pl.when(jnp.max(worst) > 0.0)
+    def _():
+        for begin, span, acc_in, top_in in states:
+
             def careful(k, carry):
-                piece(pl.multiple_of(at + k * PIECE, PIECE))
+                piece(pl.multiple_of(begin + k * PIECE, PIECE), begin, acc_in, top_in)
                 return carry
 
-            lax.fori_loop(0, CHUNK // PIECE, careful, 0)
-
-        return carry
-
-    lax.fori_loop(0, nq * ROWS // CHUNK, chunk, 0)
+            lax.fori_loop(0, span // PIECE, careful, 0)
+
     if last:
         row = iota((INFO, DH), 0)
         for i in range(nq):
@@ -251,8 +265,9 @@
             outs[i][ROWS : ROWS + INFO] = tile.astype(BF16)
 
 
-def stage(qs, kvs, state, last, name):
-    nq, g, first = len(qs), len(kvs), state is None
+def stage(qs, kvs, states, last, name):
+    nq, g = len(qs), len(kvs)
+    spans = tuple(acc.shape[0] for acc, _ in states)
     new_pad = -(-g * NEW_DEV // DH) * DH
     rows, keys = nq * ROWS, g * CACHE_DEV + new_pad
     vmem = pl.BlockSpec(memory_space=pltpu.VMEM)
@@ -271,9 +286,9 @@
     ]
     if last:
         scratch += [pltpu.VMEM((rows, DH), BF16), pltpu.VMEM((rows, DH), F32)]
-    operands = [*qs, *kvs, *(() if first else state)]
+    operands = [*qs, *kvs, *(x for state in states for x in state)]
     return pl.pallas_call(
-        functools.partial(stage_kernel, nq, g, first, last),
+        functools.partial(stage_kernel, nq, g, spans, last),
         out_shape=out_shape,
         in_specs=[vmem] * len(operands),
         out_specs=(vmem,) * len(out_shape),
@@ -339,19 +354,19 @@
     own_q = pack_q(queries, own_kv)
     own_kv, own_q = lax.optimization_barrier((own_kv, own_q))
     up1, down1 = shift_y(own_kv, 1), shift_y(own_kv, -1)
-    offsets = (2, 1, -1)
-    qs = [own_q] + [shift_z(own_q, d) for d in offsets]
-    up1, down1, qs[2], qs[3] = lax.optimization_barrier((up1, down1, qs[2], qs[3]))
+    offsets = (1, -1, 2)
+    q1, q2, q3 = [shift_z(own_q, d) for d in offsets]
+    up1, q1 = lax.optimization_barrier((up1, q1))
     up2, down2 = shift_y(up1, 1), shift_y(down1, -1)
-    up2, down2 = lax.optimization_barrier((up2, down2))
     up3, down3 = shift_y(up2, 1), shift_y(down2, -1)
-    state = stage(qs, [own_kv, up1, down1, up2, down2], None, False, "reach2")
-    up3, down3, state = lax.optimization_barrier((up3, down3, state))
+    qs = [own_q, q1, q2, q3]
+    state = stage(qs, [own_kv, up1, down1], [], False, "reach1")
+    up3, state = lax.optimization_barrier((up3, state))
     far = shift_y(up3, 1)
-    state = stage(qs, [up3, down3], state, False, "reach3")
+    state = stage(qs, [up2, down2, up3, down3], [state], False, "reach3")
     far, state = lax.optimization_barrier((far, state))
-    parts = stage(qs, [far], state, True, "reach4")
-    back = [parts[0]] + [shift_z(p, -d) for d, p in zip(offsets, parts[1:])]
+    parts = stage(qs, [far], [state], True, "reach4")
+    back = [parts[0], shift_z(parts[3], -2), shift_z(parts[1], -1), shift_z(parts[2], 1)]
     return combine(back)
 
 

time: 131 us -> 154 us (1.18)
  the two profiles are of different devices: /device:TPU:88 before, /device:TPU:102 now
where the time goes in v5:
time: 154 us; the launch traced here: 153 us
  starting transfers between devices  64.8 us (42%)
  Pallas kernels  63.9 us (41%)
  waiting for transfers between devices  20.3 us (13%)
  local copies, waits for them, and re-layouts  3.97 us (3%)
    pallas_call x3, Pallas kernels, stage(): pl.pallas_call(functools.partial(stage_kernel, nq, g, spans, last), out_s...  62.1 us
    ppermute x7, starting transfers between devices, shift_y(): return lax.ppermute(x, 'seq', pairs)  42.4 us
    ppermute x6, starting transfers between devices, shift_z(): return lax.ppermute(x, 'seq', pairs)  22.4 us
    ppermute x6, waiting for transfers between devices, shift_z(): return lax.ppermute(x, 'seq', pairs)  18.2 us
    unnamed x8, local copies, waits for them, and re-layouts  3.97 us
  transfers between devices with their start and end apart: 13, of which 6 were waited for; matrix products, arithmetic and copies ran while one was open for 0% of the time, Pallas kernels for 27%

profile of v5, /device:TPU:102, one launch (start us, length us, event | category | flops | bytes accessed | tf_op | source)
XLA Modules:
  0.0 153.2 jit_solution(3261086158995296343)
XLA Ops:
  0.0 0.7 copy.11
  0.7 1.0 copy.10
  1.8 0.0 copy-start.1
  1.8 0.6 copy-done.1
  2.4 0.0 copy-start.2
  2.4 0.7 copy-done.2
  3.1 0.7 pack_kv.1.kv_ref.refs_4_
  3.8 0.0 copy-start
  3.8 0.9 copy-done
  4.8 2.6 %collective-permute-start = (bf16[1616,128]{1,0:T(8,128)(2,1)S(1)}, bf16[1616,128]{1,0:T(8,128)(2,1)S(1)}, u32[]{:S(2)}, u32[]{:S(2)}) collective-permute-start(bf16[1616,128]{1,0:T(8,128)(2,1)S(1)} %pack_kv.1.kv_ref.refs_4_), channel_id=1, source_target_pairs={{0,4},{4,8},{8,12},{12,16},{16,20},{20,24},{24,28},{28,0},{32,36},... | collective-permute-start | bytes 1241096 | tf_op jit(solution)/shard_map/ppermute | solution.py:342
  7.3 4.5 %collective-permute-start.6 = (bf16[1616,128]{1,0:T(8,128)(2,1)S(1)}, bf16[1616,128]{1,0:T(8,128)(2,1)S(1)}, u32[]{:S(2)}, u32[]{:S(2)}) collective-permute-start(bf16[1616,128]{1,0:T(8,128)(2,1)S(1)} %pack_kv.1.kv_ref.refs_4_), channel_id=1, source_target_pairs={{0,28},{4,0},{8,4},{12,8},{16,12},{20,16},{24,20},{28,24},{32,60},... | collective-permute-start | bytes 1241096 | tf_op jit(solution)/shard_map/ppermute | solution.py:342
  11.8 6.1 %collective-permute-start.1 = (bf16[528,128]{1,0:T(8,128)(2,1)S(1)}, bf16[528,128]{1,0:T(8,128)(2,1)S(1)}, u32[]{:S(2)}, u32[]{:S(2)}) collective-permute-start(bf16[528,128]{1,0:T(8,128)(2,1)S(1)} %pack_q.1.refs_0_), channel_id=1, source_target_pairs={{0,32},{4,36},{8,40},{12,44},{16,48},{20,52},{24,56},{28,60},{32,6... | collective-permute-start | bytes 405512 | tf_op jit(solution)/shard_map/ppermute | solution.py:349
  17.9 9.8 %collective-permute-done.1.refs_1_ = bf16[528,128]{1,0:T(8,128)(2,1)S(1)} collective-permute-done((bf16[528,128]{1,0:T(8,128)(2,1)S(1)}, bf16[528,128]{1,0:T(8,128)(2,1)S(1)}, u32[]{:S(2)}, u32[]{:S(2)}) %collective-permute-start.1) | collective-permute-done | bytes 135200 | tf_op jit(solution)/shard_map/ppermute | solution.py:349
  27.8 0.0 collective-permute-done.refs_5_
  27.8 0.0 collective-permute-done.6.refs_6_
  27.8 2.2 %collective-permute-start.8 = (bf16[1616,128]{1,0:T(8,128)(2,1)S(1)}, bf16[1616,128]{1,0:T(8,128)(2,1)S(1)}, u32[]{:S(2)}, u32[]{:S(2)}) collective-permute-start(bf16[1616,128]{1,0:T(8,128)(2,1)S(1)} %collective-permute-done.6.refs_6_), channel_id=1, source_target_pairs={{0,28},{4,0},{8,4},{12,8},{16,12},{20,16},{24,20},{28,24},{32,60},... | collective-permute-start | bytes 1241096 | tf_op jit(solution)/shard_map/ppermute | solution.py:342
  30.0 3.6 %collective-permute-start.4 = (bf16[1616,128]{1,0:T(8,128)(2,1)S(1)}, bf16[1616,128]{1,0:T(8,128)(2,1)S(1)}, u32[]{:S(2)}, u32[]{:S(2)}) collective-permute-start(bf16[1616,128]{1,0:T(8,128)(2,1)S(1)} %collective-permute-done.refs_5_), channel_id=1, source_target_pairs={{0,4},{4,8},{8,12},{12,16},{16,20},{20,24},{24,28},{28,0},{32,36},... | collective-permute-start | bytes 1241096 | tf_op jit(solution)/shard_map/ppermute | solution.py:342
  33.6 5.8 %collective-permute-start.3 = (bf16[528,128]{1,0:T(8,128)(2,1)S(1)}, bf16[528,128]{1,0:T(8,128)(2,1)S(1)}, u32[]{:S(2)}, u32[]{:S(2)}) collective-permute-start(bf16[528,128]{1,0:T(8,128)(2,1)S(1)} %pack_q.1.refs_0_), channel_id=1, source_target_pairs={{0,64},{4,68},{8,72},{12,76},{16,80},{20,84},{24,88},{28,92},{32,9... | collective-permute-start | bytes 405512 | tf_op jit(solution)/shard_map/ppermute | solution.py:349
  39.4 1.9 %collective-permute-start.2 = (bf16[528,128]{1,0:T(8,128)(2,1)S(1)}, bf16[528,128]{1,0:T(8,128)(2,1)S(1)}, u32[]{:S(2)}, u32[]{:S(2)}) collective-permute-start(bf16[528,128]{1,0:T(8,128)(2,1)S(1)} %pack_q.1.refs_0_), channel_id=1, source_target_pairs={{0,96},{4,100},{8,104},{12,108},{16,112},{20,116},{24,120},{28,124... | collective-permute-start | bytes 405512 | tf_op jit(solution)/shard_map/ppermute | solution.py:349
  41.3 0.0 collective-permute-done.8.refs_5_
  41.3 3.6 %collective-permute-start.9 = (bf16[1616,128]{1,0:T(8,128)(2,1)S(1)}, bf16[1616,128]{1,0:T(8,128)(2,1)S(1)}, u32[]{:S(2)}, u32[]{:S(2)}) collective-permute-start(bf16[1616,128]{1,0:T(8,128)(2,1)S(1)} %collective-permute-done.8.refs_5_), channel_id=1, source_target_pairs={{0,28},{4,0},{8,4},{12,8},{16,12},{20,16},{24,20},{28,24},{32,60},... | collective-permute-start | bytes 1241096 | tf_op jit(solution)/shard_map/ppermute | solution.py:342
  45.0 0.0 collective-permute-done.4.refs_4_
  45.0 2.2 %collective-permute-start.5 = (bf16[1616,128]{1,0:T(8,128)(2,1)S(1)}, bf16[1616,128]{1,0:T(8,128)(2,1)S(1)}, u32[]{:S(2)}, u32[]{:S(2)}) collective-permute-start(bf16[1616,128]{1,0:T(8,128)(2,1)S(1)} %collective-permute-done.4.refs_4_), channel_id=1, source_target_pairs={{0,4},{4,8},{8,12},{12,16},{16,20},{20,24},{24,28},{28,0},{32,36},... | collective-permute-start | bytes 1241096 | tf_op jit(solution)/shard_map/ppermute | solution.py:342
  47.2 0.0 collective-permute-done.3.refs_3_
  47.2 1.8 %collective-permute-done.2.refs_2_ = bf16[528,128]{1,0:T(8,128)(2,1)S(1)} collective-permute-done((bf16[528,128]{1,0:T(8,128)(2,1)S(1)}, bf16[528,128]{1,0:T(8,128)(2,1)S(1)}, u32[]{:S(2)}, u32[]{:S(2)}) %collective-permute-start.2) | collective-permute-done | bytes 135200 | tf_op jit(solution)/shard_map/ppermute | solution.py:349
  49.0 6.9 %reach1.1 = (f32[2048,256]{1,0:T(8,128)S(1)}, f32[2048,128]{1,0:T(8,128)S(1)}) custom-call(bf16[528,128]{1,0:T(8,128)(2,1)S(1)} %pack_q.1.refs_0_, bf16[528,128]{1,0:T(8,128)(2,1)S(1)} %collective-permute-done.1.refs_1_, bf16[528,128]{1,0:T(8,128)(2,1)S(1)} %collective-permute-done.2.refs_2_, bf16[528,128]{1,0:T(8,128)(2,1)S(1)} %collective-permute-done.3.refs_3_, ...), custom_call_target="tpu_custom_call" | custom-call | flops 5100273664 | bytes 4194304 | tf_op jit(solution)/shard_map/reach1/pallas_call | solution.py:290
  55.9 2.1 %collective-permute-done.5.refs_6_ = bf16[1616,128]{1,0:T(8,128)(2,1)S(1)} collective-permute-done((bf16[1616,128]{1,0:T(8,128)(2,1)S(1)}, bf16[1616,128]{1,0:T(8,128)(2,1)S(1)}, u32[]{:S(2)}, u32[]{:S(2)}) %collective-permute-start.5) | collective-permute-done | bytes 413728 | tf_op jit(solution)/shard_map/ppermute | solution.py:342
  58.0 23.6 %collective-permute-start.7 = (bf16[1616,128]{1,0:T(8,128)(2,1)S(1)}, bf16[1616,128]{1,0:T(8,128)(2,1)S(1)}, u32[]{:S(2)}, u32[]{:S(2)}) collective-permute-start(bf16[1616,128]{1,0:T(8,128)(2,1)S(1)} %collective-permute-done.5.refs_6_), channel_id=1, source_target_pairs={{0,4},{4,8},{8,12},{12,16},{16,20},{20,24},{24,28},{28,0},{32,36},... | collective-permute-start | bytes 1241096 | tf_op jit(solution)/shard_map/ppermute | solution.py:342
  81.6 0.0 collective-permute-done.9.refs_7_
  81.7 34.7 %reach3.1 = (f32[2048,256]{1,0:T(8,128)S(1)}, f32[2048,128]{1,0:T(8,128)S(1)}) custom-call(bf16[528,128]{1,0:T(8,128)(2,1)S(1)} %pack_q.1.refs_0_, bf16[528,128]{1,0:T(8,128)(2,1)S(1)} %collective-permute-done.1.refs_1_, bf16[528,128]{1,0:T(8,128)(2,1)S(1)} %collective-permute-done.2.refs_2_, bf16[528,128]{1,0:T(8,128)(2,1)S(1)} %collective-permute-done.3.refs_3_, ...), custom_call_target="tpu_custom_call" | custom-call | flops 6710886400 | bytes 4194304 | tf_op jit(solution)/shard_map/reach3/pallas_call | solution.py:290
  116.4 0.0 collective-permute-done.7.refs_4_
  116.4 20.5 %reach4.1 = (bf16[528,128]{1,0:T(8,128)(2,1)S(1)}, bf16[528,128]{1,0:T(8,128)(2,1)S(1)}, bf16[528,128]{1,0:T(8,128)(2,1)S(1)}, bf16[528,128]{1,0:T(8,128)(2,1)S(1)}) custom-call(bf16[528,128]{1,0:T(8,128)(2,1)S(1)} %pack_q.1.refs_0_, bf16[528,128]{1,0:T(8,128)(2,1)S(1)} %collective-permute-done.1.refs_1_, ...), custom_call_target="tpu_custom_call" | custom-call | flops 1879048192 | bytes 4194304 | tf_op jit(solution)/shard_map/reach4/pallas_call | solution.py:290
  136.9 1.9 %collective-permute-start.10 = (bf16[528,128]{1,0:T(8,128)(2,1)S(1)}, bf16[528,128]{1,0:T(8,128)(2,1)S(1)}, u32[]{:S(2)}, u32[]{:S(2)}) collective-permute-start(bf16[528,128]{1,0:T(8,128)(2,1)S(1)} %get-tuple-element.38), channel_id=1, source_target_pairs={{0,64},{4,68},{8,72},{12,76},{16,80},{20,84},{24,88},{28,92},{32,9... | collective-permute-start | bytes 405512 | tf_op jit(solution)/shard_map/ppermute | solution.py:349
  138.8 1.9 %collective-permute-start.11 = (bf16[528,128]{1,0:T(8,128)(2,1)S(1)}, bf16[528,128]{1,0:T(8,128)(2,1)S(1)}, u32[]{:S(2)}, u32[]{:S(2)}) collective-permute-start(bf16[528,128]{1,0:T(8,128)(2,1)S(1)} %get-tuple-element.39), channel_id=1, source_target_pairs={{0,96},{4,100},{8,104},{12,108},{16,112},{20,116},{24,120},{28,124... | collective-permute-start | bytes 405512 | tf_op jit(solution)/shard_map/ppermute | solution.py:349
  140.8 4.8 %collective-permute-start.12 = (bf16[528,128]{1,0:T(8,128)(2,1)S(1)}, bf16[528,128]{1,0:T(8,128)(2,1)S(1)}, u32[]{:S(2)}, u32[]{:S(2)}) collective-permute-start(bf16[528,128]{1,0:T(8,128)(2,1)S(1)} %get-tuple-element.40), channel_id=1, source_target_pairs={{0,32},{4,36},{8,40},{12,44},{16,48},{20,52},{24,56},{28,60},{32,6... | collective-permute-start | bytes 405512 | tf_op jit(solution)/shard_map/ppermute | solution.py:349
  145.6 2.2 %collective-permute-done.10.refs_1_ = bf16[528,128]{1,0:T(8,128)(2,1)S(1)} collective-permute-done((bf16[528,128]{1,0:T(8,128)(2,1)S(1)}, bf16[528,128]{1,0:T(8,128)(2,1)S(1)}, u32[]{:S(2)}, u32[]{:S(2)}) %collective-permute-start.10) | collective-permute-done | bytes 135200 | tf_op jit(solution)/shard_map/ppermute | solution.py:349
  147.8 0.3 collective-permute-done.11.refs_2_
  148.1 4.0 %collective-permute-done.12.refs_3_ = bf16[528,128]{1,0:T(8,128)(2,1)S(1)} collective-permute-done((bf16[528,128]{1,0:T(8,128)(2,1)S(1)}, bf16[528,128]{1,0:T(8,128)(2,1)S(1)}, u32[]{:S(2)}, u32[]{:S(2)}) %collective-permute-start.12) | collective-permute-done | bytes 135200 | tf_op jit(solution)/shard_map/ppermute | solution.py:349
  152.1 1.1 combine.1
  (1 shorter events, 0.0 us)
Async XLA Ops:
  1.8 0.7 copy-start.1
  2.4 0.7 copy-start.2
  3.8 0.9 copy-start
  4.8 23.0 %collective-permute-start = (bf16[1616,128]{1,0:T(8,128)(2,1)S(1)}, bf16[1616,128]{1,0:T(8,128)(2,1)S(1)}, u32[]{:S(2)}, u32[]{:S(2)}) collective-permute-start(bf16[1616,128]{1,0:T(8,128)(2,1)S(1)} %pack_kv.1.kv_ref.refs_4_), channel_id=1, source_target_pairs={{0,4},{4,8},{8,12},{12,16},{16,20},{20,24},{24,28},{28,0},{32,36},... | collective-permute-start | bytes 1241096 | tf_op jit(solution)/shard_map/ppermute | solution.py:342
  7.3 20.4 %collective-permute-start.6 = (bf16[1616,128]{1,0:T(8,128)(2,1)S(1)}, bf16[1616,128]{1,0:T(8,128)(2,1)S(1)}, u32[]{:S(2)}, u32[]{:S(2)}) collective-permute-start(bf16[1616,128]{1,0:T(8,128)(2,1)S(1)} %pack_kv.1.kv_ref.refs_4_), channel_id=1, source_target_pairs={{0,28},{4,0},{8,4},{12,8},{16,12},{20,16},{24,20},{28,24},{32,60},... | collective-permute-start | bytes 1241096 | tf_op jit(solution)/shard_map/ppermute | solution.py:342
  11.8 15.9 %collective-permute-start.1 = (bf16[528,128]{1,0:T(8,128)(2,1)S(1)}, bf16[528,128]{1,0:T(8,128)(2,1)S(1)}, u32[]{:S(2)}, u32[]{:S(2)}) collective-permute-start(bf16[528,128]{1,0:T(8,128)(2,1)S(1)} %pack_q.1.refs_0_), channel_id=1, source_target_pairs={{0,32},{4,36},{8,40},{12,44},{16,48},{20,52},{24,56},{28,60},{32,6... | collective-permute-start | bytes 405512 | tf_op jit(solution)/shard_map/ppermute | solution.py:349
  27.8 13.6 %collective-permute-start.8 = (bf16[1616,128]{1,0:T(8,128)(2,1)S(1)}, bf16[1616,128]{1,0:T(8,128)(2,1)S(1)}, u32[]{:S(2)}, u32[]{:S(2)}) collective-permute-start(bf16[1616,128]{1,0:T(8,128)(2,1)S(1)} %collective-permute-done.6.refs_6_), channel_id=1, source_target_pairs={{0,28},{4,0},{8,4},{12,8},{16,12},{20,16},{24,20},{28,24},{32,60},... | collective-permute-start | bytes 1241096 | tf_op jit(solution)/shard_map/ppermute | solution.py:342
  30.0 15.0 %collective-permute-start.4 = (bf16[1616,128]{1,0:T(8,128)(2,1)S(1)}, bf16[1616,128]{1,0:T(8,128)(2,1)S(1)}, u32[]{:S(2)}, u32[]{:S(2)}) collective-permute-start(bf16[1616,128]{1,0:T(8,128)(2,1)S(1)} %collective-permute-done.refs_5_), channel_id=1, source_target_pairs={{0,4},{4,8},{8,12},{12,16},{16,20},{20,24},{24,28},{28,0},{32,36},... | collective-permute-start | bytes 1241096 | tf_op jit(solution)/shard_map/ppermute | solution.py:342
  33.6 13.6 %collective-permute-start.3 = (bf16[528,128]{1,0:T(8,128)(2,1)S(1)}, bf16[528,128]{1,0:T(8,128)(2,1)S(1)}, u32[]{:S(2)}, u32[]{:S(2)}) collective-permute-start(bf16[528,128]{1,0:T(8,128)(2,1)S(1)} %pack_q.1.refs_0_), channel_id=1, source_target_pairs={{0,64},{4,68},{8,72},{12,76},{16,80},{20,84},{24,88},{28,92},{32,9... | collective-permute-start | bytes 405512 | tf_op jit(solution)/shard_map/ppermute | solution.py:349
  39.4 9.7 %collective-permute-start.2 = (bf16[528,128]{1,0:T(8,128)(2,1)S(1)}, bf16[528,128]{1,0:T(8,128)(2,1)S(1)}, u32[]{:S(2)}, u32[]{:S(2)}) collective-permute-start(bf16[528,128]{1,0:T(8,128)(2,1)S(1)} %pack_q.1.refs_0_), channel_id=1, source_target_pairs={{0,96},{4,100},{8,104},{12,108},{16,112},{20,116},{24,120},{28,124... | collective-permute-start | bytes 405512 | tf_op jit(solution)/shard_map/ppermute | solution.py:349
  41.3 40.3 %collective-permute-start.9 = (bf16[1616,128]{1,0:T(8,128)(2,1)S(1)}, bf16[1616,128]{1,0:T(8,128)(2,1)S(1)}, u32[]{:S(2)}, u32[]{:S(2)}) collective-permute-start(bf16[1616,128]{1,0:T(8,128)(2,1)S(1)} %collective-permute-done.8.refs_5_), channel_id=1, source_target_pairs={{0,28},{4,0},{8,4},{12,8},{16,12},{20,16},{24,20},{28,24},{32,60},... | collective-permute-start | bytes 1241096 | tf_op jit(solution)/shard_map/ppermute | solution.py:342
  45.0 13.0 %collective-permute-start.5 = (bf16[1616,128]{1,0:T(8,128)(2,1)S(1)}, bf16[1616,128]{1,0:T(8,128)(2,1)S(1)}, u32[]{:S(2)}, u32[]{:S(2)}) collective-permute-start(bf16[1616,128]{1,0:T(8,128)(2,1)S(1)} %collective-permute-done.4.refs_4_), channel_id=1, source_target_pairs={{0,4},{4,8},{8,12},{12,16},{16,20},{20,24},{24,28},{28,0},{32,36},... | collective-permute-start | bytes 1241096 | tf_op jit(solution)/shard_map/ppermute | solution.py:342
  58.0 58.4 %collective-permute-start.7 = (bf16[1616,128]{1,0:T(8,128)(2,1)S(1)}, bf16[1616,128]{1,0:T(8,128)(2,1)S(1)}, u32[]{:S(2)}, u32[]{:S(2)}) collective-permute-start(bf16[1616,128]{1,0:T(8,128)(2,1)S(1)} %collective-permute-done.5.refs_6_), channel_id=1, source_target_pairs={{0,4},{4,8},{8,12},{12,16},{16,20},{20,24},{24,28},{28,0},{32,36},... | collective-permute-start | bytes 1241096 | tf_op jit(solution)/shard_map/ppermute | solution.py:342
  136.9 10.9 %collective-permute-start.10 = (bf16[528,128]{1,0:T(8,128)(2,1)S(1)}, bf16[528,128]{1,0:T(8,128)(2,1)S(1)}, u32[]{:S(2)}, u32[]{:S(2)}) collective-permute-start(bf16[528,128]{1,0:T(8,128)(2,1)S(1)} %get-tuple-element.38), channel_id=1, source_target_pairs={{0,64},{4,68},{8,72},{12,76},{16,80},{20,84},{24,88},{28,92},{32,9... | collective-permute-start | bytes 405512 | tf_op jit(solution)/shard_map/ppermute | solution.py:349
  138.8 9.3 %collective-permute-start.11 = (bf16[528,128]{1,0:T(8,128)(2,1)S(1)}, bf16[528,128]{1,0:T(8,128)(2,1)S(1)}, u32[]{:S(2)}, u32[]{:S(2)}) collective-permute-start(bf16[528,128]{1,0:T(8,128)(2,1)S(1)} %get-tuple-element.39), channel_id=1, source_target_pairs={{0,96},{4,100},{8,104},{12,108},{16,112},{20,116},{24,120},{28,124... | collective-permute-start | bytes 405512 | tf_op jit(solution)/shard_map/ppermute | solution.py:349
  140.8 11.4 %collective-permute-start.12 = (bf16[528,128]{1,0:T(8,128)(2,1)S(1)}, bf16[528,128]{1,0:T(8,128)(2,1)S(1)}, u32[]{:S(2)}, u32[]{:S(2)}) collective-permute-start(bf16[528,128]{1,0:T(8,128)(2,1)S(1)} %get-tuple-element.40), channel_id=1, source_target_pairs={{0,32},{4,36},{8,40},{12,44},{16,48},{20,52},{24,56},{28,60},{32,6... | collective-permute-start | bytes 405512 | tf_op jit(solution)/shard_map/ppermute | solution.py:349

commit v6 on v5

--- a/solution.py
+++ b/solution.py
@@ -352,11 +352,9 @@
 def body(queries, kv_cache, new_kv, cache_len, new_pos):
     own_kv = pack_kv(kv_cache, new_kv, cache_len, new_pos)
     own_q = pack_q(queries, own_kv)
-    own_kv, own_q = lax.optimization_barrier((own_kv, own_q))
     up1, down1 = shift_y(own_kv, 1), shift_y(own_kv, -1)
     offsets = (1, -1, 2)
     q1, q2, q3 = [shift_z(own_q, d) for d in offsets]
-    up1, q1 = lax.optimization_barrier((up1, q1))
     up2, down2 = shift_y(up1, 1), shift_y(down1, -1)
     up3, down3 = shift_y(up2, 1), shift_y(down2, -1)
     qs = [own_q, q1, q2, q3]

time: 154 us -> 151 us (0.981)
  the two profiles are of different devices: /device:TPU:102 before, /device:TPU:95 now
where the time goes in v6:
time: 151 us
  starting transfers between devices  88.5 us (59%)
  Pallas kernels  47 us (31%)
  waiting for transfers between devices  10.9 us (7%)
  local copies, waits for them, and re-layouts  3.97 us (3%)
    ppermute x6, starting transfers between devices, shift_z(): return lax.ppermute(x, 'seq', pairs)  65 us
    pallas_call x3, Pallas kernels, stage(): pl.pallas_call(functools.partial(stage_kernel, nq, g, spans, last), out_s...  45.1 us
    ppermute x7, starting transfers between devices, shift_y(): return lax.ppermute(x, 'seq', pairs)  23.5 us
    ppermute x7, waiting for transfers between devices, shift_y(): return lax.ppermute(x, 'seq', pairs)  7.03 us
    unnamed x8, local copies, waits for them, and re-layouts  3.97 us
    ppermute x6, waiting for transfers between devices, shift_z(): return lax.ppermute(x, 'seq', pairs)  3.87 us
  transfers between devices with their start and end apart: 13, of which 3 were waited for; matrix products, arithmetic and copies ran while one was open for 0% of the time, Pallas kernels for 28%

profile of v6, /device:TPU:95, one launch (start us, length us, event | category | flops | bytes accessed | tf_op | source)
XLA Modules:
  0.0 150.5 jit_solution(8907048396414464058)
XLA Ops:
  0.0 0.7 copy.11
  0.7 1.0 copy.10
  1.8 0.0 copy-start.1
  1.8 0.6 copy-done.1
  2.4 0.0 copy-start.2
  2.4 0.7 copy-done.2
  3.1 0.7 pack_kv.1.kv_ref.refs_4_
  3.8 2.1 %collective-permute-start.6 = (bf16[1616,128]{1,0:T(8,128)(2,1)S(1)}, bf16[1616,128]{1,0:T(8,128)(2,1)S(1)}, u32[]{:S(2)}, u32[]{:S(2)}) collective-permute-start(bf16[1616,128]{1,0:T(8,128)(2,1)S(1)} %pack_kv.1.kv_ref.refs_4_), channel_id=1, source_target_pairs={{0,28},{4,0},{8,4},{12,8},{16,12},{20,16},{24,20},{28,24},{32,60},... | collective-permute-start | bytes 1241096 | tf_op jit(solution)/shard_map/ppermute | solution.py:342
  5.9 4.4 %collective-permute-start.3 = (bf16[1616,128]{1,0:T(8,128)(2,1)S(1)}, bf16[1616,128]{1,0:T(8,128)(2,1)S(1)}, u32[]{:S(2)}, u32[]{:S(2)}) collective-permute-start(bf16[1616,128]{1,0:T(8,128)(2,1)S(1)} %pack_kv.1.kv_ref.refs_4_), channel_id=1, source_target_pairs={{0,4},{4,8},{8,12},{12,16},{16,20},{20,24},{24,28},{28,0},{32,36},... | collective-permute-start | bytes 1241096 | tf_op jit(solution)/shard_map/ppermute | solution.py:342
  10.3 7.0 %collective-permute-done.6.refs_6_ = bf16[1616,128]{1,0:T(8,128)(2,1)S(1)} collective-permute-done((bf16[1616,128]{1,0:T(8,128)(2,1)S(1)}, bf16[1616,128]{1,0:T(8,128)(2,1)S(1)}, u32[]{:S(2)}, u32[]{:S(2)}) %collective-permute-start.6) | collective-permute-done | bytes 413728 | tf_op jit(solution)/shard_map/ppermute | solution.py:342
  17.3 1.9 %collective-permute-start.8 = (bf16[1616,128]{1,0:T(8,128)(2,1)S(1)}, bf16[1616,128]{1,0:T(8,128)(2,1)S(1)}, u32[]{:S(2)}, u32[]{:S(2)}) collective-permute-start(bf16[1616,128]{1,0:T(8,128)(2,1)S(1)} %collective-permute-done.6.refs_6_), channel_id=1, source_target_pairs={{0,28},{4,0},{8,4},{12,8},{16,12},{20,16},{24,20},{28,24},{32,60},... | collective-permute-start | bytes 1241096 | tf_op jit(solution)/shard_map/ppermute | solution.py:342
  19.3 0.0 collective-permute-done.3.refs_5_
  19.3 4.6 %collective-permute-start.4 = (bf16[1616,128]{1,0:T(8,128)(2,1)S(1)}, bf16[1616,128]{1,0:T(8,128)(2,1)S(1)}, u32[]{:S(2)}, u32[]{:S(2)}) collective-permute-start(bf16[1616,128]{1,0:T(8,128)(2,1)S(1)} %collective-permute-done.3.refs_5_), channel_id=1, source_target_pairs={{0,4},{4,8},{8,12},{12,16},{16,20},{20,24},{24,28},{28,0},{32,36},... | collective-permute-start | bytes 1241096 | tf_op jit(solution)/shard_map/ppermute | solution.py:342
  23.8 0.0 copy-start
  23.9 0.9 copy-done
  24.8 9.7 %collective-permute-start.2 = (bf16[528,128]{1,0:T(8,128)(2,1)S(1)}, bf16[528,128]{1,0:T(8,128)(2,1)S(1)}, u32[]{:S(2)}, u32[]{:S(2)}) collective-permute-start(bf16[528,128]{1,0:T(8,128)(2,1)S(1)} %pack_q.1.refs_0_), channel_id=1, source_target_pairs={{0,64},{4,68},{8,72},{12,76},{16,80},{20,84},{24,88},{28,92},{32,9... | collective-permute-start | bytes 405512 | tf_op jit(solution)/shard_map/ppermute | solution.py:349
  34.5 1.9 %collective-permute-start.1 = (bf16[528,128]{1,0:T(8,128)(2,1)S(1)}, bf16[528,128]{1,0:T(8,128)(2,1)S(1)}, u32[]{:S(2)}, u32[]{:S(2)}) collective-permute-start(bf16[528,128]{1,0:T(8,128)(2,1)S(1)} %pack_q.1.refs_0_), channel_id=1, source_target_pairs={{0,96},{4,100},{8,104},{12,108},{16,112},{20,116},{24,120},{28,124... | collective-permute-start | bytes 405512 | tf_op jit(solution)/shard_map/ppermute | solution.py:349
  36.5 4.2 %collective-permute-start = (bf16[528,128]{1,0:T(8,128)(2,1)S(1)}, bf16[528,128]{1,0:T(8,128)(2,1)S(1)}, u32[]{:S(2)}, u32[]{:S(2)}) collective-permute-start(bf16[528,128]{1,0:T(8,128)(2,1)S(1)} %pack_q.1.refs_0_), channel_id=1, source_target_pairs={{0,32},{4,36},{8,40},{12,44},{16,48},{20,52},{24,56},{28,60},{32,6... | collective-permute-start | bytes 405512 | tf_op jit(solution)/shard_map/ppermute | solution.py:349
  40.7 0.0 collective-permute-done.8.refs_5_
  40.7 1.9 %collective-permute-start.9 = (bf16[1616,128]{1,0:T(8,128)(2,1)S(1)}, bf16[1616,128]{1,0:T(8,128)(2,1)S(1)}, u32[]{:S(2)}, u32[]{:S(2)}) collective-permute-start(bf16[1616,128]{1,0:T(8,128)(2,1)S(1)} %collective-permute-done.8.refs_5_), channel_id=1, source_target_pairs={{0,28},{4,0},{8,4},{12,8},{16,12},{20,16},{24,20},{28,24},{32,60},... | collective-permute-start | bytes 1241096 | tf_op jit(solution)/shard_map/ppermute | solution.py:342
  42.7 0.0 collective-permute-done.4.refs_4_
  42.7 4.6 %collective-permute-start.5 = (bf16[1616,128]{1,0:T(8,128)(2,1)S(1)}, bf16[1616,128]{1,0:T(8,128)(2,1)S(1)}, u32[]{:S(2)}, u32[]{:S(2)}) collective-permute-start(bf16[1616,128]{1,0:T(8,128)(2,1)S(1)} %collective-permute-done.4.refs_4_), channel_id=1, source_target_pairs={{0,4},{4,8},{8,12},{12,16},{16,20},{20,24},{24,28},{28,0},{32,36},... | collective-permute-start | bytes 1241096 | tf_op jit(solution)/shard_map/ppermute | solution.py:342
  47.3 0.0 collective-permute-done.2.refs_3_
  47.3 0.0 collective-permute-done.1.refs_2_
  47.3 0.0 collective-permute-done.refs_1_
  47.3 6.9 %reach1.1 = (f32[2048,256]{1,0:T(8,128)S(1)}, f32[2048,128]{1,0:T(8,128)S(1)}) custom-call(bf16[528,128]{1,0:T(8,128)(2,1)S(1)} %pack_q.1.refs_0_, bf16[528,128]{1,0:T(8,128)(2,1)S(1)} %collective-permute-done.refs_1_, bf16[528,128]{1,0:T(8,128)(2,1)S(1)} %collective-permute-done.1.refs_2_, bf16[528,128]{1,0:T(8,128)(2,1)S(1)} %collective-permute-done.2.refs_3_, ...), custom_call_target="tpu_custom_call" | custom-call | flops 5100273664 | bytes 4194304 | tf_op jit(solution)/shard_map/reach1/pallas_call | solution.py:290
  54.2 0.0 collective-permute-done.5.refs_6_
  54.2 4.0 %collective-permute-start.7 = (bf16[1616,128]{1,0:T(8,128)(2,1)S(1)}, bf16[1616,128]{1,0:T(8,128)(2,1)S(1)}, u32[]{:S(2)}, u32[]{:S(2)}) collective-permute-start(bf16[1616,128]{1,0:T(8,128)(2,1)S(1)} %collective-permute-done.5.refs_6_), channel_id=1, source_target_pairs={{0,4},{4,8},{8,12},{12,16},{16,20},{20,24},{24,28},{28,0},{32,36},... | collective-permute-start | bytes 1241096 | tf_op jit(solution)/shard_map/ppermute | solution.py:342
  58.2 0.0 collective-permute-done.9.refs_7_
  58.2 34.7 %reach3.1 = (f32[2048,256]{1,0:T(8,128)S(1)}, f32[2048,128]{1,0:T(8,128)S(1)}) custom-call(bf16[528,128]{1,0:T(8,128)(2,1)S(1)} %pack_q.1.refs_0_, bf16[528,128]{1,0:T(8,128)(2,1)S(1)} %collective-permute-done.refs_1_, bf16[528,128]{1,0:T(8,128)(2,1)S(1)} %collective-permute-done.1.refs_2_, bf16[528,128]{1,0:T(8,128)(2,1)S(1)} %collective-permute-done.2.refs_3_, ...), custom_call_target="tpu_custom_call" | custom-call | flops 6710886400 | bytes 4194304 | tf_op jit(solution)/shard_map/reach3/pallas_call | solution.py:290
  92.9 0.0 collective-permute-done.7.refs_4_
  92.9 3.6 %reach4.1 = (bf16[528,128]{1,0:T(8,128)(2,1)S(1)}, bf16[528,128]{1,0:T(8,128)(2,1)S(1)}, bf16[528,128]{1,0:T(8,128)(2,1)S(1)}, bf16[528,128]{1,0:T(8,128)(2,1)S(1)}) custom-call(bf16[528,128]{1,0:T(8,128)(2,1)S(1)} %pack_q.1.refs_0_, bf16[528,128]{1,0:T(8,128)(2,1)S(1)} %collective-permute-done.refs_1_, bf16[528,128]{1,0:T(8,128)(2,1)S(1)} %collective-permute-done.1.refs_2_, ...), custom_call_target="tpu_custom_call" | custom-call | flops 1879048192 | bytes 4194304 | tf_op jit(solution)/shard_map/reach4/pallas_call | solution.py:290
  96.5 1.9 %collective-permute-start.10 = (bf16[528,128]{1,0:T(8,128)(2,1)S(1)}, bf16[528,128]{1,0:T(8,128)(2,1)S(1)}, u32[]{:S(2)}, u32[]{:S(2)}) collective-permute-start(bf16[528,128]{1,0:T(8,128)(2,1)S(1)} %get-tuple-element.30), channel_id=1, source_target_pairs={{0,64},{4,68},{8,72},{12,76},{16,80},{20,84},{24,88},{28,92},{32,9... | collective-permute-start | bytes 405512 | tf_op jit(solution)/shard_map/ppermute | solution.py:349
  98.4 43.2 %collective-permute-start.11 = (bf16[528,128]{1,0:T(8,128)(2,1)S(1)}, bf16[528,128]{1,0:T(8,128)(2,1)S(1)}, u32[]{:S(2)}, u32[]{:S(2)}) collective-permute-start(bf16[528,128]{1,0:T(8,128)(2,1)S(1)} %get-tuple-element.31), channel_id=1, source_target_pairs={{0,96},{4,100},{8,104},{12,108},{16,112},{20,116},{24,120},{28,124... | collective-permute-start | bytes 405512 | tf_op jit(solution)/shard_map/ppermute | solution.py:349
  141.6 4.0 %collective-permute-start.12 = (bf16[528,128]{1,0:T(8,128)(2,1)S(1)}, bf16[528,128]{1,0:T(8,128)(2,1)S(1)}, u32[]{:S(2)}, u32[]{:S(2)}) collective-permute-start(bf16[528,128]{1,0:T(8,128)(2,1)S(1)} %get-tuple-element.32), channel_id=1, source_target_pairs={{0,32},{4,36},{8,40},{12,44},{16,48},{20,52},{24,56},{28,60},{32,6... | collective-permute-start | bytes 405512 | tf_op jit(solution)/shard_map/ppermute | solution.py:349
  145.6 0.0 collective-permute-done.10.refs_1_
  145.6 0.4 collective-permute-done.11.refs_2_
  146.0 3.4 %collective-permute-done.12.refs_3_ = bf16[528,128]{1,0:T(8,128)(2,1)S(1)} collective-permute-done((bf16[528,128]{1,0:T(8,128)(2,1)S(1)}, bf16[528,128]{1,0:T(8,128)(2,1)S(1)}, u32[]{:S(2)}, u32[]{:S(2)}) %collective-permute-start.12) | collective-permute-done | bytes 135200 | tf_op jit(solution)/shard_map/ppermute | solution.py:349
  149.5 1.1 combine.1
  (1 shorter events, 0.0 us)
Async XLA Ops:
  1.8 0.7 copy-start.1
  2.4 0.7 copy-start.2
  3.8 13.5 %collective-permute-start.6 = (bf16[1616,128]{1,0:T(8,128)(2,1)S(1)}, bf16[1616,128]{1,0:T(8,128)(2,1)S(1)}, u32[]{:S(2)}, u32[]{:S(2)}) collective-permute-start(bf16[1616,128]{1,0:T(8,128)(2,1)S(1)} %pack_kv.1.kv_ref.refs_4_), channel_id=1, source_target_pairs={{0,28},{4,0},{8,4},{12,8},{16,12},{20,16},{24,20},{28,24},{32,60},... | collective-permute-start | bytes 1241096 | tf_op jit(solution)/shard_map/ppermute | solution.py:342
  5.9 13.4 %collective-permute-start.3 = (bf16[1616,128]{1,0:T(8,128)(2,1)S(1)}, bf16[1616,128]{1,0:T(8,128)(2,1)S(1)}, u32[]{:S(2)}, u32[]{:S(2)}) collective-permute-start(bf16[1616,128]{1,0:T(8,128)(2,1)S(1)} %pack_kv.1.kv_ref.refs_4_), channel_id=1, source_target_pairs={{0,4},{4,8},{8,12},{12,16},{16,20},{20,24},{24,28},{28,0},{32,36},... | collective-permute-start | bytes 1241096 | tf_op jit(solution)/shard_map/ppermute | solution.py:342
  17.3 23.4 %collective-permute-start.8 = (bf16[1616,128]{1,0:T(8,128)(2,1)S(1)}, bf16[1616,128]{1,0:T(8,128)(2,1)S(1)}, u32[]{:S(2)}, u32[]{:S(2)}) collective-permute-start(bf16[1616,128]{1,0:T(8,128)(2,1)S(1)} %collective-permute-done.6.refs_6_), channel_id=1, source_target_pairs={{0,28},{4,0},{8,4},{12,8},{16,12},{20,16},{24,20},{28,24},{32,60},... | collective-permute-start | bytes 1241096 | tf_op jit(solution)/shard_map/ppermute | solution.py:342
  19.3 23.4 %collective-permute-start.4 = (bf16[1616,128]{1,0:T(8,128)(2,1)S(1)}, bf16[1616,128]{1,0:T(8,128)(2,1)S(1)}, u32[]{:S(2)}, u32[]{:S(2)}) collective-permute-start(bf16[1616,128]{1,0:T(8,128)(2,1)S(1)} %collective-permute-done.3.refs_5_), channel_id=1, source_target_pairs={{0,4},{4,8},{8,12},{12,16},{16,20},{20,24},{24,28},{28,0},{32,36},... | collective-permute-start | bytes 1241096 | tf_op jit(solution)/shard_map/ppermute | solution.py:342
  23.8 0.9 copy-start
  24.8 22.5 %collective-permute-start.2 = (bf16[528,128]{1,0:T(8,128)(2,1)S(1)}, bf16[528,128]{1,0:T(8,128)(2,1)S(1)}, u32[]{:S(2)}, u32[]{:S(2)}) collective-permute-start(bf16[528,128]{1,0:T(8,128)(2,1)S(1)} %pack_q.1.refs_0_), channel_id=1, source_target_pairs={{0,64},{4,68},{8,72},{12,76},{16,80},{20,84},{24,88},{28,92},{32,9... | collective-permute-start | bytes 405512 | tf_op jit(solution)/shard_map/ppermute | solution.py:349
  34.5 12.7 %collective-permute-start.1 = (bf16[528,128]{1,0:T(8,128)(2,1)S(1)}, bf16[528,128]{1,0:T(8,128)(2,1)S(1)}, u32[]{:S(2)}, u32[]{:S(2)}) collective-permute-start(bf16[528,128]{1,0:T(8,128)(2,1)S(1)} %pack_q.1.refs_0_), channel_id=1, source_target_pairs={{0,96},{4,100},{8,104},{12,108},{16,112},{20,116},{24,120},{28,124... | collective-permute-start | bytes 405512 | tf_op jit(solution)/shard_map/ppermute | solution.py:349
  36.5 10.8 %collective-permute-start = (bf16[528,128]{1,0:T(8,128)(2,1)S(1)}, bf16[528,128]{1,0:T(8,128)(2,1)S(1)}, u32[]{:S(2)}, u32[]{:S(2)}) collective-permute-start(bf16[528,128]{1,0:T(8,128)(2,1)S(1)} %pack_q.1.refs_0_), channel_id=1, source_target_pairs={{0,32},{4,36},{8,40},{12,44},{16,48},{20,52},{24,56},{28,60},{32,6... | collective-permute-start | bytes 405512 | tf_op jit(solution)/shard_map/ppermute | solution.py:349
  40.7 17.4 %collective-permute-start.9 = (bf16[1616,128]{1,0:T(8,128)(2,1)S(1)}, bf16[1616,128]{1,0:T(8,128)(2,1)S(1)}, u32[]{:S(2)}, u32[]{:S(2)}) collective-permute-start(bf16[1616,128]{1,0:T(8,128)(2,1)S(1)} %collective-permute-done.8.refs_5_), channel_id=1, source_target_pairs={{0,28},{4,0},{8,4},{12,8},{16,12},{20,16},{24,20},{28,24},{32,60},... | collective-permute-start | bytes 1241096 | tf_op jit(solution)/shard_map/ppermute | solution.py:342
  42.7 11.5 %collective-permute-start.5 = (bf16[1616,128]{1,0:T(8,128)(2,1)S(1)}, bf16[1616,128]{1,0:T(8,128)(2,1)S(1)}, u32[]{:S(2)}, u32[]{:S(2)}) collective-permute-start(bf16[1616,128]{1,0:T(8,128)(2,1)S(1)} %collective-permute-done.4.refs_4_), channel_id=1, source_target_pairs={{0,4},{4,8},{8,12},{12,16},{16,20},{20,24},{24,28},{28,0},{32,36},... | collective-permute-start | bytes 1241096 | tf_op jit(solution)/shard_map/ppermute | solution.py:342
  54.2 38.7 %collective-permute-start.7 = (bf16[1616,128]{1,0:T(8,128)(2,1)S(1)}, bf16[1616,128]{1,0:T(8,128)(2,1)S(1)}, u32[]{:S(2)}, u32[]{:S(2)}) collective-permute-start(bf16[1616,128]{1,0:T(8,128)(2,1)S(1)} %collective-permute-done.5.refs_6_), channel_id=1, source_target_pairs={{0,4},{4,8},{8,12},{12,16},{16,20},{20,24},{24,28},{28,0},{32,36},... | collective-permute-start | bytes 1241096 | tf_op jit(solution)/shard_map/ppermute | solution.py:342
  96.5 49.1 %collective-permute-start.10 = (bf16[528,128]{1,0:T(8,128)(2,1)S(1)}, bf16[528,128]{1,0:T(8,128)(2,1)S(1)}, u32[]{:S(2)}, u32[]{:S(2)}) collective-permute-start(bf16[528,128]{1,0:T(8,128)(2,1)S(1)} %get-tuple-element.30), channel_id=1, source_target_pairs={{0,64},{4,68},{8,72},{12,76},{16,80},{20,84},{24,88},{28,92},{32,9... | collective-permute-start | bytes 405512 | tf_op jit(solution)/shard_map/ppermute | solution.py:349
  98.4 47.6 %collective-permute-start.11 = (bf16[528,128]{1,0:T(8,128)(2,1)S(1)}, bf16[528,128]{1,0:T(8,128)(2,1)S(1)}, u32[]{:S(2)}, u32[]{:S(2)}) collective-permute-start(bf16[528,128]{1,0:T(8,128)(2,1)S(1)} %get-tuple-element.31), channel_id=1, source_target_pairs={{0,96},{4,100},{8,104},{12,108},{16,112},{20,116},{24,120},{28,124... | collective-permute-start | bytes 405512 | tf_op jit(solution)/shard_map/ppermute | solution.py:349
  141.6 7.9 %collective-permute-start.12 = (bf16[528,128]{1,0:T(8,128)(2,1)S(1)}, bf16[528,128]{1,0:T(8,128)(2,1)S(1)}, u32[]{:S(2)}, u32[]{:S(2)}) collective-permute-start(bf16[528,128]{1,0:T(8,128)(2,1)S(1)} %get-tuple-element.32), channel_id=1, source_target_pairs={{0,32},{4,36},{8,40},{12,44},{16,48},{20,52},{24,56},{28,60},{32,6... | collective-permute-start | bytes 405512 | tf_op jit(solution)/shard_map/ppermute | solution.py:349

commit v7 on v6

--- a/solution.py
+++ b/solution.py
@@ -28,7 +28,7 @@
 HIDDEN = -1e30
 CHUNK = 512
 PIECE = 64
-UNROLL = 2
+UNROLL = 4
 CEILING = 2.0**60
 
 F32 = jnp.float32
@@ -353,6 +353,7 @@
     own_kv = pack_kv(kv_cache, new_kv, cache_len, new_pos)
     own_q = pack_q(queries, own_kv)
     up1, down1 = shift_y(own_kv, 1), shift_y(own_kv, -1)
+    down1, own_q = lax.optimization_barrier((down1, own_q))
     offsets = (1, -1, 2)
     q1, q2, q3 = [shift_z(own_q, d) for d in offsets]
     up2, down2 = shift_y(up1, 1), shift_y(down1, -1)

time: 151 us -> 148 us (0.980)
  the two profiles are of different devices: /device:TPU:95 before, /device:TPU:35 now
where the time goes in v7:
time: 148 us
  starting transfers between devices  65.4 us (44%)
  Pallas kernels  62.4 us (42%)
  waiting for transfers between devices  15.6 us (11%)
  local copies, waits for them, and re-layouts  3.97 us (3%)
    pallas_call x3, Pallas kernels, stage(): pl.pallas_call(functools.partial(stage_kernel, nq, g, spans, last), out_s...  60.6 us
    ppermute x7, starting transfers between devices, shift_y(): return lax.ppermute(x, 'seq', pairs)  40.5 us
    ppermute x6, starting transfers between devices, shift_z(): return lax.ppermute(x, 'seq', pairs)  24.9 us
    ppermute x7, waiting for transfers between devices, shift_y(): return lax.ppermute(x, 'seq', pairs)  9.07 us
    ppermute x6, waiting for transfers between devices, shift_z(): return lax.ppermute(x, 'seq', pairs)  6.57 us
    unnamed x8, local copies, waits for them, and re-layouts  3.97 us
  transfers between devices with their start and end apart: 13, of which 5 were waited for; matrix products, arithmetic and copies ran while one was open for 0% of the time, Pallas kernels for 27%

profile of v7, /device:TPU:35, one launch (start us, length us, event | category | flops | bytes accessed | tf_op | source)
XLA Modules:
  0.0 147.6 jit_solution(728479211593811794)
XLA Ops:
  0.0 0.7 copy.11
  0.7 1.0 copy.10
  1.8 0.0 copy-start.1
  1.8 0.6 copy-done.1
  2.4 0.0 copy-start.2
  2.4 0.7 copy-done.2
  3.1 0.7 pack_kv.1.kv_ref.refs_4_
  3.8 2.1 %collective-permute-start = (bf16[1616,128]{1,0:T(8,128)(2,1)S(1)}, bf16[1616,128]{1,0:T(8,128)(2,1)S(1)}, u32[]{:S(2)}, u32[]{:S(2)}) collective-permute-start(bf16[1616,128]{1,0:T(8,128)(2,1)S(1)} %pack_kv.1.kv_ref.refs_4_), channel_id=1, source_target_pairs={{0,28},{4,0},{8,4},{12,8},{16,12},{20,16},{24,20},{28,24},{32,60},... | collective-permute-start | bytes 1241096 | tf_op jit(solution)/shard_map/ppermute | solution.py:342
  5.9 3.2 %collective-permute-start.4 = (bf16[1616,128]{1,0:T(8,128)(2,1)S(1)}, bf16[1616,128]{1,0:T(8,128)(2,1)S(1)}, u32[]{:S(2)}, u32[]{:S(2)}) collective-permute-start(bf16[1616,128]{1,0:T(8,128)(2,1)S(1)} %pack_kv.1.kv_ref.refs_4_), channel_id=1, source_target_pairs={{0,4},{4,8},{8,12},{12,16},{16,20},{20,24},{24,28},{28,0},{32,36},... | collective-permute-start | bytes 1241096 | tf_op jit(solution)/shard_map/ppermute | solution.py:342
  9.1 0.0 copy-start
  9.1 0.9 copy-done
  10.0 6.1 %collective-permute-done.refs_6_ = bf16[1616,128]{1,0:T(8,128)(2,1)S(1)} collective-permute-done((bf16[1616,128]{1,0:T(8,128)(2,1)S(1)}, bf16[1616,128]{1,0:T(8,128)(2,1)S(1)}, u32[]{:S(2)}, u32[]{:S(2)}) %collective-permute-start) | collective-permute-done | bytes 413728 | tf_op jit(solution)/shard_map/ppermute | solution.py:342
  16.1 3.0 %collective-permute-done.4.refs_5_ = bf16[1616,128]{1,0:T(8,128)(2,1)S(1)} collective-permute-done((bf16[1616,128]{1,0:T(8,128)(2,1)S(1)}, bf16[1616,128]{1,0:T(8,128)(2,1)S(1)}, u32[]{:S(2)}, u32[]{:S(2)}) %collective-permute-start.4) | collective-permute-done | bytes 413728 | tf_op jit(solution)/shard_map/ppermute | solution.py:342
  19.1 2.0 %collective-permute-start.5 = (bf16[1616,128]{1,0:T(8,128)(2,1)S(1)}, bf16[1616,128]{1,0:T(8,128)(2,1)S(1)}, u32[]{:S(2)}, u32[]{:S(2)}) collective-permute-start(bf16[1616,128]{1,0:T(8,128)(2,1)S(1)} %collective-permute-done.4.refs_5_), channel_id=1, source_target_pairs={{0,4},{4,8},{8,12},{12,16},{16,20},{20,24},{24,28},{28,0},{32,36},... | collective-permute-start | bytes 1241096 | tf_op jit(solution)/shard_map/ppermute | solution.py:342
  21.1 4.5 %collective-permute-start.8 = (bf16[1616,128]{1,0:T(8,128)(2,1)S(1)}, bf16[1616,128]{1,0:T(8,128)(2,1)S(1)}, u32[]{:S(2)}, u32[]{:S(2)}) collective-permute-start(bf16[1616,128]{1,0:T(8,128)(2,1)S(1)} %collective-permute-done.refs_6_), channel_id=1, source_target_pairs={{0,28},{4,0},{8,4},{12,8},{16,12},{20,16},{24,20},{28,24},{32,60},... | collective-permute-start | bytes 1241096 | tf_op jit(solution)/shard_map/ppermute | solution.py:342
  25.6 10.6 %collective-permute-start.3 = (bf16[528,128]{1,0:T(8,128)(2,1)S(1)}, bf16[528,128]{1,0:T(8,128)(2,1)S(1)}, u32[]{:S(2)}, u32[]{:S(2)}) collective-permute-start(bf16[528,128]{1,0:T(8,128)(2,1)S(1)} %pack_q.1.refs_0_), channel_id=1, source_target_pairs={{0,64},{4,68},{8,72},{12,76},{16,80},{20,84},{24,88},{28,92},{32,9... | collective-permute-start | bytes 405512 | tf_op jit(solution)/shard_map/ppermute | solution.py:349
  36.3 1.9 %collective-permute-start.2 = (bf16[528,128]{1,0:T(8,128)(2,1)S(1)}, bf16[528,128]{1,0:T(8,128)(2,1)S(1)}, u32[]{:S(2)}, u32[]{:S(2)}) collective-permute-start(bf16[528,128]{1,0:T(8,128)(2,1)S(1)} %pack_q.1.refs_0_), channel_id=1, source_target_pairs={{0,96},{4,100},{8,104},{12,108},{16,112},{20,116},{24,120},{28,124... | collective-permute-start | bytes 405512 | tf_op jit(solution)/shard_map/ppermute | solution.py:349
  38.2 4.2 %collective-permute-start.1 = (bf16[528,128]{1,0:T(8,128)(2,1)S(1)}, bf16[528,128]{1,0:T(8,128)(2,1)S(1)}, u32[]{:S(2)}, u32[]{:S(2)}) collective-permute-start(bf16[528,128]{1,0:T(8,128)(2,1)S(1)} %pack_q.1.refs_0_), channel_id=1, source_target_pairs={{0,32},{4,36},{8,40},{12,44},{16,48},{20,52},{24,56},{28,60},{32,6... | collective-permute-start | bytes 405512 | tf_op jit(solution)/shard_map/ppermute | solution.py:349
  42.4 0.0 collective-permute-done.5.refs_4_
  42.5 1.9 %collective-permute-start.6 = (bf16[1616,128]{1,0:T(8,128)(2,1)S(1)}, bf16[1616,128]{1,0:T(8,128)(2,1)S(1)}, u32[]{:S(2)}, u32[]{:S(2)}) collective-permute-start(bf16[1616,128]{1,0:T(8,128)(2,1)S(1)} %collective-permute-done.5.refs_4_), channel_id=1, source_target_pairs={{0,4},{4,8},{8,12},{12,16},{16,20},{20,24},{24,28},{28,0},{32,36},... | collective-permute-start | bytes 1241096 | tf_op jit(solution)/shard_map/ppermute | solution.py:342
  44.4 0.0 collective-permute-done.8.refs_5_
  44.4 4.6 %collective-permute-start.9 = (bf16[1616,128]{1,0:T(8,128)(2,1)S(1)}, bf16[1616,128]{1,0:T(8,128)(2,1)S(1)}, u32[]{:S(2)}, u32[]{:S(2)}) collective-permute-start(bf16[1616,128]{1,0:T(8,128)(2,1)S(1)} %collective-permute-done.8.refs_5_), channel_id=1, source_target_pairs={{0,28},{4,0},{8,4},{12,8},{16,12},{20,16},{24,20},{28,24},{32,60},... | collective-permute-start | bytes 1241096 | tf_op jit(solution)/shard_map/ppermute | solution.py:342
  49.0 0.0 collective-permute-done.3.refs_3_
  49.0 0.9 collective-permute-done.2.refs_2_
  49.9 0.0 collective-permute-done.1.refs_1_
  49.9 6.4 %reach1.1 = (f32[2048,256]{1,0:T(8,128)S(1)}, f32[2048,128]{1,0:T(8,128)S(1)}) custom-call(bf16[528,128]{1,0:T(8,128)(2,1)S(1)} %pack_q.1.refs_0_, bf16[528,128]{1,0:T(8,128)(2,1)S(1)} %collective-permute-done.1.refs_1_, bf16[528,128]{1,0:T(8,128)(2,1)S(1)} %collective-permute-done.2.refs_2_, bf16[528,128]{1,0:T(8,128)(2,1)S(1)} %collective-permute-done.3.refs_3_, ...), custom_call_target="tpu_custom_call" | custom-call | flops 5100273664 | bytes 4194304 | tf_op jit(solution)/shard_map/reach1/pallas_call | solution.py:290
  56.3 0.0 collective-permute-done.6.refs_6_
  56.3 22.3 %collective-permute-start.7 = (bf16[1616,128]{1,0:T(8,128)(2,1)S(1)}, bf16[1616,128]{1,0:T(8,128)(2,1)S(1)}, u32[]{:S(2)}, u32[]{:S(2)}) collective-permute-start(bf16[1616,128]{1,0:T(8,128)(2,1)S(1)} %collective-permute-done.6.refs_6_), channel_id=1, source_target_pairs={{0,4},{4,8},{8,12},{12,16},{16,20},{20,24},{24,28},{28,0},{32,36},... | collective-permute-start | bytes 1241096 | tf_op jit(solution)/shard_map/ppermute | solution.py:342
  78.6 0.0 collective-permute-done.9.refs_7_
  78.6 34.1 %reach3.1 = (f32[2048,256]{1,0:T(8,128)S(1)}, f32[2048,128]{1,0:T(8,128)S(1)}) custom-call(bf16[528,128]{1,0:T(8,128)(2,1)S(1)} %pack_q.1.refs_0_, bf16[528,128]{1,0:T(8,128)(2,1)S(1)} %collective-permute-done.1.refs_1_, bf16[528,128]{1,0:T(8,128)(2,1)S(1)} %collective-permute-done.2.refs_2_, bf16[528,128]{1,0:T(8,128)(2,1)S(1)} %collective-permute-done.3.refs_3_, ...), custom_call_target="tpu_custom_call" | custom-call | flops 6710886400 | bytes 4194304 | tf_op jit(solution)/shard_map/reach3/pallas_call | solution.py:290
  112.7 0.0 collective-permute-done.7.refs_4_
  112.7 20.1 %reach4.1 = (bf16[528,128]{1,0:T(8,128)(2,1)S(1)}, bf16[528,128]{1,0:T(8,128)(2,1)S(1)}, bf16[528,128]{1,0:T(8,128)(2,1)S(1)}, bf16[528,128]{1,0:T(8,128)(2,1)S(1)}) custom-call(bf16[528,128]{1,0:T(8,128)(2,1)S(1)} %pack_q.1.refs_0_, bf16[528,128]{1,0:T(8,128)(2,1)S(1)} %collective-permute-done.1.refs_1_, ...), custom_call_target="tpu_custom_call" | custom-call | flops 1879048192 | bytes 4194304 | tf_op jit(solution)/shard_map/reach4/pallas_call | solution.py:290
  132.8 1.9 %collective-permute-start.10 = (bf16[528,128]{1,0:T(8,128)(2,1)S(1)}, bf16[528,128]{1,0:T(8,128)(2,1)S(1)}, u32[]{:S(2)}, u32[]{:S(2)}) collective-permute-start(bf16[528,128]{1,0:T(8,128)(2,1)S(1)} %get-tuple-element.34), channel_id=1, source_target_pairs={{0,64},{4,68},{8,72},{12,76},{16,80},{20,84},{24,88},{28,92},{32,9... | collective-permute-start | bytes 405512 | tf_op jit(solution)/shard_map/ppermute | solution.py:349
  134.7 1.9 %collective-permute-start.11 = (bf16[528,128]{1,0:T(8,128)(2,1)S(1)}, bf16[528,128]{1,0:T(8,128)(2,1)S(1)}, u32[]{:S(2)}, u32[]{:S(2)}) collective-permute-start(bf16[528,128]{1,0:T(8,128)(2,1)S(1)} %get-tuple-element.35), channel_id=1, source_target_pairs={{0,96},{4,100},{8,104},{12,108},{16,112},{20,116},{24,120},{28,124... | collective-permute-start | bytes 405512 | tf_op jit(solution)/shard_map/ppermute | solution.py:349
  136.7 4.3 %collective-permute-start.12 = (bf16[528,128]{1,0:T(8,128)(2,1)S(1)}, bf16[528,128]{1,0:T(8,128)(2,1)S(1)}, u32[]{:S(2)}, u32[]{:S(2)}) collective-permute-start(bf16[528,128]{1,0:T(8,128)(2,1)S(1)} %get-tuple-element.36), channel_id=1, source_target_pairs={{0,32},{4,36},{8,40},{12,44},{16,48},{20,52},{24,56},{28,60},{32,6... | collective-permute-start | bytes 405512 | tf_op jit(solution)/shard_map/ppermute | solution.py:349
  140.9 1.5 %collective-permute-done.10.refs_1_ = bf16[528,128]{1,0:T(8,128)(2,1)S(1)} collective-permute-done((bf16[528,128]{1,0:T(8,128)(2,1)S(1)}, bf16[528,128]{1,0:T(8,128)(2,1)S(1)}, u32[]{:S(2)}, u32[]{:S(2)}) %collective-permute-start.10) | collective-permute-done | bytes 135200 | tf_op jit(solution)/shard_map/ppermute | solution.py:349
  142.5 0.0 collective-permute-done.11.refs_2_
  142.5 4.1 %collective-permute-done.12.refs_3_ = bf16[528,128]{1,0:T(8,128)(2,1)S(1)} collective-permute-done((bf16[528,128]{1,0:T(8,128)(2,1)S(1)}, bf16[528,128]{1,0:T(8,128)(2,1)S(1)}, u32[]{:S(2)}, u32[]{:S(2)}) %collective-permute-start.12) | collective-permute-done | bytes 135200 | tf_op jit(solution)/shard_map/ppermute | solution.py:349
  146.6 1.1 combine.1
  (1 shorter events, 0.0 us)
Async XLA Ops:
  1.8 0.7 copy-start.1
  2.4 0.7 copy-start.2
  3.8 12.3 %collective-permute-start = (bf16[1616,128]{1,0:T(8,128)(2,1)S(1)}, bf16[1616,128]{1,0:T(8,128)(2,1)S(1)}, u32[]{:S(2)}, u32[]{:S(2)}) collective-permute-start(bf16[1616,128]{1,0:T(8,128)(2,1)S(1)} %pack_kv.1.kv_ref.refs_4_), channel_id=1, source_target_pairs={{0,28},{4,0},{8,4},{12,8},{16,12},{20,16},{24,20},{28,24},{32,60},... | collective-permute-start | bytes 1241096 | tf_op jit(solution)/shard_map/ppermute | solution.py:342
  5.9 13.2 %collective-permute-start.4 = (bf16[1616,128]{1,0:T(8,128)(2,1)S(1)}, bf16[1616,128]{1,0:T(8,128)(2,1)S(1)}, u32[]{:S(2)}, u32[]{:S(2)}) collective-permute-start(bf16[1616,128]{1,0:T(8,128)(2,1)S(1)} %pack_kv.1.kv_ref.refs_4_), channel_id=1, source_target_pairs={{0,4},{4,8},{8,12},{12,16},{16,20},{20,24},{24,28},{28,0},{32,36},... | collective-permute-start | bytes 1241096 | tf_op jit(solution)/shard_map/ppermute | solution.py:342
  9.1 0.9 copy-start
  19.1 23.3 %collective-permute-start.5 = (bf16[1616,128]{1,0:T(8,128)(2,1)S(1)}, bf16[1616,128]{1,0:T(8,128)(2,1)S(1)}, u32[]{:S(2)}, u32[]{:S(2)}) collective-permute-start(bf16[1616,128]{1,0:T(8,128)(2,1)S(1)} %collective-permute-done.4.refs_5_), channel_id=1, source_target_pairs={{0,4},{4,8},{8,12},{12,16},{16,20},{20,24},{24,28},{28,0},{32,36},... | collective-permute-start | bytes 1241096 | tf_op jit(solution)/shard_map/ppermute | solution.py:342
  21.1 23.3 %collective-permute-start.8 = (bf16[1616,128]{1,0:T(8,128)(2,1)S(1)}, bf16[1616,128]{1,0:T(8,128)(2,1)S(1)}, u32[]{:S(2)}, u32[]{:S(2)}) collective-permute-start(bf16[1616,128]{1,0:T(8,128)(2,1)S(1)} %collective-permute-done.refs_6_), channel_id=1, source_target_pairs={{0,28},{4,0},{8,4},{12,8},{16,12},{20,16},{24,20},{28,24},{32,60},... | collective-permute-start | bytes 1241096 | tf_op jit(solution)/shard_map/ppermute | solution.py:342
  25.6 23.4 %collective-permute-start.3 = (bf16[528,128]{1,0:T(8,128)(2,1)S(1)}, bf16[528,128]{1,0:T(8,128)(2,1)S(1)}, u32[]{:S(2)}, u32[]{:S(2)}) collective-permute-start(bf16[528,128]{1,0:T(8,128)(2,1)S(1)} %pack_q.1.refs_0_), channel_id=1, source_target_pairs={{0,64},{4,68},{8,72},{12,76},{16,80},{20,84},{24,88},{28,92},{32,9... | collective-permute-start | bytes 405512 | tf_op jit(solution)/shard_map/ppermute | solution.py:349
  36.3 13.6 %collective-permute-start.2 = (bf16[528,128]{1,0:T(8,128)(2,1)S(1)}, bf16[528,128]{1,0:T(8,128)(2,1)S(1)}, u32[]{:S(2)}, u32[]{:S(2)}) collective-permute-start(bf16[528,128]{1,0:T(8,128)(2,1)S(1)} %pack_q.1.refs_0_), channel_id=1, source_target_pairs={{0,96},{4,100},{8,104},{12,108},{16,112},{20,116},{24,120},{28,124... | collective-permute-start | bytes 405512 | tf_op jit(solution)/shard_map/ppermute | solution.py:349
  38.2 11.7 %collective-permute-start.1 = (bf16[528,128]{1,0:T(8,128)(2,1)S(1)}, bf16[528,128]{1,0:T(8,128)(2,1)S(1)}, u32[]{:S(2)}, u32[]{:S(2)}) collective-permute-start(bf16[528,128]{1,0:T(8,128)(2,1)S(1)} %pack_q.1.refs_0_), channel_id=1, source_target_pairs={{0,32},{4,36},{8,40},{12,44},{16,48},{20,52},{24,56},{28,60},{32,6... | collective-permute-start | bytes 405512 | tf_op jit(solution)/shard_map/ppermute | solution.py:349
  42.5 13.8 %collective-permute-start.6 = (bf16[1616,128]{1,0:T(8,128)(2,1)S(1)}, bf16[1616,128]{1,0:T(8,128)(2,1)S(1)}, u32[]{:S(2)}, u32[]{:S(2)}) collective-permute-start(bf16[1616,128]{1,0:T(8,128)(2,1)S(1)} %collective-permute-done.5.refs_4_), channel_id=1, source_target_pairs={{0,4},{4,8},{8,12},{12,16},{16,20},{20,24},{24,28},{28,0},{32,36},... | collective-permute-start | bytes 1241096 | tf_op jit(solution)/shard_map/ppermute | solution.py:342
  44.4 34.2 %collective-permute-start.9 = (bf16[1616,128]{1,0:T(8,128)(2,1)S(1)}, bf16[1616,128]{1,0:T(8,128)(2,1)S(1)}, u32[]{:S(2)}, u32[]{:S(2)}) collective-permute-start(bf16[1616,128]{1,0:T(8,128)(2,1)S(1)} %collective-permute-done.8.refs_5_), channel_id=1, source_target_pairs={{0,28},{4,0},{8,4},{12,8},{16,12},{20,16},{24,20},{28,24},{32,60},... | collective-permute-start | bytes 1241096 | tf_op jit(solution)/shard_map/ppermute | solution.py:342
  56.3 56.4 %collective-permute-start.7 = (bf16[1616,128]{1,0:T(8,128)(2,1)S(1)}, bf16[1616,128]{1,0:T(8,128)(2,1)S(1)}, u32[]{:S(2)}, u32[]{:S(2)}) collective-permute-start(bf16[1616,128]{1,0:T(8,128)(2,1)S(1)} %collective-permute-done.6.refs_6_), channel_id=1, source_target_pairs={{0,4},{4,8},{8,12},{12,16},{16,20},{20,24},{24,28},{28,0},{32,36},... | collective-permute-start | bytes 1241096 | tf_op jit(solution)/shard_map/ppermute | solution.py:342
  132.8 9.7 %collective-permute-start.10 = (bf16[528,128]{1,0:T(8,128)(2,1)S(1)}, bf16[528,128]{1,0:T(8,128)(2,1)S(1)}, u32[]{:S(2)}, u32[]{:S(2)}) collective-permute-start(bf16[528,128]{1,0:T(8,128)(2,1)S(1)} %get-tuple-element.34), channel_id=1, source_target_pairs={{0,64},{4,68},{8,72},{12,76},{16,80},{20,84},{24,88},{28,92},{32,9... | collective-permute-start | bytes 405512 | tf_op jit(solution)/shard_map/ppermute | solution.py:349
  134.7 7.7 %collective-permute-start.11 = (bf16[528,128]{1,0:T(8,128)(2,1)S(1)}, bf16[528,128]{1,0:T(8,128)(2,1)S(1)}, u32[]{:S(2)}, u32[]{:S(2)}) collective-permute-start(bf16[528,128]{1,0:T(8,128)(2,1)S(1)} %get-tuple-element.35), channel_id=1, source_target_pairs={{0,96},{4,100},{8,104},{12,108},{16,112},{20,116},{24,120},{28,124... | collective-permute-start | bytes 405512 | tf_op jit(solution)/shard_map/ppermute | solution.py:349
  136.7 9.9 %collective-permute-start.12 = (bf16[528,128]{1,0:T(8,128)(2,1)S(1)}, bf16[528,128]{1,0:T(8,128)(2,1)S(1)}, u32[]{:S(2)}, u32[]{:S(2)}) collective-permute-start(bf16[528,128]{1,0:T(8,128)(2,1)S(1)} %get-tuple-element.36), channel_id=1, source_target_pairs={{0,32},{4,36},{8,40},{12,44},{16,48},{20,52},{24,56},{28,60},{32,6... | collective-permute-start | bytes 405512 | tf_op jit(solution)/shard_map/ppermute | solution.py:349

commit v8 on v7

--- a/solution.py
+++ b/solution.py
@@ -352,8 +352,9 @@
 def body(queries, kv_cache, new_kv, cache_len, new_pos):
     own_kv = pack_kv(kv_cache, new_kv, cache_len, new_pos)
     own_q = pack_q(queries, own_kv)
-    up1, down1 = shift_y(own_kv, 1), shift_y(own_kv, -1)
-    down1, own_q = lax.optimization_barrier((down1, own_q))
+    down1 = shift_y(own_kv, -1)
+    same_kv, own_q = lax.optimization_barrier((own_kv, own_q))
+    up1 = shift_y(same_kv, 1)
     offsets = (1, -1, 2)
     q1, q2, q3 = [shift_z(own_q, d) for d in offsets]
     up2, down2 = shift_y(up1, 1), shift_y(down1, -1)

time: 148 us -> 150 us (1.014)
  the two profiles are of different devices: /device:TPU:35 before, /device:TPU:27 now
where the time goes in v8:
time: 150 us; the launch traced here: 149 us
  starting transfers between devices  89.6 us (60%)
  Pallas kernels  45.5 us (30%)
  waiting for transfers between devices  10.2 us (7%)
  local copies, waits for them, and re-layouts  3.97 us (3%)
    ppermute x7, starting transfers between devices, shift_y(): return lax.ppermute(x, 'seq', pairs)  47.1 us
    pallas_call x3, Pallas kernels, stage(): pl.pallas_call(functools.partial(stage_kernel, nq, g, spans, last), out_s...  43.7 us
    ppermute x6, starting transfers between devices, shift_z(): return lax.ppermute(x, 'seq', pairs)  42.5 us
    ppermute x7, waiting for transfers between devices, shift_y(): return lax.ppermute(x, 'seq', pairs)  6.29 us
    unnamed x8, local copies, waits for them, and re-layouts  3.97 us
    ppermute x6, waiting for transfers between devices, shift_z(): return lax.ppermute(x, 'seq', pairs)  3.87 us
  transfers between devices with their start and end apart: 13, of which 3 were waited for; matrix products, arithmetic and copies ran while one was open for 0% of the time, Pallas kernels for 27%

profile of v8, /device:TPU:27, one launch (start us, length us, event | category | flops | bytes accessed | tf_op | source)
XLA Modules:
  0.0 149.4 jit_solution(16657453757000975758)
XLA Ops:
  0.0 0.7 copy.11
  0.7 1.0 copy.10
  1.8 0.0 copy-start.1
  1.8 0.6 copy-done.1
  2.4 0.0 copy-start.2
  2.4 0.7 copy-done.2
  3.1 0.7 pack_kv.1.kv_ref.refs_4_
  3.8 0.0 copy-start
  3.8 0.9 copy-done
  4.8 4.4 %collective-permute-start.3 = (bf16[1616,128]{1,0:T(8,128)(2,1)S(1)}, bf16[1616,128]{1,0:T(8,128)(2,1)S(1)}, u32[]{:S(2)}, u32[]{:S(2)}) collective-permute-start(bf16[1616,128]{1,0:T(8,128)(2,1)S(1)} %pack_kv.1.kv_ref.refs_4_), channel_id=1, source_target_pairs={{0,4},{4,8},{8,12},{12,16},{16,20},{20,24},{24,28},{28,0},{32,36},... | collective-permute-start | bytes 1241096 | tf_op jit(solution)/shard_map/ppermute | solution.py:342
  9.2 1.9 %collective-permute-start.6 = (bf16[1616,128]{1,0:T(8,128)(2,1)S(1)}, bf16[1616,128]{1,0:T(8,128)(2,1)S(1)}, u32[]{:S(2)}, u32[]{:S(2)}) collective-permute-start(bf16[1616,128]{1,0:T(8,128)(2,1)S(1)} %pack_kv.1.kv_ref.refs_4_), channel_id=1, source_target_pairs={{0,28},{4,0},{8,4},{12,8},{16,12},{20,16},{24,20},{28,24},{32,60},... | collective-permute-start | bytes 1241096 | tf_op jit(solution)/shard_map/ppermute | solution.py:342
  11.1 6.3 %collective-permute-done.3.refs_5_ = bf16[1616,128]{1,0:T(8,128)(2,1)S(1)} collective-permute-done((bf16[1616,128]{1,0:T(8,128)(2,1)S(1)}, bf16[1616,128]{1,0:T(8,128)(2,1)S(1)}, u32[]{:S(2)}, u32[]{:S(2)}) %collective-permute-start.3) | collective-permute-done | bytes 413728 | tf_op jit(solution)/shard_map/ppermute | solution.py:342
  17.4 5.3 %collective-permute-start.4 = (bf16[1616,128]{1,0:T(8,128)(2,1)S(1)}, bf16[1616,128]{1,0:T(8,128)(2,1)S(1)}, u32[]{:S(2)}, u32[]{:S(2)}) collective-permute-start(bf16[1616,128]{1,0:T(8,128)(2,1)S(1)} %collective-permute-done.3.refs_5_), channel_id=1, source_target_pairs={{0,4},{4,8},{8,12},{12,16},{16,20},{20,24},{24,28},{28,0},{32,36},... | collective-permute-start | bytes 1241096 | tf_op jit(solution)/shard_map/ppermute | solution.py:342
  22.7 0.0 collective-permute-done.6.refs_6_
  22.7 1.9 %collective-permute-start.8 = (bf16[1616,128]{1,0:T(8,128)(2,1)S(1)}, bf16[1616,128]{1,0:T(8,128)(2,1)S(1)}, u32[]{:S(2)}, u32[]{:S(2)}) collective-permute-start(bf16[1616,128]{1,0:T(8,128)(2,1)S(1)} %collective-permute-done.6.refs_6_), channel_id=1, source_target_pairs={{0,28},{4,0},{8,4},{12,8},{16,12},{20,16},{24,20},{28,24},{32,60},... | collective-permute-start | bytes 1241096 | tf_op jit(solution)/shard_map/ppermute | solution.py:342
  24.6 10.6 %collective-permute-start.2 = (bf16[528,128]{1,0:T(8,128)(2,1)S(1)}, bf16[528,128]{1,0:T(8,128)(2,1)S(1)}, u32[]{:S(2)}, u32[]{:S(2)}) collective-permute-start(bf16[528,128]{1,0:T(8,128)(2,1)S(1)} %pack_q.1.refs_0_), channel_id=1, source_target_pairs={{0,64},{4,68},{8,72},{12,76},{16,80},{20,84},{24,88},{28,92},{32,9... | collective-permute-start | bytes 405512 | tf_op jit(solution)/shard_map/ppermute | solution.py:349
  35.3 1.9 %collective-permute-start.1 = (bf16[528,128]{1,0:T(8,128)(2,1)S(1)}, bf16[528,128]{1,0:T(8,128)(2,1)S(1)}, u32[]{:S(2)}, u32[]{:S(2)}) collective-permute-start(bf16[528,128]{1,0:T(8,128)(2,1)S(1)} %pack_q.1.refs_0_), channel_id=1, source_target_pairs={{0,96},{4,100},{8,104},{12,108},{16,112},{20,116},{24,120},{28,124... | collective-permute-start | bytes 405512 | tf_op jit(solution)/shard_map/ppermute | solution.py:349
  37.2 4.2 %collective-permute-start = (bf16[528,128]{1,0:T(8,128)(2,1)S(1)}, bf16[528,128]{1,0:T(8,128)(2,1)S(1)}, u32[]{:S(2)}, u32[]{:S(2)}) collective-permute-start(bf16[528,128]{1,0:T(8,128)(2,1)S(1)} %pack_q.1.refs_0_), channel_id=1, source_target_pairs={{0,32},{4,36},{8,40},{12,44},{16,48},{20,52},{24,56},{28,60},{32,6... | collective-permute-start | bytes 405512 | tf_op jit(solution)/shard_map/ppermute | solution.py:349
  41.5 0.0 collective-permute-done.4.refs_4_
  41.5 4.6 %collective-permute-start.5 = (bf16[1616,128]{1,0:T(8,128)(2,1)S(1)}, bf16[1616,128]{1,0:T(8,128)(2,1)S(1)}, u32[]{:S(2)}, u32[]{:S(2)}) collective-permute-start(bf16[1616,128]{1,0:T(8,128)(2,1)S(1)} %collective-permute-done.4.refs_4_), channel_id=1, source_target_pairs={{0,4},{4,8},{8,12},{12,16},{16,20},{20,24},{24,28},{28,0},{32,36},... | collective-permute-start | bytes 1241096 | tf_op jit(solution)/shard_map/ppermute | solution.py:342
  46.1 0.0 collective-permute-done.8.refs_5_
  46.1 1.9 %collective-permute-start.9 = (bf16[1616,128]{1,0:T(8,128)(2,1)S(1)}, bf16[1616,128]{1,0:T(8,128)(2,1)S(1)}, u32[]{:S(2)}, u32[]{:S(2)}) collective-permute-start(bf16[1616,128]{1,0:T(8,128)(2,1)S(1)} %collective-permute-done.8.refs_5_), channel_id=1, source_target_pairs={{0,28},{4,0},{8,4},{12,8},{16,12},{20,16},{24,20},{28,24},{32,60},... | collective-permute-start | bytes 1241096 | tf_op jit(solution)/shard_map/ppermute | solution.py:342
  48.0 0.0 collective-permute-done.2.refs_3_
  48.0 0.0 collective-permute-done.1.refs_2_
  48.0 0.0 collective-permute-done.refs_1_
  48.0 6.4 %reach1.1 = (f32[2048,256]{1,0:T(8,128)S(1)}, f32[2048,128]{1,0:T(8,128)S(1)}) custom-call(bf16[528,128]{1,0:T(8,128)(2,1)S(1)} %pack_q.1.refs_0_, bf16[528,128]{1,0:T(8,128)(2,1)S(1)} %collective-permute-done.refs_1_, bf16[528,128]{1,0:T(8,128)(2,1)S(1)} %collective-permute-done.1.refs_2_, bf16[528,128]{1,0:T(8,128)(2,1)S(1)} %collective-permute-done.2.refs_3_, ...), custom_call_target="tpu_custom_call" | custom-call | flops 5100273664 | bytes 4194304 | tf_op jit(solution)/shard_map/reach1/pallas_call | solution.py:290
  54.4 0.0 collective-permute-done.5.refs_6_
  54.5 27.0 %collective-permute-start.7 = (bf16[1616,128]{1,0:T(8,128)(2,1)S(1)}, bf16[1616,128]{1,0:T(8,128)(2,1)S(1)}, u32[]{:S(2)}, u32[]{:S(2)}) collective-permute-start(bf16[1616,128]{1,0:T(8,128)(2,1)S(1)} %collective-permute-done.5.refs_6_), channel_id=1, source_target_pairs={{0,4},{4,8},{8,12},{12,16},{16,20},{20,24},{24,28},{28,0},{32,36},... | collective-permute-start | bytes 1241096 | tf_op jit(solution)/shard_map/ppermute | solution.py:342
  81.5 0.0 collective-permute-done.9.refs_7_
  81.5 34.1 %reach3.1 = (f32[2048,256]{1,0:T(8,128)S(1)}, f32[2048,128]{1,0:T(8,128)S(1)}) custom-call(bf16[528,128]{1,0:T(8,128)(2,1)S(1)} %pack_q.1.refs_0_, bf16[528,128]{1,0:T(8,128)(2,1)S(1)} %collective-permute-done.refs_1_, bf16[528,128]{1,0:T(8,128)(2,1)S(1)} %collective-permute-done.1.refs_2_, bf16[528,128]{1,0:T(8,128)(2,1)S(1)} %collective-permute-done.2.refs_3_, ...), custom_call_target="tpu_custom_call" | custom-call | flops 6710886400 | bytes 4194304 | tf_op jit(solution)/shard_map/reach3/pallas_call | solution.py:290
  115.7 0.0 collective-permute-done.7.refs_4_
  115.7 3.1 %reach4.1 = (bf16[528,128]{1,0:T(8,128)(2,1)S(1)}, bf16[528,128]{1,0:T(8,128)(2,1)S(1)}, bf16[528,128]{1,0:T(8,128)(2,1)S(1)}, bf16[528,128]{1,0:T(8,128)(2,1)S(1)}) custom-call(bf16[528,128]{1,0:T(8,128)(2,1)S(1)} %pack_q.1.refs_0_, bf16[528,128]{1,0:T(8,128)(2,1)S(1)} %collective-permute-done.refs_1_, bf16[528,128]{1,0:T(8,128)(2,1)S(1)} %collective-permute-done.1.refs_2_, ...), custom_call_target="tpu_custom_call" | custom-call | flops 1879048192 | bytes 4194304 | tf_op jit(solution)/shard_map/reach4/pallas_call | solution.py:290
  118.8 1.9 %collective-permute-start.10 = (bf16[528,128]{1,0:T(8,128)(2,1)S(1)}, bf16[528,128]{1,0:T(8,128)(2,1)S(1)}, u32[]{:S(2)}, u32[]{:S(2)}) collective-permute-start(bf16[528,128]{1,0:T(8,128)(2,1)S(1)} %get-tuple-element.34), channel_id=1, source_target_pairs={{0,64},{4,68},{8,72},{12,76},{16,80},{20,84},{24,88},{28,92},{32,9... | collective-permute-start | bytes 405512 | tf_op jit(solution)/shard_map/ppermute | solution.py:349
  120.7 19.8 %collective-permute-start.11 = (bf16[528,128]{1,0:T(8,128)(2,1)S(1)}, bf16[528,128]{1,0:T(8,128)(2,1)S(1)}, u32[]{:S(2)}, u32[]{:S(2)}) collective-permute-start(bf16[528,128]{1,0:T(8,128)(2,1)S(1)} %get-tuple-element.35), channel_id=1, source_target_pairs={{0,96},{4,100},{8,104},{12,108},{16,112},{20,116},{24,120},{28,124... | collective-permute-start | bytes 405512 | tf_op jit(solution)/shard_map/ppermute | solution.py:349
  140.5 4.0 %collective-permute-start.12 = (bf16[528,128]{1,0:T(8,128)(2,1)S(1)}, bf16[528,128]{1,0:T(8,128)(2,1)S(1)}, u32[]{:S(2)}, u32[]{:S(2)}) collective-permute-start(bf16[528,128]{1,0:T(8,128)(2,1)S(1)} %get-tuple-element.36), channel_id=1, source_target_pairs={{0,32},{4,36},{8,40},{12,44},{16,48},{20,52},{24,56},{28,60},{32,6... | collective-permute-start | bytes 405512 | tf_op jit(solution)/shard_map/ppermute | solution.py:349
  144.5 0.0 collective-permute-done.10.refs_1_
  144.5 0.4 collective-permute-done.11.refs_2_
  145.0 3.4 %collective-permute-done.12.refs_3_ = bf16[528,128]{1,0:T(8,128)(2,1)S(1)} collective-permute-done((bf16[528,128]{1,0:T(8,128)(2,1)S(1)}, bf16[528,128]{1,0:T(8,128)(2,1)S(1)}, u32[]{:S(2)}, u32[]{:S(2)}) %collective-permute-start.12) | collective-permute-done | bytes 135200 | tf_op jit(solution)/shard_map/ppermute | solution.py:349
  148.4 1.1 combine.1
  (1 shorter events, 0.0 us)
Async XLA Ops:
  1.8 0.7 copy-start.1
  2.4 0.7 copy-start.2
  3.8 0.9 copy-start
  4.8 12.6 %collective-permute-start.3 = (bf16[1616,128]{1,0:T(8,128)(2,1)S(1)}, bf16[1616,128]{1,0:T(8,128)(2,1)S(1)}, u32[]{:S(2)}, u32[]{:S(2)}) collective-permute-start(bf16[1616,128]{1,0:T(8,128)(2,1)S(1)} %pack_kv.1.kv_ref.refs_4_), channel_id=1, source_target_pairs={{0,4},{4,8},{8,12},{12,16},{16,20},{20,24},{24,28},{28,0},{32,36},... | collective-permute-start | bytes 1241096 | tf_op jit(solution)/shard_map/ppermute | solution.py:342
  9.2 13.5 %collective-permute-start.6 = (bf16[1616,128]{1,0:T(8,128)(2,1)S(1)}, bf16[1616,128]{1,0:T(8,128)(2,1)S(1)}, u32[]{:S(2)}, u32[]{:S(2)}) collective-permute-start(bf16[1616,128]{1,0:T(8,128)(2,1)S(1)} %pack_kv.1.kv_ref.refs_4_), channel_id=1, source_target_pairs={{0,28},{4,0},{8,4},{12,8},{16,12},{20,16},{24,20},{28,24},{32,60},... | collective-permute-start | bytes 1241096 | tf_op jit(solution)/shard_map/ppermute | solution.py:342
  17.4 24.1 %collective-permute-start.4 = (bf16[1616,128]{1,0:T(8,128)(2,1)S(1)}, bf16[1616,128]{1,0:T(8,128)(2,1)S(1)}, u32[]{:S(2)}, u32[]{:S(2)}) collective-permute-start(bf16[1616,128]{1,0:T(8,128)(2,1)S(1)} %collective-permute-done.3.refs_5_), channel_id=1, source_target_pairs={{0,4},{4,8},{8,12},{12,16},{16,20},{20,24},{24,28},{28,0},{32,36},... | collective-permute-start | bytes 1241096 | tf_op jit(solution)/shard_map/ppermute | solution.py:342
  22.7 23.4 %collective-permute-start.8 = (bf16[1616,128]{1,0:T(8,128)(2,1)S(1)}, bf16[1616,128]{1,0:T(8,128)(2,1)S(1)}, u32[]{:S(2)}, u32[]{:S(2)}) collective-permute-start(bf16[1616,128]{1,0:T(8,128)(2,1)S(1)} %collective-permute-done.6.refs_6_), channel_id=1, source_target_pairs={{0,28},{4,0},{8,4},{12,8},{16,12},{20,16},{24,20},{28,24},{32,60},... | collective-permute-start | bytes 1241096 | tf_op jit(solution)/shard_map/ppermute | solution.py:342
  24.6 23.4 %collective-permute-start.2 = (bf16[528,128]{1,0:T(8,128)(2,1)S(1)}, bf16[528,128]{1,0:T(8,128)(2,1)S(1)}, u32[]{:S(2)}, u32[]{:S(2)}) collective-permute-start(bf16[528,128]{1,0:T(8,128)(2,1)S(1)} %pack_q.1.refs_0_), channel_id=1, source_target_pairs={{0,64},{4,68},{8,72},{12,76},{16,80},{20,84},{24,88},{28,92},{32,9... | collective-permute-start | bytes 405512 | tf_op jit(solution)/shard_map/ppermute | solution.py:349
  35.3 12.7 %collective-permute-start.1 = (bf16[528,128]{1,0:T(8,128)(2,1)S(1)}, bf16[528,128]{1,0:T(8,128)(2,1)S(1)}, u32[]{:S(2)}, u32[]{:S(2)}) collective-permute-start(bf16[528,128]{1,0:T(8,128)(2,1)S(1)} %pack_q.1.refs_0_), channel_id=1, source_target_pairs={{0,96},{4,100},{8,104},{12,108},{16,112},{20,116},{24,120},{28,124... | collective-permute-start | bytes 405512 | tf_op jit(solution)/shard_map/ppermute | solution.py:349
  37.2 10.8 %collective-permute-start = (bf16[528,128]{1,0:T(8,128)(2,1)S(1)}, bf16[528,128]{1,0:T(8,128)(2,1)S(1)}, u32[]{:S(2)}, u32[]{:S(2)}) collective-permute-start(bf16[528,128]{1,0:T(8,128)(2,1)S(1)} %pack_q.1.refs_0_), channel_id=1, source_target_pairs={{0,32},{4,36},{8,40},{12,44},{16,48},{20,52},{24,56},{28,60},{32,6... | collective-permute-start | bytes 405512 | tf_op jit(solution)/shard_map/ppermute | solution.py:349
  41.5 13.0 %collective-permute-start.5 = (bf16[1616,128]{1,0:T(8,128)(2,1)S(1)}, bf16[1616,128]{1,0:T(8,128)(2,1)S(1)}, u32[]{:S(2)}, u32[]{:S(2)}) collective-permute-start(bf16[1616,128]{1,0:T(8,128)(2,1)S(1)} %collective-permute-done.4.refs_4_), channel_id=1, source_target_pairs={{0,4},{4,8},{8,12},{12,16},{16,20},{20,24},{24,28},{28,0},{32,36},... | collective-permute-start | bytes 1241096 | tf_op jit(solution)/shard_map/ppermute | solution.py:342
  46.1 35.4 %collective-permute-start.9 = (bf16[1616,128]{1,0:T(8,128)(2,1)S(1)}, bf16[1616,128]{1,0:T(8,128)(2,1)S(1)}, u32[]{:S(2)}, u32[]{:S(2)}) collective-permute-start(bf16[1616,128]{1,0:T(8,128)(2,1)S(1)} %collective-permute-done.8.refs_5_), channel_id=1, source_target_pairs={{0,28},{4,0},{8,4},{12,8},{16,12},{20,16},{24,20},{28,24},{32,60},... | collective-permute-start | bytes 1241096 | tf_op jit(solution)/shard_map/ppermute | solution.py:342
  54.5 61.2 %collective-permute-start.7 = (bf16[1616,128]{1,0:T(8,128)(2,1)S(1)}, bf16[1616,128]{1,0:T(8,128)(2,1)S(1)}, u32[]{:S(2)}, u32[]{:S(2)}) collective-permute-start(bf16[1616,128]{1,0:T(8,128)(2,1)S(1)} %collective-permute-done.5.refs_6_), channel_id=1, source_target_pairs={{0,4},{4,8},{8,12},{12,16},{16,20},{20,24},{24,28},{28,0},{32,36},... | collective-permute-start | bytes 1241096 | tf_op jit(solution)/shard_map/ppermute | solution.py:342
  118.8 25.7 %collective-permute-start.10 = (bf16[528,128]{1,0:T(8,128)(2,1)S(1)}, bf16[528,128]{1,0:T(8,128)(2,1)S(1)}, u32[]{:S(2)}, u32[]{:S(2)}) collective-permute-start(bf16[528,128]{1,0:T(8,128)(2,1)S(1)} %get-tuple-element.34), channel_id=1, source_target_pairs={{0,64},{4,68},{8,72},{12,76},{16,80},{20,84},{24,88},{28,92},{32,9... | collective-permute-start | bytes 405512 | tf_op jit(solution)/shard_map/ppermute | solution.py:349
  120.7 24.2 %collective-permute-start.11 = (bf16[528,128]{1,0:T(8,128)(2,1)S(1)}, bf16[528,128]{1,0:T(8,128)(2,1)S(1)}, u32[]{:S(2)}, u32[]{:S(2)}) collective-permute-start(bf16[528,128]{1,0:T(8,128)(2,1)S(1)} %get-tuple-element.35), channel_id=1, source_target_pairs={{0,96},{4,100},{8,104},{12,108},{16,112},{20,116},{24,120},{28,124... | collective-permute-start | bytes 405512 | tf_op jit(solution)/shard_map/ppermute | solution.py:349
  140.5 7.9 %collective-permute-start.12 = (bf16[528,128]{1,0:T(8,128)(2,1)S(1)}, bf16[528,128]{1,0:T(8,128)(2,1)S(1)}, u32[]{:S(2)}, u32[]{:S(2)}) collective-permute-start(bf16[528,128]{1,0:T(8,128)(2,1)S(1)} %get-tuple-element.36), channel_id=1, source_target_pairs={{0,32},{4,36},{8,40},{12,44},{16,48},{20,52},{24,56},{28,60},{32,6... | collective-permute-start | bytes 405512 | tf_op jit(solution)/shard_map/ppermute | solution.py:349
